TPU v7x, 256 devices: a whole 4x4x8 slice. The times are simulated.
256 devices in a mesh: gy: 64 (over y, z, core), gz: 4 (over x).
Axes of the slice: x: 4, y: 4, z: 8, core: 2. Of those that a mesh axis runs over, the one named last changes fastest.
Arguments:
- velocity: float32 [3, 256, 64, 512], P(None, 'gy', 'gz'), may hold values from -24 to 24
- smag_coef: float32 [256, 64, 512], P('gy', 'gz'), may hold values from 0.3 to 3
- snap_code: int32 [128], replicated, may hold values from 0 to 191, as said below
Outputs:
- final_velocity: float32 [3, 256, 64, 512], P(None, 'gy', 'gz')
- pod_modes: float32 [112, 3, 64, 16, 128], P(None, None, 'gy', 'gz')
Inputs may be any that keep to these rules, and one draw needn't show every extreme that they name: `snap_code`: the 128 entries are distinct.
All inputs are finite; a program needn't handle non-finite values.
Results may differ from a plain program's by a relative error of at most 0.0003.
Values sent between devices are 32-bit elements; how exact they have to be, the bound alone decides.
No kernel may reach another device: no remote copies, remote signals or barrier semaphores. Data moves between devices by JAX's collectives and lax.ppermute only.
A program may use at most 64 MiB of HBM per device.

v0:
```python
import functools

import jax
import jax.numpy as jnp
from jax import lax
from jax.experimental import pallas as pl
from jax.experimental.pallas import tpu as pltpu
from jax.sharding import PartitionSpec as P

RANK = 112
ITERS = 3
PANEL = 8


nu_limit = 0.125
ridge = 1.0
highest = lax.Precision.HIGHEST


def with_halo(cells, sides, width):
    for axis, dim in sides:
        count = lax.axis_size(axis)
        head = lax.slice_in_dim(cells, 0, width, axis=dim)
        tail = lax.slice_in_dim(cells, cells.shape[dim] - width, cells.shape[dim], axis=dim)
        cells = jnp.concatenate(
            [
                lax.ppermute(tail, axis, [(i, (i + 1) % count) for i in range(count)]),
                cells,
                lax.ppermute(head, axis, [((i + 1) % count, i) for i in range(count)]),
            ],
            axis=dim,
        )
    return cells


def advance(velocity_ext, coefficient):
    grad_y = (velocity_ext[:, 2:, 1:-1, 1:-1] - velocity_ext[:, :-2, 1:-1, 1:-1]) * 0.5
    grad_z = (velocity_ext[:, 1:-1, 2:, 1:-1] - velocity_ext[:, 1:-1, :-2, 1:-1]) * 0.5
    grad_x = (velocity_ext[:, 1:-1, 1:-1, 2:] - velocity_ext[:, 1:-1, 1:-1, :-2]) * 0.5
    grads = [[grad_x[c], grad_y[c], grad_z[c]] for c in range(3)]
    strain = jnp.zeros_like(grad_x[0])
    for c in range(3):
        for d in range(3):
            strain = strain + 0.5 * (grads[c][d] + grads[d][c]) ** 2
    strain_rate = coefficient[1:-1, 1:-1, 1:-1] * jnp.sqrt(strain)
    viscosity = nu_limit * strain_rate / (1.0 + strain_rate)
    inner_field = velocity_ext[:, 1:-1, 1:-1, 1:-1]
    centre = inner_field[:, 1:-1, 1:-1, 1:-1]
    visc_mid = viscosity[1:-1, 1:-1, 1:-1]
    inside = slice(1, -1)
    ahead = slice(2, None)
    behind = slice(None, -2)
    shifts = [
        (ahead, inside, inside),
        (behind, inside, inside),
        (inside, ahead, inside),
        (inside, behind, inside),
        (inside, inside, ahead),
        (inside, inside, behind),
    ]
    result = centre
    for neighbour in shifts:
        face_visc = 0.5 * (visc_mid + viscosity[neighbour])
        result = result + face_visc * (inner_field[(slice(None),) + neighbour] - centre)
    return result


def wall_masks(margin, rows_y):
    global_row = lax.axis_index("gy") * rows_y + jnp.arange(rows_y + 2 * margin) - margin
    return (global_row < 0, global_row >= rows_y * lax.axis_size("gy"))


def zero_walls(field_data, margin, rows_y):
    below, above = wall_masks(margin, rows_y)
    outside = jnp.logical_or(below, above)
    return jnp.where(outside[None, :, None, None], jnp.float32(0.0), field_data)


def edge_walls(coefficient, margin, rows_y):
    below, above = wall_masks(margin, rows_y)
    first_row = coefficient[margin][None]
    last_row = coefficient[margin + rows_y - 1][None]
    coefficient = jnp.where(below[:, None, None], first_row, coefficient)
    return jnp.where(above[:, None, None], last_row, coefficient)


def wrap_x(field_data, margin):
    return jnp.concatenate(
        [field_data[..., -margin:], field_data, field_data[..., :margin]], axis=-1
    )


def decimate(field_data):
    size_y, size_z, size_x = (field_data.shape[1], field_data.shape[2], field_data.shape[3])
    cell = jnp.arange(size_x, dtype=jnp.int32)
    place = (cell % 4) * (size_x // 4) + cell // 4
    sorting = (place[:, None] == cell[None, :]).astype(jnp.float32)
    in_order = jnp.dot(field_data.reshape(-1, size_x), sorting, precision=highest)
    blocks = in_order.reshape(3, size_y // 4, 4, size_z // 4, 4, 4, size_x // 4)
    return blocks.transpose(2, 4, 5, 0, 1, 3, 6).reshape(64, -1)


def recip(value):
    guess = pl.reciprocal(value, approx=True)
    return guess * (2.0 - value * guess)


def spread(block, lane):
    return jnp.broadcast_to(block[:, lane : lane + 1], block.shape)


def repeat(block, row):
    return jnp.broadcast_to(block[row : row + 1, :], block.shape)


def orthonormal_rows(inner, wide):
    panels = RANK // PANEL
    row_id = lax.broadcasted_iota(jnp.int32, (PANEL, inner.shape[1]), 0)
    left = [inner[PANEL * k : PANEL * (k + 1), :] for k in range(panels)]
    right = [wide[PANEL * k : PANEL * (k + 1), :] for k in range(panels)]
    rows = []
    for k in range(panels):
        follows = k + 1 < panels
        own_left, own_right = left[k], right[k]
        own_cols = [spread(own_left, PANEL * k + j) for j in range(PANEL)]
        if follows:
            next_left, next_right = left[k + 1], right[k + 1]
            next_cols = [spread(next_left, PANEL * k + j) for j in range(PANEL)]
        pivots = jnp.ones_like(own_left)
        for j in range(PANEL):
            pivot = repeat(own_cols[j], j)
            inverse = recip(pivot)
            pivots = jnp.where(row_id == j, pivot, pivots)
            own_factor = own_cols[j] * inverse
            for m in range(j + 1, PANEL):
                own_cols[m] = own_cols[m] - own_factor * repeat(own_cols[j], m)
            row_left, row_right = repeat(own_left, j), repeat(own_right, j)
            if follows:
                next_factor = next_cols[j] * inverse
                for m in range(j + 1, PANEL):
                    next_cols[m] = next_cols[m] - next_factor * repeat(own_cols[j], m)
                next_left = next_left - next_factor * row_left
                next_right = next_right - next_factor * row_right
            below = jnp.where(row_id > j, own_factor, 0.0)
            own_left = own_left - below * row_left
            own_right = own_right - below * row_right
        if follows:
            left[k + 1], right[k + 1] = next_left, next_right
        if k + 2 < panels:
            scale = recip(pivots)
            update = lax.dot_general(
                own_left[:, PANEL * (k + 2) : RANK],
                jnp.concatenate([own_left * scale, own_right * scale], axis=1),
                (((0,), (0,)), ((), ())),
                precision=highest,
                preferred_element_type=jnp.float32,
            )
            width = own_left.shape[1]
            for m in range(k + 2, panels):
                start = PANEL * (m - k - 2)
                left[m] = left[m] - update[start : start + PANEL, :width]
                right[m] = right[m] - update[start : start + PANEL, width:]
        root = lax.rsqrt(pivots)
        rows.append(own_right * (root * (1.5 - 0.5 * pivots * root * root)))
    return jnp.concatenate(rows, axis=0)


def basis_kernel(total_ref, snap_ref, out_ref, basis_ref, *, rows_all):
    cols = total_ref.shape[0]
    row_id = lax.broadcasted_iota(jnp.int32, (cols, cols), 0)
    col_id = lax.broadcasted_iota(jnp.int32, (cols, cols), 1)
    gram_matrix = total_ref[...] / rows_all + jnp.where(row_id == col_id, jnp.float32(ridge), 0.0)

    def sweep(step, carry):
        @pl.when(step == 0)
        def _():
            basis_ref[...] = gram_matrix[:RANK, :]

        @pl.when(step > 0)
        def _():
            basis_ref[...] = jnp.dot(
                basis_ref[...], gram_matrix, precision=highest, preferred_element_type=jnp.float32
            )

        wide = basis_ref[...]
        full = jnp.concatenate([wide, jnp.zeros((cols - RANK, cols), jnp.float32)], axis=0)
        inner = lax.dot_general(
            wide, full, (((1,), (1,)), ((), ())), precision=highest, preferred_element_type=jnp.float32
        )
        basis_ref[...] = orthonormal_rows(inner, wide)
        return carry

    lax.fori_loop(0, ITERS, sweep, 0)
    basis = basis_ref[...]
    blocks = out_ref.shape[0] // RANK
    for block in range(blocks):
        out_ref[pl.ds(block, RANK, stride=blocks), :] = jnp.dot(
            basis,
            snap_ref[:, 128 * block : 128 * (block + 1)],
            precision=highest,
            preferred_element_type=jnp.float32,
        )


def project(gram_total, snapshots, rows_all):
    cols, rows = snapshots.shape
    return pl.pallas_call(
        functools.partial(basis_kernel, rows_all=rows_all),
        out_shape=jax.ShapeDtypeStruct((RANK * rows // 128, 128), jnp.float32),
        in_specs=[pl.BlockSpec(memory_space=pltpu.VMEM)] * 2,
        out_specs=pl.BlockSpec(memory_space=pltpu.VMEM),
        scratch_shapes=[pltpu.VMEM((RANK, cols), jnp.float32)],
        compiler_params=pltpu.CompilerParams(vmem_limit_bytes=16 * 2**20),
        name="basis",
    )(gram_total, snapshots)


def device_sum(part):
    steps = [
        ("gz", lambda i: i ^ 1),
        ("gz", lambda i: 3 - i),
        ("gy", lambda i: i ^ 1),
        ("gy", lambda i: i ^ 2),
        ("gy", lambda i: i ^ 6),
        ("gy", lambda i: i ^ 14),
        ("gy", lambda i: i ^ 16),
        ("gy", lambda i: i ^ 48),
    ]
    for axis, partner in steps:
        count = lax.axis_size(axis)
        part = part + lax.ppermute(part, axis, [(i, partner(i)) for i in range(count)])
    return part


def local(velocity, smag_coef, snap_code):
    rows_y = velocity.shape[1]
    stacked = jnp.concatenate([velocity, smag_coef[None]], axis=0)
    padded = with_halo(stacked, (("gy", 1), ("gz", 2)), 2)
    velocity_ext = wrap_x(zero_walls(padded[:3], 2, rows_y), 2)
    coefficient = wrap_x(edge_walls(padded[3], 2, rows_y), 2)
    state_one = advance(velocity_ext, coefficient)
    second = with_halo(state_one, (("gy", 1), ("gz", 2)), 2)
    state_two = advance(wrap_x(zero_walls(second, 2, rows_y), 2), coefficient)
    selector = (snap_code[:, None] == jnp.arange(192, dtype=jnp.int32)[None, :]).astype(jnp.float32)
    all_rows = jnp.concatenate(
        [decimate(velocity), decimate(state_one), decimate(state_two)], axis=0
    )
    snapshots = jnp.dot(selector, all_rows, precision=highest)
    gram_total = device_sum(jnp.dot(snapshots, snapshots.T, precision=highest))
    rows_all = snapshots.shape[1] * lax.axis_size("gy") * lax.axis_size("gz")
    pod_modes = project(gram_total, snapshots, rows_all)
    shaped = pod_modes.reshape(
        RANK, 3, rows_y // 4, velocity.shape[2] // 4, velocity.shape[3] // 4
    )
    return (state_two, shaped)


def solution(mesh):
    placed = (P(None, "gy", "gz", None), P("gy", "gz", None), P())
    return jax.shard_map(
        local,
        mesh=mesh,
        in_specs=placed,
        out_specs=(P(None, "gy", "gz", None), P(None, None, "gy", "gz", None)),
        check_vma=False,
    )
```

profile of v0, /device:TPU:32, one launch (start us, length us, event | category | flops | bytes accessed | tf_op | source)
XLA Modules:
  0.0 107.5 jit_solution(4655406625382594827)
XLA Ops:
  0.7 1.2 %fusion.115 = (f32[4,2,16,512]{3,2,1,0:T(8,128)S(1)}, f32[4,2,16,512]{3,2,1,0:T(8,128)S(1)}) fusion(f32[3,4,16,512]{3,2,1,0:T(8,128)} %param.3, f32[1,4,16,512]{3,2,1,0:T(8,128)} %bitcast.163), kind=kLoop, calls=%fused_computation.168 | loop fusion | flops 131072 | bytes 1048576 | tf_op jit(solution)/shard_map/concatenate | solution.py:237
  2.4 3.4 %collective-permute-done.1 = f32[4,2,16,512]{3,2,1,0:T(8,128)S(1)} collective-permute-done((f32[4,2,16,512]{3,2,1,0:T(8,128)S(1)}, f32[4,2,16,512]{3,2,1,0:T(8,128)S(1)}, u32[]{:S(2)}, u32[]{:S(2)}) %collective-permute-start.1) | collective-permute-done | bytes 262176 | tf_op jit(solution)/shard_map/ppermute | solution.py:29
  5.8 2.1 %collective-permute-done = f32[4,2,16,512]{3,2,1,0:T(8,128)S(1)} collective-permute-done((f32[4,2,16,512]{3,2,1,0:T(8,128)S(1)}, f32[4,2,16,512]{3,2,1,0:T(8,128)S(1)}, u32[]{:S(2)}, u32[]{:S(2)}) %collective-permute-start) | collective-permute-done | bytes 262176 | tf_op jit(solution)/shard_map/ppermute | solution.py:27
  8.9 2.7 %collective-permute-start.3 = (f32[4,8,2,512]{3,2,1,0:T(2,128)S(1)}, f32[4,8,2,512]{3,2,1,0:T(2,128)S(1)}, u32[]{:S(2)}, u32[]{:S(2)}) collective-permute-start(f32[4,8,2,512]{3,2,1,0:T(2,128)S(1)} %get-tuple-element.17), channel_id=1, source_target_pairs={{1,0},{2,1},{3,2},{0,3},{5,4},{6,5},{7,6},{4,7},{9,8},{10,9},{11,1... | collective-permute-start | bytes 393224 | tf_op jit(solution)/shard_map/ppermute | solution.py:29
  11.6 3.1 %collective-permute-done.3 = f32[4,8,2,512]{3,2,1,0:T(2,128)S(1)} collective-permute-done((f32[4,8,2,512]{3,2,1,0:T(2,128)S(1)}, f32[4,8,2,512]{3,2,1,0:T(2,128)S(1)}, u32[]{:S(2)}, u32[]{:S(2)}) %collective-permute-start.3) | collective-permute-done | bytes 131104 | tf_op jit(solution)/shard_map/ppermute | solution.py:29
  14.7 3.4 %collective-permute-done.2 = f32[4,8,2,512]{3,2,1,0:T(2,128)S(1)} collective-permute-done((f32[4,8,2,512]{3,2,1,0:T(2,128)S(1)}, f32[4,8,2,512]{3,2,1,0:T(2,128)S(1)}, u32[]{:S(2)}, u32[]{:S(2)}) %collective-permute-start.2) | collective-permute-done | bytes 131104 | tf_op jit(solution)/shard_map/ppermute | solution.py:27
  19.3 1.7 %fusion.17 = (f32[3,6,18,514]{3,2,1,0:T(8,128)S(1)}, f32[3,6,18,514]{3,2,1,0:T(8,128)S(1)}, f32[3,6,18,514]{3,2,1,0:T(8,128)S(1)}) fusion(f32[3,8,20,516]{3,2,1,0:T(8,128)S(1)} %pad_maximum_fusion.1, f32[3,8,20,512]{3,2,1,0:T(8,128)S(1)} %slice_select_fusion, f32[3,8,20,2]{3,2,1,0:T(8,128)S(1)} %get-tuple-element.15, f32[3,8,20,2]{3,2,1,0:T(8,128)S(1)} %get-tuple-element.14), kind=kLoop, calls=%fused_computation.37 | loop fusion | flops 1332288 | bytes 5653728 | tf_op jit(solution)/shard_map/mul | solution.py:37
  22.6 1.4 %collective-permute-start.5 = (f32[3,2,16,512]{3,2,1,0:T(8,128)S(1)}, f32[3,2,16,512]{3,2,1,0:T(8,128)S(1)}, u32[]{:S(2)}, u32[]{:S(2)}) collective-permute-start(f32[3,2,16,512]{3,2,1,0:T(8,128)S(1)} %get-tuple-element.23), channel_id=1, source_target_pairs={{4,0},{8,4},{12,8},{16,12},{20,16},{24,20},{28,24},{32,28},{36,32}... | collective-permute-start | bytes 589832 | tf_op jit(solution)/shard_map/ppermute | solution.py:29
  25.3 1.9 %collective-permute-done.5 = f32[3,2,16,512]{3,2,1,0:T(8,128)S(1)} collective-permute-done((f32[3,2,16,512]{3,2,1,0:T(8,128)S(1)}, f32[3,2,16,512]{3,2,1,0:T(8,128)S(1)}, u32[]{:S(2)}, u32[]{:S(2)}) %collective-permute-start.5) | collective-permute-done | bytes 196640 | tf_op jit(solution)/shard_map/ppermute | solution.py:29
  27.2 9.7 %collective-permute-done.4 = f32[3,2,16,512]{3,2,1,0:T(8,128)S(1)} collective-permute-done((f32[3,2,16,512]{3,2,1,0:T(8,128)S(1)}, f32[3,2,16,512]{3,2,1,0:T(8,128)S(1)}, u32[]{:S(2)}, u32[]{:S(2)}) %collective-permute-start.4) | collective-permute-done | bytes 196640 | tf_op jit(solution)/shard_map/ppermute | solution.py:27
  37.1 2.0 %collective-permute-start.6 = (f32[3,8,2,512]{3,2,1,0:T(2,128)S(1)}, f32[3,8,2,512]{3,2,1,0:T(2,128)S(1)}, u32[]{:S(2)}, u32[]{:S(2)}) collective-permute-start(f32[3,8,2,512]{3,2,1,0:T(2,128)S(1)} %get-tuple-element.18), channel_id=1, source_target_pairs={{0,1},{1,2},{2,3},{3,0},{4,5},{5,6},{6,7},{7,4},{8,9},{9,10},{10,1... | collective-permute-start | bytes 294920 | tf_op jit(solution)/shard_map/ppermute | solution.py:27
  40.3 1.4 %collective-permute-done.7 = f32[3,8,2,512]{3,2,1,0:T(2,128)S(1)} collective-permute-done((f32[3,8,2,512]{3,2,1,0:T(2,128)S(1)}, f32[3,8,2,512]{3,2,1,0:T(2,128)S(1)}, u32[]{:S(2)}, u32[]{:S(2)}) %collective-permute-start.7) | collective-permute-done | bytes 98336 | tf_op jit(solution)/shard_map/ppermute | solution.py:29
  41.7 1.5 %collective-permute-done.6 = f32[3,8,2,512]{3,2,1,0:T(2,128)S(1)} collective-permute-done((f32[3,8,2,512]{3,2,1,0:T(2,128)S(1)}, f32[3,8,2,512]{3,2,1,0:T(2,128)S(1)}, u32[]{:S(2)}, u32[]{:S(2)}) %collective-permute-start.6) | collective-permute-done | bytes 98336 | tf_op jit(solution)/shard_map/ppermute | solution.py:27
  44.5 1.3 %fusion.15 = (f32[3,6,18,514]{3,2,1,0:T(8,128)S(1)}, f32[3,6,18,514]{3,2,1,0:T(8,128)S(1)}) fusion(f32[3,8,20,516]{3,2,1,0:T(8,128)S(1)} %pad_maximum_fusion.2), kind=kLoop, calls=%fused_computation.33 | loop fusion | flops 666144 | bytes 3996864 | tf_op jit(solution)/shard_map/mul | solution.py:37
  51.1 3.3 %collective-permute-done.8 = f32[128,128]{1,0:T(8,128)S(1)} collective-permute-done((f32[128,128]{1,0:T(8,128)S(1)}, f32[128,128]{1,0:T(8,128)S(1)}, u32[]{:S(2)}, u32[]{:S(2)}) %collective-permute-start.8) | collective-permute-done | bytes 65568 | tf_op jit(solution)/shard_map/ppermute | solution.py:231
  54.5 5.5 %collective-permute-done.9 = f32[128,128]{1,0:T(8,128)S(1)} collective-permute-done((f32[128,128]{1,0:T(8,128)S(1)}, f32[128,128]{1,0:T(8,128)S(1)}, u32[]{:S(2)}, u32[]{:S(2)}) %collective-permute-start.9) | collective-permute-done | bytes 65568 | tf_op jit(solution)/shard_map/ppermute | solution.py:231
  60.1 1.2 %collective-permute-done.10 = f32[128,128]{1,0:T(8,128)S(1)} collective-permute-done((f32[128,128]{1,0:T(8,128)S(1)}, f32[128,128]{1,0:T(8,128)S(1)}, u32[]{:S(2)}, u32[]{:S(2)}) %collective-permute-start.10) | collective-permute-done | bytes 65568 | tf_op jit(solution)/shard_map/ppermute | solution.py:231
  61.3 5.1 %collective-permute-start.11 = (f32[128,128]{1,0:T(8,128)S(1)}, f32[128,128]{1,0:T(8,128)S(1)}, u32[]{:S(2)}, u32[]{:S(2)}) collective-permute-start(f32[128,128]{1,0:T(8,128)S(1)} %add.337), channel_id=1, source_target_pairs={{0,8},{4,12},{8,0},{12,4},{16,24},{20,28},{24,16},{28,20},{32,40},... | collective-permute-start | bytes 196616 | tf_op jit(solution)/shard_map/ppermute | solution.py:231
  66.4 2.4 %collective-permute-done.11 = f32[128,128]{1,0:T(8,128)S(1)} collective-permute-done((f32[128,128]{1,0:T(8,128)S(1)}, f32[128,128]{1,0:T(8,128)S(1)}, u32[]{:S(2)}, u32[]{:S(2)}) %collective-permute-start.11) | collective-permute-done | bytes 65568 | tf_op jit(solution)/shard_map/ppermute | solution.py:231
  69.0 5.0 %collective-permute-done.12 = f32[128,128]{1,0:T(8,128)S(1)} collective-permute-done((f32[128,128]{1,0:T(8,128)S(1)}, f32[128,128]{1,0:T(8,128)S(1)}, u32[]{:S(2)}, u32[]{:S(2)}) %collective-permute-start.12) | collective-permute-done | bytes 65568 | tf_op jit(solution)/shard_map/ppermute | solution.py:231
  74.0 7.3 %collective-permute-done.13 = f32[128,128]{1,0:T(8,128)S(1)} collective-permute-done((f32[128,128]{1,0:T(8,128)S(1)}, f32[128,128]{1,0:T(8,128)S(1)}, u32[]{:S(2)}, u32[]{:S(2)}) %collective-permute-start.13) | collective-permute-done | bytes 65568 | tf_op jit(solution)/shard_map/ppermute | solution.py:231
  81.4 4.3 %collective-permute-done.14 = f32[128,128]{1,0:T(8,128)S(1)} collective-permute-done((f32[128,128]{1,0:T(8,128)S(1)}, f32[128,128]{1,0:T(8,128)S(1)}, u32[]{:S(2)}, u32[]{:S(2)}) %collective-permute-start.14) | collective-permute-done | bytes 65568 | tf_op jit(solution)/shard_map/ppermute | solution.py:231
  86.0 5.5 %collective-permute-done.15 = f32[128,128]{1,0:T(8,128)S(1)} collective-permute-done((f32[128,128]{1,0:T(8,128)S(1)}, f32[128,128]{1,0:T(8,128)S(1)}, u32[]{:S(2)}, u32[]{:S(2)}) %collective-permute-start.15) | collective-permute-done | bytes 65568 | tf_op jit(solution)/shard_map/ppermute | solution.py:231
  91.5 16.0 %basis.1 = f32[1344,128]{1,0:T(8,128)} custom-call(f32[128,128]{1,0:T(8,128)S(1)} %add.342.total_ref, f32[128,1536]{1,0:T(8,128)S(1)} %fusion.snap_ref), custom_call_target="tpu_custom_call" | custom-call | tf_op jit(solution)/shard_map/basis/pallas_call | solution.py:207
  (66 shorter events, 14.4 us)
Async XLA Ops:
  0.6 7.3 %copy-start = (f32[3,4,16,512]{3,2,1,0:T(8,128)S(1)}, f32[3,4,16,512]{3,2,1,0:T(8,128)}, u32[]{:S(2)}) copy-start(f32[3,4,16,512]{3,2,1,0:T(8,128)} %param.3) | copy-start | bytes 1179652
  0.6 17.5 %copy-start.1 = (f32[4,16,512]{2,1,0:T(8,128)S(1)}, f32[4,16,512]{2,1,0:T(8,128)}, u32[]{:S(2)}) copy-start(f32[4,16,512]{2,1,0:T(8,128)} %param.4) | copy-start | bytes 393220
  1.8 4.0 %collective-permute-start.1 = (f32[4,2,16,512]{3,2,1,0:T(8,128)S(1)}, f32[4,2,16,512]{3,2,1,0:T(8,128)S(1)}, u32[]{:S(2)}, u32[]{:S(2)}) collective-permute-start(f32[4,2,16,512]{3,2,1,0:T(8,128)S(1)} %get-tuple-element.21), channel_id=1, source_target_pairs={{4,0},{8,4},{12,8},{16,12},{20,16},{24,20},{28,24},{32,28},{36,32}... | collective-permute-start | bytes 786440 | tf_op jit(solution)/shard_map/ppermute | solution.py:29
  1.9 6.0 %collective-permute-start = (f32[4,2,16,512]{3,2,1,0:T(8,128)S(1)}, f32[4,2,16,512]{3,2,1,0:T(8,128)S(1)}, u32[]{:S(2)}, u32[]{:S(2)}) collective-permute-start(f32[4,2,16,512]{3,2,1,0:T(8,128)S(1)} %get-tuple-element.20), channel_id=1, source_target_pairs={{0,4},{4,8},{8,12},{12,16},{16,20},{20,24},{24,28},{28,32},{32,36}... | collective-permute-start | bytes 786440 | tf_op jit(solution)/shard_map/ppermute | solution.py:27
  8.9 5.8 %collective-permute-start.3 = (f32[4,8,2,512]{3,2,1,0:T(2,128)S(1)}, f32[4,8,2,512]{3,2,1,0:T(2,128)S(1)}, u32[]{:S(2)}, u32[]{:S(2)}) collective-permute-start(f32[4,8,2,512]{3,2,1,0:T(2,128)S(1)} %get-tuple-element.17), channel_id=1, source_target_pairs={{1,0},{2,1},{3,2},{0,3},{5,4},{6,5},{7,6},{4,7},{9,8},{10,9},{11,1... | collective-permute-start | bytes 393224 | tf_op jit(solution)/shard_map/ppermute | solution.py:29
  11.6 6.5 %collective-permute-start.2 = (f32[4,8,2,512]{3,2,1,0:T(2,128)S(1)}, f32[4,8,2,512]{3,2,1,0:T(2,128)S(1)}, u32[]{:S(2)}, u32[]{:S(2)}) collective-permute-start(f32[4,8,2,512]{3,2,1,0:T(2,128)S(1)} %get-tuple-element.16), channel_id=1, source_target_pairs={{0,1},{1,2},{2,3},{3,0},{4,5},{5,6},{6,7},{7,4},{8,9},{9,10},{10,1... | collective-permute-start | bytes 393224 | tf_op jit(solution)/shard_map/ppermute | solution.py:27
  22.6 4.6 %collective-permute-start.5 = (f32[3,2,16,512]{3,2,1,0:T(8,128)S(1)}, f32[3,2,16,512]{3,2,1,0:T(8,128)S(1)}, u32[]{:S(2)}, u32[]{:S(2)}) collective-permute-start(f32[3,2,16,512]{3,2,1,0:T(8,128)S(1)} %get-tuple-element.23), channel_id=1, source_target_pairs={{4,0},{8,4},{12,8},{16,12},{20,16},{24,20},{28,24},{32,28},{36,32}... | collective-permute-start | bytes 589832 | tf_op jit(solution)/shard_map/ppermute | solution.py:29
  24.0 12.9 %collective-permute-start.4 = (f32[3,2,16,512]{3,2,1,0:T(8,128)S(1)}, f32[3,2,16,512]{3,2,1,0:T(8,128)S(1)}, u32[]{:S(2)}, u32[]{:S(2)}) collective-permute-start(f32[3,2,16,512]{3,2,1,0:T(8,128)S(1)} %get-tuple-element.22), channel_id=1, source_target_pairs={{0,4},{4,8},{8,12},{12,16},{16,20},{20,24},{24,28},{28,32},{32,36}... | collective-permute-start | bytes 589832 | tf_op jit(solution)/shard_map/ppermute | solution.py:27
  37.0 4.7 %collective-permute-start.7 = (f32[3,8,2,512]{3,2,1,0:T(2,128)S(1)}, f32[3,8,2,512]{3,2,1,0:T(2,128)S(1)}, u32[]{:S(2)}, u32[]{:S(2)}) collective-permute-start(f32[3,8,2,512]{3,2,1,0:T(2,128)S(1)} %get-tuple-element.19), channel_id=1, source_target_pairs={{1,0},{2,1},{3,2},{0,3},{5,4},{6,5},{7,6},{4,7},{9,8},{10,9},{11,1... | collective-permute-start | bytes 294920 | tf_op jit(solution)/shard_map/ppermute | solution.py:29
  37.1 6.1 %collective-permute-start.6 = (f32[3,8,2,512]{3,2,1,0:T(2,128)S(1)}, f32[3,8,2,512]{3,2,1,0:T(2,128)S(1)}, u32[]{:S(2)}, u32[]{:S(2)}) collective-permute-start(f32[3,8,2,512]{3,2,1,0:T(2,128)S(1)} %get-tuple-element.18), channel_id=1, source_target_pairs={{0,1},{1,2},{2,3},{3,0},{4,5},{5,6},{6,7},{7,4},{8,9},{9,10},{10,1... | collective-permute-start | bytes 294920 | tf_op jit(solution)/shard_map/ppermute | solution.py:27
  47.2 1.2 %copy-start.2 = (f32[3,4,16,512]{3,2,1,0:T(8,128)}, f32[3,4,16,512]{3,2,1,0:T(8,128)S(1)}, u32[]{:S(2)}) copy-start(f32[3,4,16,512]{3,2,1,0:T(8,128)S(1)} %fusion.29) | copy-start | bytes 1179652
  47.3 1.3 %copy-start.3 = (s32[128]{0:T(128)S(1)}, s32[128]{0:T(128)}, u32[]{:S(2)}) copy-start(s32[128]{0:T(128)} %param.5) | copy-start | bytes 1540
  50.0 4.4 %collective-permute-start.8 = (f32[128,128]{1,0:T(8,128)S(1)}, f32[128,128]{1,0:T(8,128)S(1)}, u32[]{:S(2)}, u32[]{:S(2)}) collective-permute-start(f32[128,128]{1,0:T(8,128)S(1)} %fusion.146), channel_id=1, source_target_pairs={{0,1},{1,0},{2,3},{3,2},{4,5},{5,4},{6,7},{7,6},{8,9},{9,8},{10,11... | collective-permute-start | bytes 196616 | tf_op jit(solution)/shard_map/ppermute | solution.py:231
  54.4 5.6 %collective-permute-start.9 = (f32[128,128]{1,0:T(8,128)S(1)}, f32[128,128]{1,0:T(8,128)S(1)}, u32[]{:S(2)}, u32[]{:S(2)}) collective-permute-start(f32[128,128]{1,0:T(8,128)S(1)} %add.335), channel_id=1, source_target_pairs={{0,3},{1,2},{2,1},{3,0},{4,7},{5,6},{6,5},{7,4},{8,11},{9,10},{10,... | collective-permute-start | bytes 196616 | tf_op jit(solution)/shard_map/ppermute | solution.py:231
  60.0 1.3 %collective-permute-start.10 = (f32[128,128]{1,0:T(8,128)S(1)}, f32[128,128]{1,0:T(8,128)S(1)}, u32[]{:S(2)}, u32[]{:S(2)}) collective-permute-start(f32[128,128]{1,0:T(8,128)S(1)} %add.336), channel_id=1, source_target_pairs={{0,4},{4,0},{8,12},{12,8},{16,20},{20,16},{24,28},{28,24},{32,36},... | collective-permute-start | bytes 196616 | tf_op jit(solution)/shard_map/ppermute | solution.py:231
  61.3 7.5 %collective-permute-start.11 = (f32[128,128]{1,0:T(8,128)S(1)}, f32[128,128]{1,0:T(8,128)S(1)}, u32[]{:S(2)}, u32[]{:S(2)}) collective-permute-start(f32[128,128]{1,0:T(8,128)S(1)} %add.337), channel_id=1, source_target_pairs={{0,8},{4,12},{8,0},{12,4},{16,24},{20,28},{24,16},{28,20},{32,40},... | collective-permute-start | bytes 196616 | tf_op jit(solution)/shard_map/ppermute | solution.py:231
  68.9 5.1 %collective-permute-start.12 = (f32[128,128]{1,0:T(8,128)S(1)}, f32[128,128]{1,0:T(8,128)S(1)}, u32[]{:S(2)}, u32[]{:S(2)}) collective-permute-start(f32[128,128]{1,0:T(8,128)S(1)} %add.338), channel_id=1, source_target_pairs={{0,24},{4,28},{8,16},{12,20},{16,8},{20,12},{24,0},{28,4},{32,56},... | collective-permute-start | bytes 196616 | tf_op jit(solution)/shard_map/ppermute | solution.py:231
  73.9 7.4 %collective-permute-start.13 = (f32[128,128]{1,0:T(8,128)S(1)}, f32[128,128]{1,0:T(8,128)S(1)}, u32[]{:S(2)}, u32[]{:S(2)}) collective-permute-start(f32[128,128]{1,0:T(8,128)S(1)} %add.339), channel_id=1, source_target_pairs={{0,56},{4,60},{8,48},{12,52},{16,40},{20,44},{24,32},{28,36},{32,2... | collective-permute-start | bytes 196616 | tf_op jit(solution)/shard_map/ppermute | solution.py:231
  81.3 4.4 %collective-permute-start.14 = (f32[128,128]{1,0:T(8,128)S(1)}, f32[128,128]{1,0:T(8,128)S(1)}, u32[]{:S(2)}, u32[]{:S(2)}) collective-permute-start(f32[128,128]{1,0:T(8,128)S(1)} %add.340), channel_id=1, source_target_pairs={{0,64},{4,68},{8,72},{12,76},{16,80},{20,84},{24,88},{28,92},{32,9... | collective-permute-start | bytes 196616 | tf_op jit(solution)/shard_map/ppermute | solution.py:231
  85.7 5.8 %collective-permute-start.15 = (f32[128,128]{1,0:T(8,128)S(1)}, f32[128,128]{1,0:T(8,128)S(1)}, u32[]{:S(2)}, u32[]{:S(2)}) collective-permute-start(f32[128,128]{1,0:T(8,128)S(1)} %add.341), channel_id=1, source_target_pairs={{0,192},{4,196},{8,200},{12,204},{16,208},{20,212},{24,216},{28,22... | collective-permute-start | bytes 196616 | tf_op jit(solution)/shard_map/ppermute | solution.py:231
where the time goes:
time: 108 us
  waiting for transfers between devices  60.8 us (56%)
  Pallas kernels  16 us (15%)
  starting transfers between devices  13.8 us (13%)
  other arithmetic  10.3 us (10%)
  matrix products  3.89 us (4%)
  local copies, waits for them, and re-layouts  1.75 us (2%)
    ppermute x8, waiting for transfers between devices, device_sum(): lax.ppermute(part, axis, [(i, partner(i)) for i in range(count)])  34.3 us
    ppermute x4, waiting for transfers between devices, with_halo(): lax.ppermute(tail, axis, [(i, (i + 1) % count) for i in range(count)])  16.7 us
    pallas_call x1, Pallas kernels, project(): pl.pallas_call(functools.partial(basis_kernel, rows_all=rows_all), out_sh...  16 us
    ppermute x4, waiting for transfers between devices, with_halo(): lax.ppermute(head, axis, [((i + 1) % count, i) for i in range(count)])  9.74 us
    ppermute x8, starting transfers between devices, device_sum(): lax.ppermute(part, axis, [(i, partner(i)) for i in range(count)])  6.97 us
    ppermute x4, starting transfers between devices, with_halo(): lax.ppermute(head, axis, [((i + 1) % count, i) for i in range(count)])  4.27 us
    mul x2, other arithmetic, advance(): (velocity_ext[:, 2:, 1:-1, 1:-1] - velocity_ext[:, :-2, 1:-1, 1:-1]) * 0.5  2.94 us
    ppermute x4, starting transfers between devices, with_halo(): lax.ppermute(tail, axis, [(i, (i + 1) % count) for i in range(count)])  2.52 us
  transfers between devices with their start and end apart: 16, of which 16 were waited for; matrix products, arithmetic and copies ran while one was open for 2% of the time, Pallas kernels for 0%

commit v1 on v0

v1 whole, which is shorter than its diff:
```python
import functools

import jax
import jax.numpy as jnp
from jax import lax
from jax.experimental import pallas as pl
from jax.experimental.pallas import tpu as pltpu
from jax.sharding import PartitionSpec as P

RANK = 112
ITERS = 3
PANEL = 8
LANES = 128
SLOT = 16


nu_limit = 0.125
ridge = 1.0
highest = lax.Precision.HIGHEST


def recip(value):
    guess = pl.reciprocal(value, approx=True)
    return guess * (2.0 - value * guess)


def spread(block, lane):
    return jnp.broadcast_to(block[:, lane : lane + 1], block.shape)


def repeat(block, row):
    return jnp.broadcast_to(block[row : row + 1, :], block.shape)


def orthonormal_rows(inner, wide):
    panels = RANK // PANEL
    row_id = lax.broadcasted_iota(jnp.int32, (PANEL, inner.shape[1]), 0)
    left = [inner[PANEL * k : PANEL * (k + 1), :] for k in range(panels)]
    right = [wide[PANEL * k : PANEL * (k + 1), :] for k in range(panels)]
    rows = []
    for k in range(panels):
        follows = k + 1 < panels
        own_left, own_right = left[k], right[k]
        own_cols = [spread(own_left, PANEL * k + j) for j in range(PANEL)]
        if follows:
            next_left, next_right = left[k + 1], right[k + 1]
            next_cols = [spread(next_left, PANEL * k + j) for j in range(PANEL)]
        pivots = jnp.ones_like(own_left)
        for j in range(PANEL):
            pivot = repeat(own_cols[j], j)
            inverse = recip(pivot)
            pivots = jnp.where(row_id == j, pivot, pivots)
            own_factor = own_cols[j] * inverse
            for m in range(j + 1, PANEL):
                own_cols[m] = own_cols[m] - own_factor * repeat(own_cols[j], m)
            row_left, row_right = repeat(own_left, j), repeat(own_right, j)
            if follows:
                next_factor = next_cols[j] * inverse
                for m in range(j + 1, PANEL):
                    next_cols[m] = next_cols[m] - next_factor * repeat(own_cols[j], m)
                next_left = next_left - next_factor * row_left
                next_right = next_right - next_factor * row_right
            below = jnp.where(row_id > j, own_factor, 0.0)
            own_left = own_left - below * row_left
            own_right = own_right - below * row_right
        if follows:
            left[k + 1], right[k + 1] = next_left, next_right
        if k + 2 < panels:
            scale = recip(pivots)
            update = lax.dot_general(
                own_left[:, PANEL * (k + 2) : RANK],
                jnp.concatenate([own_left * scale, own_right * scale], axis=1),
                (((0,), (0,)), ((), ())),
                precision=highest,
                preferred_element_type=jnp.float32,
            )
            width = own_left.shape[1]
            for m in range(k + 2, panels):
                start = PANEL * (m - k - 2)
                left[m] = left[m] - update[start : start + PANEL, :width]
                right[m] = right[m] - update[start : start + PANEL, width:]
        root = lax.rsqrt(pivots)
        rows.append(own_right * (root * (1.5 - 0.5 * pivots * root * root)))
    return jnp.concatenate(rows, axis=0)


def basis_kernel(total_ref, snap_ref, out_ref, basis_ref, *, rows_all):
    cols = total_ref.shape[0]
    row_id = lax.broadcasted_iota(jnp.int32, (cols, cols), 0)
    col_id = lax.broadcasted_iota(jnp.int32, (cols, cols), 1)
    gram_matrix = total_ref[...] / rows_all + jnp.where(row_id == col_id, jnp.float32(ridge), 0.0)

    def sweep(step, carry):
        @pl.when(step == 0)
        def _():
            basis_ref[...] = gram_matrix[:RANK, :]

        @pl.when(step > 0)
        def _():
            basis_ref[...] = jnp.dot(
                basis_ref[...], gram_matrix, precision=highest, preferred_element_type=jnp.float32
            )

        wide = basis_ref[...]
        full = jnp.concatenate([wide, jnp.zeros((cols - RANK, cols), jnp.float32)], axis=0)
        inner = lax.dot_general(
            wide, full, (((1,), (1,)), ((), ())), precision=highest, preferred_element_type=jnp.float32
        )
        basis_ref[...] = orthonormal_rows(inner, wide)
        return carry

    lax.fori_loop(0, ITERS, sweep, 0)
    basis = basis_ref[...]
    blocks, cols = out_ref.shape[0] // RANK, basis.shape[1]
    for block in range(blocks):
        out_ref[pl.ds(block, RANK, stride=blocks), :] = jnp.dot(
            basis,
            snap_ref[pl.ds(block, cols, stride=SLOT), :],
            precision=highest,
            preferred_element_type=jnp.float32,
        )


def project(gram_total, snapshots, rows_all):
    cols = gram_total.shape[0]
    return pl.pallas_call(
        functools.partial(basis_kernel, rows_all=rows_all),
        out_shape=jax.ShapeDtypeStruct((RANK * 12, LANES), jnp.float32),
        in_specs=[pl.BlockSpec(memory_space=pltpu.VMEM)] * 2,
        out_specs=pl.BlockSpec(memory_space=pltpu.VMEM),
        scratch_shapes=[pltpu.VMEM((RANK, cols), jnp.float32)],
        compiler_params=pltpu.CompilerParams(vmem_limit_bytes=16 * 2**20),
        name="basis",
    )(gram_total, snapshots)


def exact_dot(values, one_hot):
    high = values.astype(jnp.bfloat16)
    rest = values - high.astype(jnp.float32)
    middle = rest.astype(jnp.bfloat16)
    low = (rest - middle.astype(jnp.float32)).astype(jnp.bfloat16)
    dot = functools.partial(jnp.dot, preferred_element_type=jnp.float32)
    return (dot(low, one_hot) + dot(middle, one_hot)) + dot(high, one_hot)


def sorting(size, to_sorted):
    cell = lax.broadcasted_iota(jnp.int32, (size, size), 0 if to_sorted else 1)
    spot = lax.broadcasted_iota(jnp.int32, (size, size), 1 if to_sorted else 0)
    place = (cell & 3) * (size // 4) + (cell >> 2)
    return jnp.where(place == spot, 1.0, 0.0).astype(jnp.bfloat16)


def pack_kernel(velocity_ref, coef_ref, block_ref, low_ref, high_ref):
    rows_y, rows_z, size_x = coef_ref.shape
    rows = jnp.concatenate(
        [velocity_ref[c].reshape(-1, size_x) for c in range(3)] + [coef_ref[...].reshape(-1, size_x)]
    )
    done = exact_dot(rows, sorting(size_x, True))
    for c in range(4):
        for y in range(rows_y):
            start = (c * rows_y + y) * rows_z
            for o in range(4):
                plane = done[start : start + rows_z, LANES * o : LANES * (o + 1)]
                block_ref[c, y, o] = plane
                low_ref[c, y, 4 * o : 4 * o + 4, :] = plane[:4]
                high_ref[c, y, 4 * o : 4 * o + 4, :] = plane[rows_z - 4 :]


def pack(velocity, smag_coef):
    rows_y, rows_z, size_x = smag_coef.shape
    edge = jax.ShapeDtypeStruct((4, rows_y, 16, LANES), jnp.float32)
    return pl.pallas_call(
        pack_kernel,
        out_shape=(jax.ShapeDtypeStruct((4, rows_y, 4, rows_z, LANES), jnp.float32), edge, edge),
        in_specs=[pl.BlockSpec(memory_space=pltpu.VMEM)] * 2,
        out_specs=[pl.BlockSpec(memory_space=pltpu.VMEM)] * 3,
        compiler_params=pltpu.CompilerParams(vmem_limit_bytes=24 * 2**20),
        name="pack",
    )(velocity, smag_coef)


def around_x(ref, index, o):
    ahead = ref[(*index, o + 1)] if o < 3 else pltpu.roll(ref[(*index, 0)], LANES - 1, 1)
    behind = ref[(*index, o - 1)] if o > 0 else pltpu.roll(ref[(*index, 3)], 1, 1)
    return ahead, behind


def around_z(plane):
    return pltpu.roll(plane, plane.shape[0] - 1, 0), pltpu.roll(plane, 1, 0)


def half_viscosity(cells_ref, y, o, coefficient):
    jump = []
    for c in range(3):
        x_ahead, x_behind = around_x(cells_ref, (c, y), o)
        z_ahead, z_behind = around_z(cells_ref[c, y, o])
        jump.append(
            (x_ahead - x_behind, cells_ref[c, y + 1, o] - cells_ref[c, y - 1, o], z_ahead - z_behind)
        )
    total = jump[0][0] ** 2 + jump[1][1] ** 2 + jump[2][2] ** 2
    total = total + total
    for c, d in ((0, 1), (0, 2), (1, 2)):
        total = total + (jump[c][d] + jump[d][c]) ** 2
    rate = coefficient * (0.5 * jnp.sqrt(total))
    return (0.5 * nu_limit) * rate * recip(1.0 + rate)


def stepped(cells_ref, y, visc_ref, v, o):
    here = visc_ref[v, o]
    visc = [*around_x(visc_ref, (v,), o), visc_ref[v + 1, o], visc_ref[v - 1, o], *around_z(here)]
    visc = [here + other for other in visc]
    result = []
    for c in range(3):
        centre = cells_ref[c, y, o]
        cells = [
            *around_x(cells_ref, (c, y), o),
            cells_ref[c, y + 1, o],
            cells_ref[c, y - 1, o],
            *around_z(centre),
        ]
        change = visc[0] * (cells[0] - centre)
        for n in range(1, 6):
            change = change + visc[n] * (cells[n] - centre)
        result.append(centre + change)
    return result


def steps_kernel(
    place_ref, block_ref, before_ref, after_ref, low_ref, high_ref, corner_before_ref, corner_after_ref,
    final_ref, snap_ref, gram_ref,
    cells_ref, visc_ref, one_ref, two_ref, wide_ref, all_ref,
):
    rows_y, rows_z = block_ref.shape[1], block_ref.shape[3]
    cols = gram_ref.shape[0]
    first, last = place_ref[cols] == 1, place_ref[cols + 1] == 1
    over, under = slice(rows_z, rows_z + 4), slice(rows_z + 4, rows_z + 8)
    for c in range(4):
        for y in range(rows_y):
            for o in range(4):
                rows = slice(4 * o, 4 * o + 4)
                own, above, below = rows_y + y, 2 * rows_y + y, y
                cells_ref[c, own, o, :rows_z] = block_ref[c, y, o]
                cells_ref[c, own, o, over] = high_ref[c, y, rows]
                cells_ref[c, own, o, under] = low_ref[c, y, rows]
                cells_ref[c, below, o, :rows_z] = before_ref[c, y, o]
                cells_ref[c, above, o, :rows_z] = after_ref[c, y, o]
                if y > 0:
                    cells_ref[c, below, o, over] = corner_before_ref[c, 3 + y - 1, rows]
                    cells_ref[c, below, o, under] = corner_before_ref[c, y - 1, rows]
                if y < rows_y - 1:
                    cells_ref[c, above, o, over] = corner_after_ref[c, 3 + y, rows]
                    cells_ref[c, above, o, under] = corner_after_ref[c, y, rows]

    @pl.when(first)
    def _():
        for y in range(1, rows_y):
            cells_ref[3, y] = cells_ref[3, rows_y]

    @pl.when(last)
    def _():
        for y in range(rows_y - 1):
            cells_ref[3, 2 * rows_y + y] = cells_ref[3, 2 * rows_y - 1]

    def visc_one(y, carry):
        for o in range(4):
            visc_ref[y, o] = half_viscosity(cells_ref, y, o, cells_ref[3, y, o])
        return carry

    lax.fori_loop(1, 3 * rows_y - 1, visc_one, 0)

    def step_one(y, carry):
        outside = jnp.logical_or(
            jnp.logical_and(first, y < rows_y), jnp.logical_and(last, y >= 2 * rows_y)
        )
        for o in range(4):
            for c, cells in enumerate(stepped(cells_ref, y, visc_ref, y, o)):
                one_ref[c, y, o] = jnp.where(outside, 0.0, cells)
        return carry

    lax.fori_loop(2, 3 * rows_y - 2, step_one, 0)

    def visc_two(y, carry):
        for o in range(4):
            visc_ref[y, o] = half_viscosity(one_ref, y, o, cells_ref[3, y, o])
        return carry

    lax.fori_loop(rows_y - 1, 2 * rows_y + 1, visc_two, 0)

    for y in range(rows_y):
        for o in range(4):
            for c, cells in enumerate(stepped(one_ref, rows_y + y, visc_ref, rows_y + y, o)):
                two_ref[c, y, o] = cells[:rows_z]
                start = (c * rows_y + y) * rows_z
                wide_ref[start : start + rows_z, LANES * o : LANES * (o + 1)] = cells[:rows_z]
    final_ref[...] = exact_dot(wide_ref[...], sorting(4 * LANES, False)).reshape(final_ref.shape)

    for state, (ref, shift) in enumerate(((block_ref, 0), (one_ref, rows_y), (two_ref, 0))):
        for y in range(rows_y):
            for z in range(4):
                for o in range(4):
                    start = SLOT * (64 * state + 16 * y + 4 * z + o)
                    for c in range(3):
                        piece = ref[c, shift + y, o, pl.ds(z, rows_z // 4, stride=4), :]
                        all_ref[start + 4 * c : start + 4 * c + 4, :] = piece

    def choose(column, carry):
        source = pl.multiple_of(place_ref[column] * SLOT, SLOT)
        target = pl.multiple_of(column * SLOT, SLOT)
        snap_ref[pl.ds(target, SLOT), :] = all_ref[pl.ds(source, SLOT), :]
        return carry

    lax.fori_loop(0, cols, choose, 0, unroll=8)
    gram = jnp.zeros((cols, cols), jnp.float32)
    for block in range(0, 12, 2):
        part = jnp.concatenate(
            [snap_ref[pl.ds(block + i, cols, stride=SLOT), :] for i in range(2)], axis=1
        )
        gram = gram + lax.dot_general(
            part, part, (((1,), (1,)), ((), ())), precision=highest, preferred_element_type=jnp.float32
        )
    gram_ref[...] = gram


def both_steps(place, block, *halo):
    _, rows_y, _, rows_z, _ = block.shape
    cols = place.shape[0] - 2
    f32 = lambda *shape: jax.ShapeDtypeStruct(shape, jnp.float32)
    scratch = lambda *shape: pltpu.VMEM(shape, jnp.float32)
    depth = rows_z + 8
    return pl.pallas_call(
        steps_kernel,
        out_shape=(
            f32(3, rows_y, rows_z, 4 * LANES),
            f32(SLOT * cols, LANES),
            f32(cols, cols),
        ),
        in_specs=[pl.BlockSpec(memory_space=pltpu.SMEM)]
        + [pl.BlockSpec(memory_space=pltpu.VMEM)] * (1 + len(halo)),
        out_specs=[pl.BlockSpec(memory_space=pltpu.VMEM)] * 3,
        scratch_shapes=[
            scratch(4, 3 * rows_y, 4, depth, LANES),
            scratch(3 * rows_y, 4, depth, LANES),
            scratch(3, 3 * rows_y, 4, depth, LANES),
            scratch(3, rows_y, 4, rows_z, LANES),
            scratch(3 * rows_y * rows_z, 4 * LANES),
            scratch(SLOT * 192, LANES),
        ],
        compiler_params=pltpu.CompilerParams(vmem_limit_bytes=32 * 2**20),
        name="steps",
    )(place, block, *halo)


def device_sum(part):
    steps = [
        ("gz", lambda i: i ^ 1),
        ("gz", lambda i: 3 - i),
        ("gy", lambda i: i ^ 1),
        ("gy", lambda i: i ^ 2),
        ("gy", lambda i: i ^ 6),
        ("gy", lambda i: i ^ 14),
        ("gy", lambda i: i ^ 16),
        ("gy", lambda i: i ^ 48),
    ]
    for axis, partner in steps:
        count = lax.axis_size(axis)
        part = part + lax.ppermute(part, axis, [(i, partner(i)) for i in range(count)])
    return part


def local(velocity, smag_coef, snap_code):
    block, low, high = pack(velocity, smag_coef)
    count_y, count_z = lax.axis_size("gy"), lax.axis_size("gz")

    def along_z(part, step):
        return lax.ppermute(part, "gz", [(i, (i + step) % count_z) for i in range(count_z)])

    def along_y(part, step):
        pairs = [(i, i + step) for i in range(count_y) if 0 <= i + step < count_y]
        return lax.ppermute(part, "gy", pairs)

    from_low, from_high = along_z(high, 1), along_z(low, -1)
    before, after = along_y(block, 1), along_y(block, -1)
    corner_before = along_y(jnp.concatenate([from_low[:, 1:], from_high[:, 1:]], axis=1), 1)
    corner_after = along_y(jnp.concatenate([from_low[:, :-1], from_high[:, :-1]], axis=1), -1)
    row = lax.axis_index("gy")
    walls = jnp.stack([row == 0, row == count_y - 1]).astype(jnp.int32)
    final, snapshots, gram = both_steps(
        jnp.concatenate([snap_code, walls]),
        block, before, after, from_low, from_high, corner_before, corner_after,
    )
    rows_y, rows_z = velocity.shape[1], velocity.shape[2]
    rows_all = 12 * LANES * count_y * count_z
    pod_modes = project(device_sum(gram), snapshots, rows_all)
    return (final, pod_modes.reshape(RANK, 3, rows_y // 4, rows_z // 4, LANES))


def solution(mesh):
    placed = (P(None, "gy", "gz", None), P("gy", "gz", None), P())
    return jax.shard_map(
        local,
        mesh=mesh,
        in_specs=placed,
        out_specs=(P(None, "gy", "gz", None), P(None, None, "gy", "gz", None)),
        check_vma=False,
    )
```

time: 108 us -> 92.9 us (0.86); the launches traced: 108 us -> 91.2 us
  waiting for transfers between devices: 60.8 us -> 37.7 us
  starting transfers between devices: 13.8 us -> 26.5 us
  other arithmetic: 10.3 us -> 0.19 us
  Pallas kernels: 16 us -> 23.5 us
  matrix products: 3.89 us -> 0 us
    ppermute x8 -> x6, waiting for transfers between devices: 26.4 us -> 9.54 us  [the longest x2 7.03 us: along_z(): lax.ppermute(part, 'gz', [(i, (i + step) % count_z) for i in range(count_...]
    pallas_call x0 -> x2, Pallas kernels: none -> 7.39 us  [the longest x1 6.74 us: both_steps(): pl.pallas_call(steps_kernel, out_shape=(f32(3, rows_y, rows_z, 4 * LANES)...]
    ppermute x8, starting transfers between devices: 6.97 us -> 13.7 us  [device_sum(): lax.ppermute(part, axis, [(i, partner(i)) for i in range(count)])]
    ppermute x8, waiting for transfers between devices: 34.3 us -> 28.2 us  [device_sum(): lax.ppermute(part, axis, [(i, partner(i)) for i in range(count)])]
    ppermute x8 -> x6, starting transfers between devices: 6.79 us -> 12.8 us  [the longest x4 9.88 us: along_y(): return lax.ppermute(part, 'gy', pairs)]
    mul x5 -> x0, other arithmetic: 3.9 us -> none  [the longest x2 2.94 us: advance(): (velocity_ext[:, 2:, 1:-1, 1:-1] - velocity_ext[:, :-2, 1:-1, 1:-1]) * 0.5]
    dot_general x5 -> x0, matrix products: 3.89 us -> none  [the longest x3 2.46 us: decimate(): jnp.dot(field_data.reshape(-1, size_x), sorting, precision=highest)]
    unnamed x8 -> x6, local copies, waits for them, and re-layouts: 0.02 us -> 2.46 us
  transfers between devices with their start and end apart: 16 -> 14, of which waited for: 16 -> 11; matrix products, arithmetic and copies ran while one was open for 2% -> 0% of each run, Pallas kernels for 0% -> 0%
where the time goes in v1:
time: 92.9 us; the launch traced here: 91.2 us
  waiting for transfers between devices  37.7 us (41%)
  starting transfers between devices  26.5 us (29%)
  Pallas kernels  23.5 us (25%)
  local copies, waits for them, and re-layouts  2.49 us (3%)
    ppermute x8, waiting for transfers between devices, device_sum(): lax.ppermute(part, axis, [(i, partner(i)) for i in range(count)])  28.2 us
    pallas_call x1, Pallas kernels, project(): pl.pallas_call(functools.partial(basis_kernel, rows_all=rows_all), out_sh...  16.1 us
    ppermute x8, starting transfers between devices, device_sum(): lax.ppermute(part, axis, [(i, partner(i)) for i in range(count)])  13.7 us
    ppermute x4, starting transfers between devices, along_y(): return lax.ppermute(part, 'gy', pairs)  9.88 us
    ppermute x2, waiting for transfers between devices, along_z(): lax.ppermute(part, 'gz', [(i, (i + step) % count_z) for i in range(count_...  7.03 us
    pallas_call x1, Pallas kernels, both_steps(): pl.pallas_call(steps_kernel, out_shape=(f32(3, rows_y, rows_z, 4 * LANES)...  6.74 us
    ppermute x2, starting transfers between devices, along_z(): lax.ppermute(part, 'gz', [(i, (i + step) % count_z) for i in range(count_...  2.92 us
    ppermute x4, waiting for transfers between devices, along_y(): return lax.ppermute(part, 'gy', pairs)  2.5 us
  transfers between devices with their start and end apart: 14, of which 11 were waited for; matrix products, arithmetic and copies ran while one was open for 0% of the time, Pallas kernels for 0%

profile of v1, /device:TPU:32, one launch (start us, length us, event | category | flops | bytes accessed | tf_op | source)
XLA Modules:
  0.0 91.2 jit_solution(7186457236524680153)
XLA Ops:
  0.6 1.0 %copy-done = f32[3,4,16,512]{3,2,1,0:T(8,128)S(1)} copy-done((f32[3,4,16,512]{3,2,1,0:T(8,128)S(1)}, f32[3,4,16,512]{3,2,1,0:T(8,128)}, u32[]{:S(2)}) %copy-start) | copy-done | bytes 393240
  1.6 0.9 copy-done.1
  3.2 2.8 %collective-permute-start.3 = (f32[4,4,16,128]{3,2,1,0:T(8,128)S(1)}, f32[4,4,16,128]{3,2,1,0:T(8,128)S(1)}, u32[]{:S(2)}, u32[]{:S(2)}) collective-permute-start(f32[4,4,16,128]{3,2,1,0:T(8,128)S(1)} %get-tuple-element.10), channel_id=1, source_target_pairs={{0,3},{1,0},{2,1},{3,2},{4,7},{5,4},{6,5},{7,6},{8,11},{9,8},{10,9... | collective-permute-start | bytes 393224 | tf_op jit(solution)/shard_map/ppermute | solution.py:375
  6.0 1.9 %collective-permute-start.1 = (f32[4,4,4,16,128]{4,3,2,1,0:T(8,128)S(1)}, f32[4,4,4,16,128]{4,3,2,1,0:T(8,128)S(1)}, u32[]{:S(2)}, u32[]{:S(2)}) collective-permute-start(f32[4,4,4,16,128]{4,3,2,1,0:T(8,128)S(1)} %get-tuple-element.8.block_ref), channel_id=1, source_target_pairs={{4,0},{8,4},{12,8},{16,12},{20,16},{24,20},{28,24},{32,28},{36,32}... | collective-permute-start | bytes 1572872 | tf_op jit(solution)/shard_map/ppermute | solution.py:379
  7.9 2.4 %collective-permute-start = (f32[4,4,4,16,128]{4,3,2,1,0:T(8,128)S(1)}, f32[4,4,4,16,128]{4,3,2,1,0:T(8,128)S(1)}, u32[]{:S(2)}, u32[]{:S(2)}) collective-permute-start(f32[4,4,4,16,128]{4,3,2,1,0:T(8,128)S(1)} %get-tuple-element.8.block_ref), channel_id=1, source_target_pairs={{0,4},{4,8},{8,12},{12,16},{16,20},{20,24},{24,28},{28,32},{32,36}... | collective-permute-start | bytes 1572872 | tf_op jit(solution)/shard_map/ppermute | solution.py:379
  10.5 7.0 %collective-permute-done.2.low_ref = f32[4,4,16,128]{3,2,1,0:T(8,128)S(1)} collective-permute-done((f32[4,4,16,128]{3,2,1,0:T(8,128)S(1)}, f32[4,4,16,128]{3,2,1,0:T(8,128)S(1)}, u32[]{:S(2)}, u32[]{:S(2)}) %collective-permute-start.2) | collective-permute-done | bytes 131104 | tf_op jit(solution)/shard_map/ppermute | solution.py:375
  17.6 2.2 %collective-permute-start.4 = (f32[4,6,16,128]{3,2,1,0:T(8,128)S(1)}, f32[4,6,16,128]{3,2,1,0:T(8,128)S(1)}, u32[]{:S(2)}, u32[]{:S(2)}) collective-permute-start(f32[4,6,16,128]{3,2,1,0:T(8,128)S(1)} %pad_maximum_fusion), channel_id=1, source_target_pairs={{0,4},{4,8},{8,12},{12,16},{16,20},{20,24},{24,28},{28,32},{32,36}... | collective-permute-start | bytes 589832 | tf_op jit(solution)/shard_map/ppermute | solution.py:379
  19.8 3.3 %collective-permute-start.5 = (f32[4,6,16,128]{3,2,1,0:T(8,128)S(1)}, f32[4,6,16,128]{3,2,1,0:T(8,128)S(1)}, u32[]{:S(2)}, u32[]{:S(2)}) collective-permute-start(f32[4,6,16,128]{3,2,1,0:T(8,128)S(1)} %pad_maximum_fusion.1), channel_id=1, source_target_pairs={{4,0},{8,4},{12,8},{16,12},{20,16},{24,20},{28,24},{32,28},{36,32}... | collective-permute-start | bytes 589832 | tf_op jit(solution)/shard_map/ppermute | solution.py:379
  23.8 0.7 collective-permute-done.4.corner_before_ref
  24.6 1.8 %collective-permute-done.5.corner_after_ref = f32[4,6,16,128]{3,2,1,0:T(8,128)S(1)} collective-permute-done((f32[4,6,16,128]{3,2,1,0:T(8,128)S(1)}, f32[4,6,16,128]{3,2,1,0:T(8,128)S(1)}, u32[]{:S(2)}, u32[]{:S(2)}) %collective-permute-start.5) | collective-permute-done | bytes 196640 | tf_op jit(solution)/shard_map/ppermute | solution.py:379
  26.3 6.7 %steps.1 = (f32[3,4,16,512]{3,2,1,0:T(8,128)}, f32[2048,128]{1,0:T(8,128)S(1)}, f32[128,128]{1,0:T(8,128)S(1)}) custom-call(s32[130]{0:T(256)S(1)} %pad_add_fusion.place_ref, f32[4,4,4,16,128]{4,3,2,1,0:T(8,128)S(1)} %get-tuple-element.8.block_ref, f32[4,4,4,16,128]{4,3,2,1,0:T(8,128)S(1)} %collective-permute-done.before_ref, ...), custom_call_target="tpu_custom_call" | custom-call | tf_op jit(solution)/shard_map/steps/pallas_call | solution.py:330
  33.1 4.3 %collective-permute-done.6 = f32[128,128]{1,0:T(8,128)S(1)} collective-permute-done((f32[128,128]{1,0:T(8,128)S(1)}, f32[128,128]{1,0:T(8,128)S(1)}, u32[]{:S(2)}, u32[]{:S(2)}) %collective-permute-start.6) | collective-permute-done | bytes 65568 | tf_op jit(solution)/shard_map/ppermute | solution.py:366
  37.5 6.1 %collective-permute-done.7 = f32[128,128]{1,0:T(8,128)S(1)} collective-permute-done((f32[128,128]{1,0:T(8,128)S(1)}, f32[128,128]{1,0:T(8,128)S(1)}, u32[]{:S(2)}, u32[]{:S(2)}) %collective-permute-start.7) | collective-permute-done | bytes 65568 | tf_op jit(solution)/shard_map/ppermute | solution.py:366
  43.8 1.1 %collective-permute-done.8 = f32[128,128]{1,0:T(8,128)S(1)} collective-permute-done((f32[128,128]{1,0:T(8,128)S(1)}, f32[128,128]{1,0:T(8,128)S(1)}, u32[]{:S(2)}, u32[]{:S(2)}) %collective-permute-start.8) | collective-permute-done | bytes 65568 | tf_op jit(solution)/shard_map/ppermute | solution.py:366
  45.0 4.3 %collective-permute-done.9 = f32[128,128]{1,0:T(8,128)S(1)} collective-permute-done((f32[128,128]{1,0:T(8,128)S(1)}, f32[128,128]{1,0:T(8,128)S(1)}, u32[]{:S(2)}, u32[]{:S(2)}) %collective-permute-start.9) | collective-permute-done | bytes 65568 | tf_op jit(solution)/shard_map/ppermute | solution.py:366
  49.3 3.9 %collective-permute-start.10 = (f32[128,128]{1,0:T(8,128)S(1)}, f32[128,128]{1,0:T(8,128)S(1)}, u32[]{:S(2)}, u32[]{:S(2)}) collective-permute-start(f32[128,128]{1,0:T(8,128)S(1)} %add.27), channel_id=1, source_target_pairs={{0,24},{4,28},{8,16},{12,20},{16,8},{20,12},{24,0},{28,4},{32,56},... | collective-permute-start | bytes 196616 | tf_op jit(solution)/shard_map/ppermute | solution.py:366
  53.2 3.6 %collective-permute-done.10 = f32[128,128]{1,0:T(8,128)S(1)} collective-permute-done((f32[128,128]{1,0:T(8,128)S(1)}, f32[128,128]{1,0:T(8,128)S(1)}, u32[]{:S(2)}, u32[]{:S(2)}) %collective-permute-start.10) | collective-permute-done | bytes 65568 | tf_op jit(solution)/shard_map/ppermute | solution.py:366
  56.8 3.1 %collective-permute-start.11 = (f32[128,128]{1,0:T(8,128)S(1)}, f32[128,128]{1,0:T(8,128)S(1)}, u32[]{:S(2)}, u32[]{:S(2)}) collective-permute-start(f32[128,128]{1,0:T(8,128)S(1)} %add.28), channel_id=1, source_target_pairs={{0,56},{4,60},{8,48},{12,52},{16,40},{20,44},{24,32},{28,36},{32,2... | collective-permute-start | bytes 196616 | tf_op jit(solution)/shard_map/ppermute | solution.py:366
  59.9 4.3 %collective-permute-done.11 = f32[128,128]{1,0:T(8,128)S(1)} collective-permute-done((f32[128,128]{1,0:T(8,128)S(1)}, f32[128,128]{1,0:T(8,128)S(1)}, u32[]{:S(2)}, u32[]{:S(2)}) %collective-permute-start.11) | collective-permute-done | bytes 65568 | tf_op jit(solution)/shard_map/ppermute | solution.py:366
  64.3 2.3 %collective-permute-start.12 = (f32[128,128]{1,0:T(8,128)S(1)}, f32[128,128]{1,0:T(8,128)S(1)}, u32[]{:S(2)}, u32[]{:S(2)}) collective-permute-start(f32[128,128]{1,0:T(8,128)S(1)} %add.29), channel_id=1, source_target_pairs={{0,64},{4,68},{8,72},{12,76},{16,80},{20,84},{24,88},{28,92},{32,9... | collective-permute-start | bytes 196616 | tf_op jit(solution)/shard_map/ppermute | solution.py:366
  66.6 2.2 %collective-permute-done.12 = f32[128,128]{1,0:T(8,128)S(1)} collective-permute-done((f32[128,128]{1,0:T(8,128)S(1)}, f32[128,128]{1,0:T(8,128)S(1)}, u32[]{:S(2)}, u32[]{:S(2)}) %collective-permute-start.12) | collective-permute-done | bytes 65568 | tf_op jit(solution)/shard_map/ppermute | solution.py:366
  68.9 4.0 %collective-permute-start.13 = (f32[128,128]{1,0:T(8,128)S(1)}, f32[128,128]{1,0:T(8,128)S(1)}, u32[]{:S(2)}, u32[]{:S(2)}) collective-permute-start(f32[128,128]{1,0:T(8,128)S(1)} %add.30), channel_id=1, source_target_pairs={{0,192},{4,196},{8,200},{12,204},{16,208},{20,212},{24,216},{28,22... | collective-permute-start | bytes 196616 | tf_op jit(solution)/shard_map/ppermute | solution.py:366
  72.9 2.2 %collective-permute-done.13 = f32[128,128]{1,0:T(8,128)S(1)} collective-permute-done((f32[128,128]{1,0:T(8,128)S(1)}, f32[128,128]{1,0:T(8,128)S(1)}, u32[]{:S(2)}, u32[]{:S(2)}) %collective-permute-start.13) | collective-permute-done | bytes 65568 | tf_op jit(solution)/shard_map/ppermute | solution.py:366
  75.2 16.1 %basis.1 = f32[1344,128]{1,0:T(8,128)} custom-call(f32[128,128]{1,0:T(8,128)S(1)} %add.31.total_ref, f32[2048,128]{1,0:T(8,128)S(1)} %get-tuple-element.13.snap_ref), custom_call_target="tpu_custom_call" | custom-call | tf_op jit(solution)/shard_map/basis/pallas_call | solution.py:126
  (27 shorter events, 1.9 us)
Async XLA Ops:
  0.6 1.0 %copy-start = (f32[3,4,16,512]{3,2,1,0:T(8,128)S(1)}, f32[3,4,16,512]{3,2,1,0:T(8,128)}, u32[]{:S(2)}) copy-start(f32[3,4,16,512]{3,2,1,0:T(8,128)} %velocity_ref.1) | copy-start | bytes 1179652
  1.6 0.9 copy-start.1
  3.2 7.3 %collective-permute-start.3 = (f32[4,4,16,128]{3,2,1,0:T(8,128)S(1)}, f32[4,4,16,128]{3,2,1,0:T(8,128)S(1)}, u32[]{:S(2)}, u32[]{:S(2)}) collective-permute-start(f32[4,4,16,128]{3,2,1,0:T(8,128)S(1)} %get-tuple-element.10), channel_id=1, source_target_pairs={{0,3},{1,0},{2,1},{3,2},{4,7},{5,4},{6,5},{7,6},{8,11},{9,8},{10,9... | collective-permute-start | bytes 393224 | tf_op jit(solution)/shard_map/ppermute | solution.py:375
  6.0 20.3 %collective-permute-start.1 = (f32[4,4,4,16,128]{4,3,2,1,0:T(8,128)S(1)}, f32[4,4,4,16,128]{4,3,2,1,0:T(8,128)S(1)}, u32[]{:S(2)}, u32[]{:S(2)}) collective-permute-start(f32[4,4,4,16,128]{4,3,2,1,0:T(8,128)S(1)} %get-tuple-element.8.block_ref), channel_id=1, source_target_pairs={{4,0},{8,4},{12,8},{16,12},{20,16},{24,20},{28,24},{32,28},{36,32}... | collective-permute-start | bytes 1572872 | tf_op jit(solution)/shard_map/ppermute | solution.py:379
  7.9 18.4 %collective-permute-start = (f32[4,4,4,16,128]{4,3,2,1,0:T(8,128)S(1)}, f32[4,4,4,16,128]{4,3,2,1,0:T(8,128)S(1)}, u32[]{:S(2)}, u32[]{:S(2)}) collective-permute-start(f32[4,4,4,16,128]{4,3,2,1,0:T(8,128)S(1)} %get-tuple-element.8.block_ref), channel_id=1, source_target_pairs={{0,4},{4,8},{8,12},{12,16},{16,20},{20,24},{24,28},{28,32},{32,36}... | collective-permute-start | bytes 1572872 | tf_op jit(solution)/shard_map/ppermute | solution.py:379
  10.4 7.2 %collective-permute-start.2 = (f32[4,4,16,128]{3,2,1,0:T(8,128)S(1)}, f32[4,4,16,128]{3,2,1,0:T(8,128)S(1)}, u32[]{:S(2)}, u32[]{:S(2)}) collective-permute-start(f32[4,4,16,128]{3,2,1,0:T(8,128)S(1)} %get-tuple-element.9), channel_id=1, source_target_pairs={{0,1},{1,2},{2,3},{3,0},{4,5},{5,6},{6,7},{7,4},{8,9},{9,10},{10,1... | collective-permute-start | bytes 393224 | tf_op jit(solution)/shard_map/ppermute | solution.py:375
  17.6 7.0 %collective-permute-start.4 = (f32[4,6,16,128]{3,2,1,0:T(8,128)S(1)}, f32[4,6,16,128]{3,2,1,0:T(8,128)S(1)}, u32[]{:S(2)}, u32[]{:S(2)}) collective-permute-start(f32[4,6,16,128]{3,2,1,0:T(8,128)S(1)} %pad_maximum_fusion), channel_id=1, source_target_pairs={{0,4},{4,8},{8,12},{12,16},{16,20},{20,24},{24,28},{28,32},{32,36}... | collective-permute-start | bytes 589832 | tf_op jit(solution)/shard_map/ppermute | solution.py:379
  19.8 6.5 %collective-permute-start.5 = (f32[4,6,16,128]{3,2,1,0:T(8,128)S(1)}, f32[4,6,16,128]{3,2,1,0:T(8,128)S(1)}, u32[]{:S(2)}, u32[]{:S(2)}) collective-permute-start(f32[4,6,16,128]{3,2,1,0:T(8,128)S(1)} %pad_maximum_fusion.1), channel_id=1, source_target_pairs={{4,0},{8,4},{12,8},{16,12},{20,16},{24,20},{28,24},{32,28},{36,32}... | collective-permute-start | bytes 589832 | tf_op jit(solution)/shard_map/ppermute | solution.py:379
  23.2 0.7 copy-start.2
  33.1 4.3 %collective-permute-start.6 = (f32[128,128]{1,0:T(8,128)S(1)}, f32[128,128]{1,0:T(8,128)S(1)}, u32[]{:S(2)}, u32[]{:S(2)}) collective-permute-start(f32[128,128]{1,0:T(8,128)S(1)} %get-tuple-element.12), channel_id=1, source_target_pairs={{0,1},{1,0},{2,3},{3,2},{4,5},{5,4},{6,7},{7,6},{8,9},{9,8},{10,11... | collective-permute-start | bytes 196616 | tf_op jit(solution)/shard_map/ppermute | solution.py:366
  37.4 6.2 %collective-permute-start.7 = (f32[128,128]{1,0:T(8,128)S(1)}, f32[128,128]{1,0:T(8,128)S(1)}, u32[]{:S(2)}, u32[]{:S(2)}) collective-permute-start(f32[128,128]{1,0:T(8,128)S(1)} %add.24), channel_id=1, source_target_pairs={{0,3},{1,2},{2,1},{3,0},{4,7},{5,6},{6,5},{7,4},{8,11},{9,10},{10,... | collective-permute-start | bytes 196616 | tf_op jit(solution)/shard_map/ppermute | solution.py:366
  43.6 1.3 %collective-permute-start.8 = (f32[128,128]{1,0:T(8,128)S(1)}, f32[128,128]{1,0:T(8,128)S(1)}, u32[]{:S(2)}, u32[]{:S(2)}) collective-permute-start(f32[128,128]{1,0:T(8,128)S(1)} %add.25), channel_id=1, source_target_pairs={{0,4},{4,0},{8,12},{12,8},{16,20},{20,16},{24,28},{28,24},{32,36},... | collective-permute-start | bytes 196616 | tf_op jit(solution)/shard_map/ppermute | solution.py:366
  44.9 4.4 %collective-permute-start.9 = (f32[128,128]{1,0:T(8,128)S(1)}, f32[128,128]{1,0:T(8,128)S(1)}, u32[]{:S(2)}, u32[]{:S(2)}) collective-permute-start(f32[128,128]{1,0:T(8,128)S(1)} %add.26), channel_id=1, source_target_pairs={{0,8},{4,12},{8,0},{12,4},{16,24},{20,28},{24,16},{28,20},{32,40},... | collective-permute-start | bytes 196616 | tf_op jit(solution)/shard_map/ppermute | solution.py:366
  49.3 7.6 %collective-permute-start.10 = (f32[128,128]{1,0:T(8,128)S(1)}, f32[128,128]{1,0:T(8,128)S(1)}, u32[]{:S(2)}, u32[]{:S(2)}) collective-permute-start(f32[128,128]{1,0:T(8,128)S(1)} %add.27), channel_id=1, source_target_pairs={{0,24},{4,28},{8,16},{12,20},{16,8},{20,12},{24,0},{28,4},{32,56},... | collective-permute-start | bytes 196616 | tf_op jit(solution)/shard_map/ppermute | solution.py:366
  56.8 7.4 %collective-permute-start.11 = (f32[128,128]{1,0:T(8,128)S(1)}, f32[128,128]{1,0:T(8,128)S(1)}, u32[]{:S(2)}, u32[]{:S(2)}) collective-permute-start(f32[128,128]{1,0:T(8,128)S(1)} %add.28), channel_id=1, source_target_pairs={{0,56},{4,60},{8,48},{12,52},{16,40},{20,44},{24,32},{28,36},{32,2... | collective-permute-start | bytes 196616 | tf_op jit(solution)/shard_map/ppermute | solution.py:366
  64.3 4.6 %collective-permute-start.12 = (f32[128,128]{1,0:T(8,128)S(1)}, f32[128,128]{1,0:T(8,128)S(1)}, u32[]{:S(2)}, u32[]{:S(2)}) collective-permute-start(f32[128,128]{1,0:T(8,128)S(1)} %add.29), channel_id=1, source_target_pairs={{0,64},{4,68},{8,72},{12,76},{16,80},{20,84},{24,88},{28,92},{32,9... | collective-permute-start | bytes 196616 | tf_op jit(solution)/shard_map/ppermute | solution.py:366
  68.9 6.3 %collective-permute-start.13 = (f32[128,128]{1,0:T(8,128)S(1)}, f32[128,128]{1,0:T(8,128)S(1)}, u32[]{:S(2)}, u32[]{:S(2)}) collective-permute-start(f32[128,128]{1,0:T(8,128)S(1)} %add.30), channel_id=1, source_target_pairs={{0,192},{4,196},{8,200},{12,204},{16,208},{20,212},{24,216},{28,22... | collective-permute-start | bytes 196616 | tf_op jit(solution)/shard_map/ppermute | solution.py:366

commit v2 on v1

--- a/solution.py
+++ b/solution.py
@@ -85,10 +85,10 @@
 
 
 def basis_kernel(total_ref, snap_ref, out_ref, basis_ref, *, rows_all):
-    cols = total_ref.shape[0]
-    row_id = lax.broadcasted_iota(jnp.int32, (cols, cols), 0)
-    col_id = lax.broadcasted_iota(jnp.int32, (cols, cols), 1)
-    gram_matrix = total_ref[...] / rows_all + jnp.where(row_id == col_id, jnp.float32(ridge), 0.0)
+    cols = total_ref.shape[1]
+    row_id, col_id = ids((cols, cols))
+    identity = jnp.where(row_id == col_id, jnp.float32(ridge), 0.0)
+    gram_matrix = unfolded(total_ref[...]) / rows_all + identity
 
     def sweep(step, carry):
         @pl.when(step == 0)
@@ -122,7 +122,7 @@
 
 
 def project(gram_total, snapshots, rows_all):
-    cols = gram_total.shape[0]
+    cols = gram_total.shape[1]
     return pl.pallas_call(
         functools.partial(basis_kernel, rows_all=rows_all),
         out_shape=jax.ShapeDtypeStruct((RANK * 12, LANES), jnp.float32),
@@ -225,13 +225,40 @@
     return result
 
 
+def ids(shape):
+    return lax.broadcasted_iota(jnp.int32, shape, 0), lax.broadcasted_iota(jnp.int32, shape, 1)
+
+
+def folded(gram):
+    half = gram.shape[0] // 2
+    row, lane = ids((half, 2 * half))
+    corner = pltpu.roll(gram[half:], half, 1)
+    square = jnp.where(lane < row, corner, gram[:half])
+    diagonal = jnp.sum(jnp.where(lane == row, corner, 0.0), axis=0, keepdims=True)
+    return jnp.concatenate([square, jnp.broadcast_to(diagonal, (8, 2 * half))], axis=0)
+
+
+def unfolded(parts):
+    half = parts.shape[1] // 2
+    row, lane = ids((half, 2 * half))
+    square = parts[:half]
+    upper = jnp.where(lane > row, square, 0.0)
+    lower = pltpu.roll(jnp.where(lane < row, square, 0.0), half, 1)
+    one_side = jnp.concatenate([upper, lower], axis=0)
+    below = pltpu.roll(jnp.broadcast_to(parts[half : half + 1], square.shape), half, 1)
+    diagonal = jnp.concatenate(
+        [jnp.where(lane == row, square, 0.0), jnp.where(lane == row + half, below, 0.0)], axis=0
+    )
+    return one_side + one_side.T + diagonal
+
+
 def steps_kernel(
     place_ref, block_ref, before_ref, after_ref, low_ref, high_ref, corner_before_ref, corner_after_ref,
     final_ref, snap_ref, gram_ref,
     cells_ref, visc_ref, one_ref, two_ref, wide_ref, all_ref,
 ):
     rows_y, rows_z = block_ref.shape[1], block_ref.shape[3]
-    cols = gram_ref.shape[0]
+    cols = gram_ref.shape[1]
     first, last = place_ref[cols] == 1, place_ref[cols + 1] == 1
     over, under = slice(rows_z, rows_z + 4), slice(rows_z + 4, rows_z + 8)
     for c in range(4):
@@ -242,14 +269,18 @@
                 cells_ref[c, own, o, :rows_z] = block_ref[c, y, o]
                 cells_ref[c, own, o, over] = high_ref[c, y, rows]
                 cells_ref[c, own, o, under] = low_ref[c, y, rows]
-                cells_ref[c, below, o, :rows_z] = before_ref[c, y, o]
-                cells_ref[c, above, o, :rows_z] = after_ref[c, y, o]
+                cells_ref[c, below, o, :rows_z] = jnp.where(first, 0.0, before_ref[c, y, o])
+                cells_ref[c, above, o, :rows_z] = jnp.where(last, 0.0, after_ref[c, y, o])
                 if y > 0:
-                    cells_ref[c, below, o, over] = corner_before_ref[c, 3 + y - 1, rows]
-                    cells_ref[c, below, o, under] = corner_before_ref[c, y - 1, rows]
+                    halo = jnp.where(first, 0.0, corner_before_ref[c, 3 + y - 1, rows])
+                    cells_ref[c, below, o, over] = halo
+                    halo = jnp.where(first, 0.0, corner_before_ref[c, y - 1, rows])
+                    cells_ref[c, below, o, under] = halo
                 if y < rows_y - 1:
-                    cells_ref[c, above, o, over] = corner_after_ref[c, 3 + y, rows]
-                    cells_ref[c, above, o, under] = corner_after_ref[c, y, rows]
+                    halo = jnp.where(last, 0.0, corner_after_ref[c, 3 + y, rows])
+                    cells_ref[c, above, o, over] = halo
+                    halo = jnp.where(last, 0.0, corner_after_ref[c, y, rows])
+                    cells_ref[c, above, o, under] = halo
 
     @pl.when(first)
     def _():
@@ -318,7 +349,7 @@
         gram = gram + lax.dot_general(
             part, part, (((1,), (1,)), ((), ())), precision=highest, preferred_element_type=jnp.float32
         )
-    gram_ref[...] = gram
+    gram_ref[...] = folded(gram)
 
 
 def both_steps(place, block, *halo):
@@ -332,7 +363,7 @@
         out_shape=(
             f32(3, rows_y, rows_z, 4 * LANES),
             f32(SLOT * cols, LANES),
-            f32(cols, cols),
+            f32(cols // 2 + 8, cols),
         ),
         in_specs=[pl.BlockSpec(memory_space=pltpu.SMEM)]
         + [pl.BlockSpec(memory_space=pltpu.VMEM)] * (1 + len(halo)),
@@ -351,19 +382,10 @@
 
 
 def device_sum(part):
-    steps = [
-        ("gz", lambda i: i ^ 1),
-        ("gz", lambda i: 3 - i),
-        ("gy", lambda i: i ^ 1),
-        ("gy", lambda i: i ^ 2),
-        ("gy", lambda i: i ^ 6),
-        ("gy", lambda i: i ^ 14),
-        ("gy", lambda i: i ^ 16),
-        ("gy", lambda i: i ^ 48),
-    ]
-    for axis, partner in steps:
+    steps = [("gy", 1), ("gz", 1), ("gy", 16), ("gy", 2), ("gz", 3), ("gy", 48), ("gy", 6), ("gy", 14)]
+    for axis, flip in steps:
         count = lax.axis_size(axis)
-        part = part + lax.ppermute(part, axis, [(i, partner(i)) for i in range(count)])
+        part = part + lax.ppermute(part, axis, [(i, i ^ flip) for i in range(count)])
     return part
 
 
@@ -375,8 +397,7 @@
         return lax.ppermute(part, "gz", [(i, (i + step) % count_z) for i in range(count_z)])
 
     def along_y(part, step):
-        pairs = [(i, i + step) for i in range(count_y) if 0 <= i + step < count_y]
-        return lax.ppermute(part, "gy", pairs)
+        return lax.ppermute(part, "gy", [(i, (i + step) % count_y) for i in range(count_y)])
 
     from_low, from_high = along_z(high, 1), along_z(low, -1)
     before, after = along_y(block, 1), along_y(block, -1)

time: 92.9 us -> 85 us (0.915)
  starting transfers between devices: 26.5 us -> 20.3 us
  waiting for transfers between devices: 37.7 us -> 36.5 us
    ppermute x12, starting transfers between devices: 23.6 us -> 17.5 us  [the longest x8 15.1 us: device_sum(): lax.ppermute(part, axis, [(i, i ^ flip) for i in range(count)])]
    ppermute x12, waiting for transfers between devices: 30.7 us -> 29.4 us  [the longest x8 26.8 us: device_sum(): lax.ppermute(part, axis, [(i, i ^ flip) for i in range(count)])]
where the time goes in v2:
time: 85 us; the launch traced here: 83.4 us
  waiting for transfers between devices  36.5 us (43%)
  Pallas kernels  23.3 us (27%)
  starting transfers between devices  20.3 us (24%)
  local copies, waits for them, and re-layouts  2.5 us (3%)
    ppermute x8, waiting for transfers between devices, device_sum(): lax.ppermute(part, axis, [(i, i ^ flip) for i in range(count)])  26.8 us
    pallas_call x1, Pallas kernels, project(): pl.pallas_call(functools.partial(basis_kernel, rows_all=rows_all), out_sh...  16.2 us
    ppermute x8, starting transfers between devices, device_sum(): lax.ppermute(part, axis, [(i, i ^ flip) for i in range(count)])  15.1 us
    ppermute x2, waiting for transfers between devices, along_z(): lax.ppermute(part, 'gz', [(i, (i + step) % count_z) for i in range(count_...  7.07 us
    pallas_call x1, Pallas kernels, both_steps(): pl.pallas_call(steps_kernel, out_shape=(f32(3, rows_y, rows_z, 4 * LANES)...  6.4 us
    ppermute x2, starting transfers between devices, along_z(): lax.ppermute(part, 'gz', [(i, (i + step) % count_z) for i in range(count_...  2.84 us
    ppermute x4, waiting for transfers between devices, along_y(): lax.ppermute(part, 'gy', [(i, (i + step) % count_y) for i in range(count_...  2.6 us
    unnamed x6, local copies, waits for them, and re-layouts  2.47 us
  transfers between devices with their start and end apart: 14, of which 11 were waited for; matrix products, arithmetic and copies ran while one was open for 0% of the time, Pallas kernels for 0%

profile of v2, /device:TPU:32, one launch (start us, length us, event | category | flops | bytes accessed | tf_op | source)
XLA Modules:
  0.0 83.4 jit_solution(5593496803284881326)
XLA Ops:
  0.6 1.0 %copy-done = f32[3,4,16,512]{3,2,1,0:T(8,128)S(1)} copy-done((f32[3,4,16,512]{3,2,1,0:T(8,128)S(1)}, f32[3,4,16,512]{3,2,1,0:T(8,128)}, u32[]{:S(2)}) %copy-start) | copy-done | bytes 393240
  1.6 0.9 %copy-done.1 = f32[4,16,512]{2,1,0:T(8,128)S(1)} copy-done((f32[4,16,512]{2,1,0:T(8,128)S(1)}, f32[4,16,512]{2,1,0:T(8,128)}, u32[]{:S(2)}) %copy-start.1) | copy-done | bytes 131096
  2.5 0.7 pack.1
  3.2 2.8 %collective-permute-start.3 = (f32[4,4,16,128]{3,2,1,0:T(8,128)S(1)}, f32[4,4,16,128]{3,2,1,0:T(8,128)S(1)}, u32[]{:S(2)}, u32[]{:S(2)}) collective-permute-start(f32[4,4,16,128]{3,2,1,0:T(8,128)S(1)} %get-tuple-element.10), channel_id=1, source_target_pairs={{0,3},{1,0},{2,1},{3,2},{4,7},{5,4},{6,5},{7,6},{8,11},{9,8},{10,9... | collective-permute-start | bytes 393224 | tf_op jit(solution)/shard_map/ppermute | solution.py:397
  6.0 0.5 collective-permute-start
  6.5 2.2 %collective-permute-done.3.high_ref = f32[4,4,16,128]{3,2,1,0:T(8,128)S(1)} collective-permute-done((f32[4,4,16,128]{3,2,1,0:T(8,128)S(1)}, f32[4,4,16,128]{3,2,1,0:T(8,128)S(1)}, u32[]{:S(2)}, u32[]{:S(2)}) %collective-permute-start.3) | collective-permute-done | bytes 131104 | tf_op jit(solution)/shard_map/ppermute | solution.py:397
  8.8 4.9 %collective-permute-done.2.low_ref = f32[4,4,16,128]{3,2,1,0:T(8,128)S(1)} collective-permute-done((f32[4,4,16,128]{3,2,1,0:T(8,128)S(1)}, f32[4,4,16,128]{3,2,1,0:T(8,128)S(1)}, u32[]{:S(2)}, u32[]{:S(2)}) %collective-permute-start.2) | collective-permute-done | bytes 131104 | tf_op jit(solution)/shard_map/ppermute | solution.py:397
  14.1 1.5 %collective-permute-start.5 = (f32[4,6,16,128]{3,2,1,0:T(8,128)S(1)}, f32[4,6,16,128]{3,2,1,0:T(8,128)S(1)}, u32[]{:S(2)}, u32[]{:S(2)}) collective-permute-start(f32[4,6,16,128]{3,2,1,0:T(8,128)S(1)} %pad_maximum_fusion.1), channel_id=1, source_target_pairs={{0,252},{4,0},{8,4},{12,8},{16,12},{20,16},{24,20},{28,24},{32,28}... | collective-permute-start | bytes 589832 | tf_op jit(solution)/shard_map/ppermute | solution.py:400
  15.7 0.6 copy-done.2
  16.3 2.6 %collective-permute-done.4.corner_before_ref = f32[4,6,16,128]{3,2,1,0:T(8,128)S(1)} collective-permute-done((f32[4,6,16,128]{3,2,1,0:T(8,128)S(1)}, f32[4,6,16,128]{3,2,1,0:T(8,128)S(1)}, u32[]{:S(2)}, u32[]{:S(2)}) %collective-permute-start.4) | collective-permute-done | bytes 196640 | tf_op jit(solution)/shard_map/ppermute | solution.py:400
  18.9 6.4 %steps.1 = (f32[3,4,16,512]{3,2,1,0:T(8,128)}, f32[2048,128]{1,0:T(8,128)S(1)}, f32[72,128]{1,0:T(8,128)S(1)}) custom-call(s32[130]{0:T(256)S(1)} %pad_add_fusion.place_ref, f32[4,4,4,16,128]{4,3,2,1,0:T(8,128)S(1)} %get-tuple-element.8.block_ref, f32[4,4,4,16,128]{4,3,2,1,0:T(8,128)S(1)} %collective-permute-done.before_ref, ...), custom_call_target="tpu_custom_call" | custom-call | tf_op jit(solution)/shard_map/steps/pallas_call | solution.py:361
  25.3 2.2 %collective-permute-start.6 = (f32[72,128]{1,0:T(8,128)S(1)}, f32[72,128]{1,0:T(8,128)S(1)}, u32[]{:S(2)}, u32[]{:S(2)}) collective-permute-start(f32[72,128]{1,0:T(8,128)S(1)} %get-tuple-element.12), channel_id=1, source_target_pairs={{0,4},{4,0},{8,12},{12,8},{16,20},{20,16},{24,28},{28,24},{32,36},... | collective-permute-start | bytes 110600 | tf_op jit(solution)/shard_map/ppermute | solution.py:388
  27.5 0.9 %collective-permute-done.6 = f32[72,128]{1,0:T(8,128)S(1)} collective-permute-done((f32[72,128]{1,0:T(8,128)S(1)}, f32[72,128]{1,0:T(8,128)S(1)}, u32[]{:S(2)}, u32[]{:S(2)}) %collective-permute-start.6) | collective-permute-done | bytes 36896 | tf_op jit(solution)/shard_map/ppermute | solution.py:388
  28.4 4.0 %collective-permute-done.7 = f32[72,128]{1,0:T(8,128)S(1)} collective-permute-done((f32[72,128]{1,0:T(8,128)S(1)}, f32[72,128]{1,0:T(8,128)S(1)}, u32[]{:S(2)}, u32[]{:S(2)}) %collective-permute-start.7) | collective-permute-done | bytes 36896 | tf_op jit(solution)/shard_map/ppermute | solution.py:388
  32.3 1.6 %collective-permute-start.8 = (f32[72,128]{1,0:T(8,128)S(1)}, f32[72,128]{1,0:T(8,128)S(1)}, u32[]{:S(2)}, u32[]{:S(2)}) collective-permute-start(f32[72,128]{1,0:T(8,128)S(1)} %add.25), channel_id=1, source_target_pairs={{0,64},{4,68},{8,72},{12,76},{16,80},{20,84},{24,88},{28,92},{32,9... | collective-permute-start | bytes 110600 | tf_op jit(solution)/shard_map/ppermute | solution.py:388
  33.9 2.4 %collective-permute-done.8 = f32[72,128]{1,0:T(8,128)S(1)} collective-permute-done((f32[72,128]{1,0:T(8,128)S(1)}, f32[72,128]{1,0:T(8,128)S(1)}, u32[]{:S(2)}, u32[]{:S(2)}) %collective-permute-start.8) | collective-permute-done | bytes 36896 | tf_op jit(solution)/shard_map/ppermute | solution.py:388
  36.3 7.7 %collective-permute-start.9 = (f32[72,128]{1,0:T(8,128)S(1)}, f32[72,128]{1,0:T(8,128)S(1)}, u32[]{:S(2)}, u32[]{:S(2)}) collective-permute-start(f32[72,128]{1,0:T(8,128)S(1)} %add.26), channel_id=1, source_target_pairs={{0,8},{4,12},{8,0},{12,4},{16,24},{20,28},{24,16},{28,20},{32,40},... | collective-permute-start | bytes 110600 | tf_op jit(solution)/shard_map/ppermute | solution.py:388
  44.0 1.9 %collective-permute-done.9 = f32[72,128]{1,0:T(8,128)S(1)} collective-permute-done((f32[72,128]{1,0:T(8,128)S(1)}, f32[72,128]{1,0:T(8,128)S(1)}, u32[]{:S(2)}, u32[]{:S(2)}) %collective-permute-start.9) | collective-permute-done | bytes 36896 | tf_op jit(solution)/shard_map/ppermute | solution.py:388
  46.1 5.0 %collective-permute-done.10 = f32[72,128]{1,0:T(8,128)S(1)} collective-permute-done((f32[72,128]{1,0:T(8,128)S(1)}, f32[72,128]{1,0:T(8,128)S(1)}, u32[]{:S(2)}, u32[]{:S(2)}) %collective-permute-start.10) | collective-permute-done | bytes 36896 | tf_op jit(solution)/shard_map/ppermute | solution.py:388
  51.1 5.2 %collective-permute-done.11 = f32[72,128]{1,0:T(8,128)S(1)} collective-permute-done((f32[72,128]{1,0:T(8,128)S(1)}, f32[72,128]{1,0:T(8,128)S(1)}, u32[]{:S(2)}, u32[]{:S(2)}) %collective-permute-start.11) | collective-permute-done | bytes 36896 | tf_op jit(solution)/shard_map/ppermute | solution.py:388
  56.3 3.9 %collective-permute-done.12 = f32[72,128]{1,0:T(8,128)S(1)} collective-permute-done((f32[72,128]{1,0:T(8,128)S(1)}, f32[72,128]{1,0:T(8,128)S(1)}, u32[]{:S(2)}, u32[]{:S(2)}) %collective-permute-start.12) | collective-permute-done | bytes 36896 | tf_op jit(solution)/shard_map/ppermute | solution.py:388
  60.2 3.4 %collective-permute-start.13 = (f32[72,128]{1,0:T(8,128)S(1)}, f32[72,128]{1,0:T(8,128)S(1)}, u32[]{:S(2)}, u32[]{:S(2)}) collective-permute-start(f32[72,128]{1,0:T(8,128)S(1)} %add.30), channel_id=1, source_target_pairs={{0,56},{4,60},{8,48},{12,52},{16,40},{20,44},{24,32},{28,36},{32,2... | collective-permute-start | bytes 110600 | tf_op jit(solution)/shard_map/ppermute | solution.py:388
  63.7 3.5 %collective-permute-done.13 = f32[72,128]{1,0:T(8,128)S(1)} collective-permute-done((f32[72,128]{1,0:T(8,128)S(1)}, f32[72,128]{1,0:T(8,128)S(1)}, u32[]{:S(2)}, u32[]{:S(2)}) %collective-permute-start.13) | collective-permute-done | bytes 36896 | tf_op jit(solution)/shard_map/ppermute | solution.py:388
  67.2 16.2 %basis.1 = f32[1344,128]{1,0:T(8,128)} custom-call(f32[72,128]{1,0:T(8,128)S(1)} %add.31.total_ref, f32[2048,128]{1,0:T(8,128)S(1)} %get-tuple-element.13.snap_ref), custom_call_target="tpu_custom_call" | custom-call | tf_op jit(solution)/shard_map/basis/pallas_call | solution.py:126
  (27 shorter events, 0.7 us)
Async XLA Ops:
  0.6 1.0 %copy-start = (f32[3,4,16,512]{3,2,1,0:T(8,128)S(1)}, f32[3,4,16,512]{3,2,1,0:T(8,128)}, u32[]{:S(2)}) copy-start(f32[3,4,16,512]{3,2,1,0:T(8,128)} %velocity_ref.1) | copy-start | bytes 1179652
  1.6 0.9 %copy-start.1 = (f32[4,16,512]{2,1,0:T(8,128)S(1)}, f32[4,16,512]{2,1,0:T(8,128)}, u32[]{:S(2)}) copy-start(f32[4,16,512]{2,1,0:T(8,128)} %coef_ref.1) | copy-start | bytes 393220
  3.2 5.6 %collective-permute-start.3 = (f32[4,4,16,128]{3,2,1,0:T(8,128)S(1)}, f32[4,4,16,128]{3,2,1,0:T(8,128)S(1)}, u32[]{:S(2)}, u32[]{:S(2)}) collective-permute-start(f32[4,4,16,128]{3,2,1,0:T(8,128)S(1)} %get-tuple-element.10), channel_id=1, source_target_pairs={{0,3},{1,0},{2,1},{3,2},{4,7},{5,4},{6,5},{7,6},{8,11},{9,8},{10,9... | collective-permute-start | bytes 393224 | tf_op jit(solution)/shard_map/ppermute | solution.py:397
  6.0 12.8 %collective-permute-start.1 = (f32[4,4,4,16,128]{4,3,2,1,0:T(8,128)S(1)}, f32[4,4,4,16,128]{4,3,2,1,0:T(8,128)S(1)}, u32[]{:S(2)}, u32[]{:S(2)}) collective-permute-start(f32[4,4,4,16,128]{4,3,2,1,0:T(8,128)S(1)} %get-tuple-element.8.block_ref), channel_id=1, source_target_pairs={{0,252},{4,0},{8,4},{12,8},{16,12},{20,16},{24,20},{28,24},{32,28}... | collective-permute-start | bytes 1572872 | tf_op jit(solution)/shard_map/ppermute | solution.py:400
  6.0 12.8 %collective-permute-start = (f32[4,4,4,16,128]{4,3,2,1,0:T(8,128)S(1)}, f32[4,4,4,16,128]{4,3,2,1,0:T(8,128)S(1)}, u32[]{:S(2)}, u32[]{:S(2)}) collective-permute-start(f32[4,4,4,16,128]{4,3,2,1,0:T(8,128)S(1)} %get-tuple-element.8.block_ref), channel_id=1, source_target_pairs={{0,4},{4,8},{8,12},{12,16},{16,20},{20,24},{24,28},{28,32},{32,36}... | collective-permute-start | bytes 1572872 | tf_op jit(solution)/shard_map/ppermute | solution.py:400
  6.5 7.1 %collective-permute-start.2 = (f32[4,4,16,128]{3,2,1,0:T(8,128)S(1)}, f32[4,4,16,128]{3,2,1,0:T(8,128)S(1)}, u32[]{:S(2)}, u32[]{:S(2)}) collective-permute-start(f32[4,4,16,128]{3,2,1,0:T(8,128)S(1)} %get-tuple-element.9), channel_id=1, source_target_pairs={{0,1},{1,2},{2,3},{3,0},{4,5},{5,6},{6,7},{7,4},{8,9},{9,10},{10,1... | collective-permute-start | bytes 393224 | tf_op jit(solution)/shard_map/ppermute | solution.py:397
  13.7 5.2 %collective-permute-start.4 = (f32[4,6,16,128]{3,2,1,0:T(8,128)S(1)}, f32[4,6,16,128]{3,2,1,0:T(8,128)S(1)}, u32[]{:S(2)}, u32[]{:S(2)}) collective-permute-start(f32[4,6,16,128]{3,2,1,0:T(8,128)S(1)} %pad_maximum_fusion), channel_id=1, source_target_pairs={{0,4},{4,8},{8,12},{12,16},{16,20},{20,24},{24,28},{28,32},{32,36}... | collective-permute-start | bytes 589832 | tf_op jit(solution)/shard_map/ppermute | solution.py:400
  14.1 4.8 %collective-permute-start.5 = (f32[4,6,16,128]{3,2,1,0:T(8,128)S(1)}, f32[4,6,16,128]{3,2,1,0:T(8,128)S(1)}, u32[]{:S(2)}, u32[]{:S(2)}) collective-permute-start(f32[4,6,16,128]{3,2,1,0:T(8,128)S(1)} %pad_maximum_fusion.1), channel_id=1, source_target_pairs={{0,252},{4,0},{8,4},{12,8},{16,12},{20,16},{24,20},{28,24},{32,28}... | collective-permute-start | bytes 589832 | tf_op jit(solution)/shard_map/ppermute | solution.py:400
  15.6 0.7 copy-start.2
  25.3 3.1 %collective-permute-start.6 = (f32[72,128]{1,0:T(8,128)S(1)}, f32[72,128]{1,0:T(8,128)S(1)}, u32[]{:S(2)}, u32[]{:S(2)}) collective-permute-start(f32[72,128]{1,0:T(8,128)S(1)} %get-tuple-element.12), channel_id=1, source_target_pairs={{0,4},{4,0},{8,12},{12,8},{16,20},{20,16},{24,28},{28,24},{32,36},... | collective-permute-start | bytes 110600 | tf_op jit(solution)/shard_map/ppermute | solution.py:388
  28.3 4.0 %collective-permute-start.7 = (f32[72,128]{1,0:T(8,128)S(1)}, f32[72,128]{1,0:T(8,128)S(1)}, u32[]{:S(2)}, u32[]{:S(2)}) collective-permute-start(f32[72,128]{1,0:T(8,128)S(1)} %add.24), channel_id=1, source_target_pairs={{0,1},{1,0},{2,3},{3,2},{4,5},{5,4},{6,7},{7,6},{8,9},{9,8},{10,11... | collective-permute-start | bytes 110600 | tf_op jit(solution)/shard_map/ppermute | solution.py:388
  32.3 4.0 %collective-permute-start.8 = (f32[72,128]{1,0:T(8,128)S(1)}, f32[72,128]{1,0:T(8,128)S(1)}, u32[]{:S(2)}, u32[]{:S(2)}) collective-permute-start(f32[72,128]{1,0:T(8,128)S(1)} %add.25), channel_id=1, source_target_pairs={{0,64},{4,68},{8,72},{12,76},{16,80},{20,84},{24,88},{28,92},{32,9... | collective-permute-start | bytes 110600 | tf_op jit(solution)/shard_map/ppermute | solution.py:388
  36.3 9.6 %collective-permute-start.9 = (f32[72,128]{1,0:T(8,128)S(1)}, f32[72,128]{1,0:T(8,128)S(1)}, u32[]{:S(2)}, u32[]{:S(2)}) collective-permute-start(f32[72,128]{1,0:T(8,128)S(1)} %add.26), channel_id=1, source_target_pairs={{0,8},{4,12},{8,0},{12,4},{16,24},{20,28},{24,16},{28,20},{32,40},... | collective-permute-start | bytes 110600 | tf_op jit(solution)/shard_map/ppermute | solution.py:388
  45.9 5.2 %collective-permute-start.10 = (f32[72,128]{1,0:T(8,128)S(1)}, f32[72,128]{1,0:T(8,128)S(1)}, u32[]{:S(2)}, u32[]{:S(2)}) collective-permute-start(f32[72,128]{1,0:T(8,128)S(1)} %add.27), channel_id=1, source_target_pairs={{0,3},{1,2},{2,1},{3,0},{4,7},{5,6},{6,5},{7,4},{8,11},{9,10},{10,... | collective-permute-start | bytes 110600 | tf_op jit(solution)/shard_map/ppermute | solution.py:388
  51.1 5.2 %collective-permute-start.11 = (f32[72,128]{1,0:T(8,128)S(1)}, f32[72,128]{1,0:T(8,128)S(1)}, u32[]{:S(2)}, u32[]{:S(2)}) collective-permute-start(f32[72,128]{1,0:T(8,128)S(1)} %add.28), channel_id=1, source_target_pairs={{0,192},{4,196},{8,200},{12,204},{16,208},{20,212},{24,216},{28,22... | collective-permute-start | bytes 110600 | tf_op jit(solution)/shard_map/ppermute | solution.py:388
  56.3 4.0 %collective-permute-start.12 = (f32[72,128]{1,0:T(8,128)S(1)}, f32[72,128]{1,0:T(8,128)S(1)}, u32[]{:S(2)}, u32[]{:S(2)}) collective-permute-start(f32[72,128]{1,0:T(8,128)S(1)} %add.29), channel_id=1, source_target_pairs={{0,24},{4,28},{8,16},{12,20},{16,8},{20,12},{24,0},{28,4},{32,56},... | collective-permute-start | bytes 110600 | tf_op jit(solution)/shard_map/ppermute | solution.py:388
  60.2 7.0 %collective-permute-start.13 = (f32[72,128]{1,0:T(8,128)S(1)}, f32[72,128]{1,0:T(8,128)S(1)}, u32[]{:S(2)}, u32[]{:S(2)}) collective-permute-start(f32[72,128]{1,0:T(8,128)S(1)} %add.30), channel_id=1, source_target_pairs={{0,56},{4,60},{8,48},{12,52},{16,40},{20,44},{24,32},{28,36},{32,2... | collective-permute-start | bytes 110600 | tf_op jit(solution)/shard_map/ppermute | solution.py:388

commit v3 on v2

v3 whole, which is shorter than its diff:
```python
import functools

import jax
import jax.numpy as jnp
from jax import lax
from jax.experimental import pallas as pl
from jax.experimental.pallas import tpu as pltpu
from jax.sharding import PartitionSpec as P

RANK = 112
ITERS = 3
PANEL = 8
LANES = 128
SLOT = 16


nu_limit = 0.125
ridge = 1.0
highest = lax.Precision.HIGHEST


def recip(value):
    return pltpu.reciprocal(value, approx=True)


def spread(block, lane):
    return jnp.broadcast_to(block[:, lane : lane + 1], block.shape)


def repeat(block, row):
    return jnp.broadcast_to(block[row : row + 1, :], block.shape)


def parts_of(value):
    high = value.astype(jnp.bfloat16).astype(jnp.float32)
    rest = value - high
    middle = rest.astype(jnp.bfloat16).astype(jnp.float32)
    return high, middle, rest - middle


def outer_sum(left, right):
    lh, lm, ll = parts_of(left)
    rh, rm, rl = parts_of(right)
    stacked_left = jnp.concatenate([lh, lh, lh, lm, lm, ll]).astype(jnp.bfloat16)
    stacked_right = jnp.concatenate([rh, rm, rl, rh, rm, rh]).astype(jnp.bfloat16)
    return lax.dot_general(
        stacked_left, stacked_right, (((0,), (0,)), ((), ())), preferred_element_type=jnp.float32
    )


def eliminate(cols, blocks, others):
    row_id = lax.broadcasted_iota(jnp.int32, blocks[0].shape, 0)
    pivots, inverses = jnp.ones_like(blocks[0]), jnp.ones_like(blocks[0])
    for j in range(0, PANEL, 2):
        first, cross = repeat(cols[j], j), repeat(cols[j], j + 1)
        corner = repeat(cols[j + 1], j + 1)
        first_inverse = recip(first)
        second_inverse = first * recip(first * corner - cross * cross)
        second = corner - cross * (cross * first_inverse)
        for i, pivot, inverse in ((j, first, first_inverse), (j + 1, second, second_inverse)):
            pivots = jnp.where(row_id == i, pivot, pivots)
            inverses = jnp.where(row_id == i, inverse, inverses)
        one = cols[j] * first_inverse
        cols[j + 1] = cols[j + 1] - one * cross
        two = cols[j + 1] * second_inverse
        for other in others:
            below = other["below"]
            other_one = below[j] * first_inverse
            below[j + 1] = below[j + 1] - other_one * cross
            other_two = below[j + 1] * second_inverse
            for m in range(j + 2, PANEL):
                a, b = repeat(cols[j], m), repeat(cols[j + 1], m)
                below[m] = (below[m] - other_one * a) - other_two * b
            for m in range(PANEL):
                a, b = repeat(below[j], m), repeat(below[j + 1], m)
                other["cols"][m] = (other["cols"][m] - other_one * a) - other_two * b
            for n, block in enumerate(blocks):
                other["blocks"][n] = other["blocks"][n] - other_one * repeat(block, j)
            other["two"] = other_two
        for m in range(j + 2, PANEL):
            a, b = repeat(cols[j], m), repeat(cols[j + 1], m)
            cols[m] = (cols[m] - one * a) - two * b
        one = jnp.where(row_id > j, one, 0.0)
        two = jnp.where(row_id > j + 1, two, 0.0)
        for n in range(len(blocks)):
            blocks[n] = blocks[n] - one * repeat(blocks[n], j)
            row = repeat(blocks[n], j + 1)
            blocks[n] = blocks[n] - two * row
            for other in others:
                other["blocks"][n] = other["blocks"][n] - other["two"] * row
    return pivots, inverses


def orthonormal_rows(inner, wide):
    width = inner.shape[1]
    both = jnp.concatenate([inner, wide], axis=1)
    matrix = [both[PANEL * k : PANEL * (k + 1)] for k in range(RANK // PANEL)]
    rows = []
    for k in range(0, len(matrix), 2):
        upper = [matrix[k][:, :width], matrix[k][:, width:]]
        lower = [matrix[k + 1][:, :width], matrix[k + 1][:, width:]]
        cols = [spread(upper[0], PANEL * k + j) for j in range(PANEL)]
        other = {
            "below": [spread(lower[0], PANEL * k + j) for j in range(PANEL)],
            "cols": [spread(lower[0], PANEL * (k + 1) + j) for j in range(PANEL)],
            "blocks": lower,
        }
        upper_pivots, upper_inverses = eliminate(cols, upper, [other])
        lower_pivots, lower_inverses = eliminate(other["cols"], lower, [])
        rows += [upper[1] * lax.rsqrt(upper_pivots), lower[1] * lax.rsqrt(lower_pivots)]
        if k + 2 < len(matrix):
            scaled = jnp.concatenate(
                [
                    jnp.concatenate([block * upper_inverses for block in upper], axis=1),
                    jnp.concatenate([block * lower_inverses for block in lower], axis=1),
                ]
            )
            update = outer_sum(jnp.concatenate([upper[0], lower[0]]), scaled)
            for m in range(k + 2, len(matrix)):
                matrix[m] = matrix[m] - update[PANEL * m : PANEL * (m + 1)]
    return jnp.concatenate(rows, axis=0)


def basis_kernel(total_ref, snap_ref, out_ref, basis_ref, *, rows_all):
    cols = total_ref.shape[1]
    row_id, col_id = ids((cols, cols))
    identity = jnp.where(row_id == col_id, jnp.float32(ridge), 0.0)
    gram_matrix = unfolded(total_ref[...]) / rows_all + identity

    def sweep(step, carry):
        @pl.when(step == 0)
        def _():
            basis_ref[...] = gram_matrix[:RANK, :]

        @pl.when(step > 0)
        def _():
            basis_ref[...] = jnp.dot(
                basis_ref[...], gram_matrix, precision=highest, preferred_element_type=jnp.float32
            )

        wide = basis_ref[...]
        full = jnp.concatenate([wide, jnp.zeros((cols - RANK, cols), jnp.float32)], axis=0)
        inner = lax.dot_general(
            wide, full, (((1,), (1,)), ((), ())), precision=highest, preferred_element_type=jnp.float32
        )
        basis_ref[...] = orthonormal_rows(inner, wide)
        return carry

    lax.fori_loop(0, ITERS, sweep, 0)
    basis = basis_ref[...]
    blocks, cols = out_ref.shape[0] // RANK, basis.shape[1]
    for block in range(blocks):
        out_ref[pl.ds(block, RANK, stride=blocks), :] = jnp.dot(
            basis,
            snap_ref[pl.ds(block, cols, stride=SLOT), :],
            precision=highest,
            preferred_element_type=jnp.float32,
        )


def project(gram_total, snapshots, rows_all):
    cols = gram_total.shape[1]
    return pl.pallas_call(
        functools.partial(basis_kernel, rows_all=rows_all),
        out_shape=jax.ShapeDtypeStruct((RANK * 12, LANES), jnp.float32),
        in_specs=[pl.BlockSpec(memory_space=pltpu.VMEM)] * 2,
        out_specs=pl.BlockSpec(memory_space=pltpu.VMEM),
        scratch_shapes=[pltpu.VMEM((RANK, cols), jnp.float32)],
        compiler_params=pltpu.CompilerParams(vmem_limit_bytes=16 * 2**20),
        name="basis",
    )(gram_total, snapshots)


def exact_dot(values, one_hot):
    high, middle, low = (part.astype(jnp.bfloat16) for part in parts_of(values))
    dot = functools.partial(jnp.dot, preferred_element_type=jnp.float32)
    return (dot(low, one_hot) + dot(middle, one_hot)) + dot(high, one_hot)


def sorting(size, to_sorted):
    cell = lax.broadcasted_iota(jnp.int32, (size, size), 0 if to_sorted else 1)
    spot = lax.broadcasted_iota(jnp.int32, (size, size), 1 if to_sorted else 0)
    place = (cell & 3) * (size // 4) + (cell >> 2)
    return jnp.where(place == spot, 1.0, 0.0).astype(jnp.bfloat16)


def edges_kernel(velocity_ref, coef_ref, low_ref, high_ref, arrived):
    layers, rows_z = low_ref.shape[2], coef_ref.shape[1]
    copies = []
    for n, (edge_ref, start) in enumerate(((low_ref, 0), (high_ref, rows_z - layers))):
        rows = pl.ds(start, layers)
        copies += [
            pltpu.make_async_copy(velocity_ref.at[:, :, rows], edge_ref.at[:3], arrived.at[2 * n]),
            pltpu.make_async_copy(coef_ref.at[:, rows], edge_ref.at[3], arrived.at[2 * n + 1]),
        ]
    for copy in copies:
        copy.start()
    for copy in copies:
        copy.wait()


def edges(velocity, smag_coef):
    rows_y, _, size_x = smag_coef.shape
    edge = jax.ShapeDtypeStruct((4, rows_y, 4, size_x), jnp.float32)
    return pl.pallas_call(
        edges_kernel,
        out_shape=(edge, edge),
        in_specs=[pl.BlockSpec(memory_space=pltpu.HBM)] * 2,
        out_specs=[pl.BlockSpec(memory_space=pltpu.VMEM)] * 2,
        scratch_shapes=[pltpu.SemaphoreType.DMA((4,))],
        compiler_params=pltpu.CompilerParams(vmem_limit_bytes=2 * 2**20),
        name="edges",
    )(*(pltpu.with_memory_space_constraint(a, pltpu.HBM) for a in (velocity, smag_coef)))


def pack_kernel(velocity_ref, coef_ref, block_ref):
    rows_y, rows_z, size_x = coef_ref.shape
    rows = [velocity_ref[c].reshape(-1, size_x) for c in range(3)] + [coef_ref[...].reshape(-1, size_x)]
    done = exact_dot(jnp.concatenate(rows), sorting(size_x, True))
    for c in range(4):
        for y in range(rows_y):
            start = (c * rows_y + y) * rows_z
            for o in range(4):
                block_ref[c, y, o] = done[start : start + rows_z, LANES * o : LANES * (o + 1)]


def pack(velocity, smag_coef):
    rows_y, rows_z, _ = smag_coef.shape
    return pl.pallas_call(
        pack_kernel,
        out_shape=jax.ShapeDtypeStruct((4, rows_y, 4, rows_z, LANES), jnp.float32),
        in_specs=[pl.BlockSpec(memory_space=pltpu.VMEM)] * 2,
        out_specs=pl.BlockSpec(memory_space=pltpu.VMEM),
        compiler_params=pltpu.CompilerParams(vmem_limit_bytes=12 * 2**20),
        name="pack",
    )(velocity, smag_coef)


def sides_kernel(low_ref, high_ref, sides_ref, up_ref, down_ref):
    rows_y, layers, size_x = low_ref.shape[1:]
    rows = jnp.concatenate([high_ref[...], low_ref[...]], axis=2).reshape(-1, size_x)
    done = exact_dot(rows, sorting(size_x, True))
    for c in range(4):
        for y in range(rows_y):
            start = 2 * layers * (c * rows_y + y)
            for o in range(4):
                part = done[start : start + 2 * layers, LANES * o : LANES * (o + 1)]
                sides_ref[c, y, o] = part
                near, far = (0, layers + 2), rows_y - 2
                for ref, away in ((up_ref, rows_y - 1 - y), (down_ref, y)):
                    if away == 0:
                        ref[c, 0, o] = part
                    elif away <= far:
                        for side, begin in enumerate(near):
                            to = 4 * (away - 1) + 2 * side
                            ref[c, 1, o, to : to + 2] = part[begin : begin + 2]


def sort_sides(low, high):
    _, rows_y, layers, _ = low.shape
    shape = lambda rows: jax.ShapeDtypeStruct((4, rows, 4, 2 * layers, LANES), jnp.float32)
    return pl.pallas_call(
        sides_kernel,
        out_shape=(shape(rows_y), shape(2), shape(2)),
        in_specs=[pl.BlockSpec(memory_space=pltpu.VMEM)] * 2,
        out_specs=[pl.BlockSpec(memory_space=pltpu.VMEM)] * 3,
        compiler_params=pltpu.CompilerParams(vmem_limit_bytes=12 * 2**20),
        cost_estimate=pl.CostEstimate(flops=2 * 10**10, bytes_accessed=10**6, transcendentals=0),
        name="sides",
    )(low, high)


def around_x(ref, index, o):
    ahead = ref[(*index, o + 1)] if o < 3 else pltpu.roll(ref[(*index, 0)], LANES - 1, 1)
    behind = ref[(*index, o - 1)] if o > 0 else pltpu.roll(ref[(*index, 3)], 1, 1)
    return ahead, behind


def around_z(plane):
    return pltpu.roll(plane, plane.shape[0] - 1, 0), pltpu.roll(plane, 1, 0)


def half_viscosity(cells_ref, y, o, coefficient):
    jump = []
    for c in range(3):
        x_ahead, x_behind = around_x(cells_ref, (c, y), o)
        z_ahead, z_behind = around_z(cells_ref[c, y, o])
        jump.append(
            (x_ahead - x_behind, cells_ref[c, y + 1, o] - cells_ref[c, y - 1, o], z_ahead - z_behind)
        )
    total = jump[0][0] ** 2 + jump[1][1] ** 2 + jump[2][2] ** 2
    total = total + total
    for c, d in ((0, 1), (0, 2), (1, 2)):
        total = total + (jump[c][d] + jump[d][c]) ** 2
    rate = coefficient * (0.5 * total * lax.rsqrt(jnp.maximum(total, 1e-37)))
    return (0.5 * nu_limit) * rate * recip(1.0 + rate)


def stepped(cells_ref, y, visc_ref, v, o):
    here = visc_ref[v, o]
    visc = [*around_x(visc_ref, (v,), o), visc_ref[v + 1, o], visc_ref[v - 1, o], *around_z(here)]
    visc = [here + other for other in visc]
    result = []
    for c in range(3):
        centre = cells_ref[c, y, o]
        cells = [
            *around_x(cells_ref, (c, y), o),
            cells_ref[c, y + 1, o],
            cells_ref[c, y - 1, o],
            *around_z(centre),
        ]
        change = visc[0] * (cells[0] - centre)
        for n in range(1, 6):
            change = change + visc[n] * (cells[n] - centre)
        result.append(centre + change)
    return result


def ids(shape):
    return lax.broadcasted_iota(jnp.int32, shape, 0), lax.broadcasted_iota(jnp.int32, shape, 1)


def folded(gram):
    half = gram.shape[0] // 2
    row, lane = ids((half, 2 * half))
    corner = pltpu.roll(gram[half:], half, 1)
    square = jnp.where(lane < row, corner, gram[:half])
    diagonal = jnp.sum(jnp.where(lane == row, corner, 0.0), axis=0, keepdims=True)
    return jnp.concatenate([square, jnp.broadcast_to(diagonal, (8, 2 * half))], axis=0)


def unfolded(parts):
    half = parts.shape[1] // 2
    row, lane = ids((half, 2 * half))
    square = parts[:half]
    upper = jnp.where(lane > row, square, 0.0)
    lower = pltpu.roll(jnp.where(lane < row, square, 0.0), half, 1)
    one_side = jnp.concatenate([upper, lower], axis=0)
    below = pltpu.roll(jnp.broadcast_to(parts[half : half + 1], square.shape), half, 1)
    diagonal = jnp.concatenate(
        [jnp.where(lane == row, square, 0.0), jnp.where(lane == row + half, below, 0.0)], axis=0
    )
    return one_side + one_side.T + diagonal


def steps_kernel(
    code_ref, block_ref, before_ref, after_ref, sides_ref, side_before_ref, side_after_ref,
    wide_ref, snap_ref, gram_ref,
    cells_ref, visc_ref, one_ref, two_ref, all_ref,
):
    _, rows_y, _, rows_z, _ = block_ref.shape
    cols = gram_ref.shape[1]
    place_y = lax.axis_index("gy")
    first, last = place_y == 0, place_y == lax.axis_size("gy") - 1
    for c in range(4):
        for y in range(rows_y):
            for o in range(4):
                cells_ref[c, rows_y + y, o, :rows_z] = block_ref[c, y, o]
                halo = jnp.where(first, 0.0, before_ref[c, y, o])
                cells_ref[c, y, o, :rows_z] = halo
                halo = jnp.where(last, 0.0, after_ref[c, y, o])
                cells_ref[c, 2 * rows_y + y, o, :rows_z] = halo
                side = (slice(rows_z, rows_z + sides_ref.shape[3]),)
                cells_ref[(c, rows_y + y, o, *side)] = sides_ref[c, y, o]
                for ref, wall, at, away in (
                    (side_before_ref, first, y, rows_y - 1 - y),
                    (side_after_ref, last, 2 * rows_y + y, y),
                ):
                    if away == 0:
                        cells_ref[(c, at, o, *side)] = jnp.where(wall, 0.0, ref[c, 0, o])
                    elif away <= rows_y - 2:
                        for n, begin in enumerate((rows_z, rows_z + sides_ref.shape[3] - 2)):
                            to = 4 * (away - 1) + 2 * n
                            halo = jnp.where(wall, 0.0, ref[c, 1, o, to : to + 2])
                            cells_ref[c, at, o, begin : begin + 2] = halo

    @pl.when(first)
    def _():
        for y in range(1, rows_y):
            cells_ref[3, y] = cells_ref[3, rows_y]

    @pl.when(last)
    def _():
        for y in range(rows_y - 1):
            cells_ref[3, 2 * rows_y + y] = cells_ref[3, 2 * rows_y - 1]

    def visc_one(y, carry):
        for o in range(4):
            visc_ref[y, o] = half_viscosity(cells_ref, y, o, cells_ref[3, y, o])
        return carry

    lax.fori_loop(1, 3 * rows_y - 1, visc_one, 0)

    def step_one(y, carry):
        outside = jnp.logical_or(
            jnp.logical_and(first, y < rows_y), jnp.logical_and(last, y >= 2 * rows_y)
        )
        for o in range(4):
            for c, cells in enumerate(stepped(cells_ref, y, visc_ref, y, o)):
                one_ref[c, y, o] = jnp.where(outside, 0.0, cells)
        return carry

    lax.fori_loop(2, 3 * rows_y - 2, step_one, 0)

    def visc_two(y, carry):
        for o in range(4):
            visc_ref[y, o] = half_viscosity(one_ref, y, o, cells_ref[3, y, o])
        return carry

    lax.fori_loop(rows_y - 1, 2 * rows_y + 1, visc_two, 0)

    for y in range(rows_y):
        for o in range(4):
            for c, cells in enumerate(stepped(one_ref, rows_y + y, visc_ref, rows_y + y, o)):
                two_ref[c, y, o] = cells[:rows_z]
                start = (c * rows_y + y) * rows_z
                wide_ref[start : start + rows_z, LANES * o : LANES * (o + 1)] = cells[:rows_z]
    for state, (ref, shift) in enumerate(((block_ref, 0), (one_ref, rows_y), (two_ref, 0))):
        for y in range(rows_y):
            for z in range(4):
                for o in range(4):
                    start = SLOT * (64 * state + 16 * y + 4 * z + o)
                    for c in range(3):
                        piece = ref[c, shift + y, o, pl.ds(z, rows_z // 4, stride=4), :]
                        all_ref[start + 4 * c : start + 4 * c + 4, :] = piece

    def choose(column, carry):
        source = pl.multiple_of(code_ref[column] * SLOT, SLOT)
        target = pl.multiple_of(column * SLOT, SLOT)
        snap_ref[pl.ds(target, SLOT), :] = all_ref[pl.ds(source, SLOT), :]
        return carry

    lax.fori_loop(0, cols, choose, 0, unroll=16)
    even, odd = jnp.zeros((cols, cols), jnp.float32), jnp.zeros((cols, cols), jnp.float32)
    across = functools.partial(
        lax.dot_general,
        dimension_numbers=(((1,), (1,)), ((), ())),
        preferred_element_type=jnp.float32,
    )
    for block in range(0, 12, 2):
        part = jnp.concatenate(
            [snap_ref[pl.ds(block + i, cols, stride=SLOT), :] for i in range(2)], axis=1
        )
        high, middle, low = (p.astype(jnp.bfloat16) for p in parts_of(part))
        odd = odd + (across(high, low) + across(high, middle))
        even = even + (across(middle, middle) + across(high, high))
    gram_ref[...] = folded(even + (odd + odd.T))


def unsort_kernel(wide_ref, final_ref):
    final_ref[...] = exact_dot(wide_ref[...], sorting(wide_ref.shape[1], False)).reshape(final_ref.shape)


def unsort(wide, shape):
    return pl.pallas_call(
        unsort_kernel,
        out_shape=jax.ShapeDtypeStruct(shape, jnp.float32),
        in_specs=[pl.BlockSpec(memory_space=pltpu.VMEM)],
        out_specs=pl.BlockSpec(memory_space=pltpu.VMEM),
        compiler_params=pltpu.CompilerParams(vmem_limit_bytes=12 * 2**20),
        cost_estimate=pl.CostEstimate(flops=4 * 10**9, bytes_accessed=10**6, transcendentals=0),
        name="unsort",
    )(wide)


def both_steps(snap_code, block, *halo):
    _, rows_y, _, rows_z, _ = block.shape
    cols = snap_code.shape[0]
    f32 = lambda *shape: jax.ShapeDtypeStruct(shape, jnp.float32)
    scratch = lambda *shape: pltpu.VMEM(shape, jnp.float32)
    depth = rows_z + 8
    return pl.pallas_call(
        steps_kernel,
        out_shape=(
            f32(3 * rows_y * rows_z, 4 * LANES),
            f32(SLOT * cols, LANES),
            f32(cols // 2 + 8, cols),
        ),
        in_specs=[pl.BlockSpec(memory_space=pltpu.SMEM)]
        + [pl.BlockSpec(memory_space=pltpu.VMEM)] * (1 + len(halo)),
        out_specs=[pl.BlockSpec(memory_space=pltpu.VMEM)] * 3,
        scratch_shapes=[
            scratch(4, 3 * rows_y, 4, depth, LANES),
            scratch(3 * rows_y, 4, depth, LANES),
            scratch(3, 3 * rows_y, 4, depth, LANES),
            scratch(3, rows_y, 4, rows_z, LANES),
            scratch(SLOT * 192, LANES),
        ],
        compiler_params=pltpu.CompilerParams(vmem_limit_bytes=32 * 2**20),
        name="steps",
    )(snap_code, block, *halo)


def device_sum(part):
    ring = 8
    swaps = (lambda z: z ^ 1, lambda z: ((z + 1) ^ 1) - 1, lambda z: 7 - z if z % 4 in (1, 2) else z ^ 3)

    def along_z(swap):
        return lambda i: i - i // 2 % ring * 2 + swap(i // 2 % ring) % ring * 2

    flip = lambda bits: lambda i: i ^ bits
    steps = [
        ("gy", flip(1)),
        ("gz", flip(1)),
        ("gy", flip(16)),
        ("gy", along_z(swaps[0])),
        ("gz", flip(3)),
        ("gy", flip(48)),
        ("gy", along_z(swaps[1])),
        ("gy", along_z(swaps[2])),
    ]
    for axis, partner in steps:
        count = lax.axis_size(axis)
        part = part + lax.ppermute(part, axis, [(i, partner(i)) for i in range(count)])
    return part


def local(velocity, smag_coef, snap_code):
    count_y, count_z = lax.axis_size("gy"), lax.axis_size("gz")

    def along_z(part, step):
        return lax.ppermute(part, "gz", [(i, (i + step) % count_z) for i in range(count_z)])

    def along_y(part, step):
        return lax.ppermute(part, "gy", [(i, (i + step) % count_y) for i in range(count_y)])

    low, high = edges(velocity, smag_coef)
    velocity, smag_coef, low, high = lax.optimization_barrier((velocity, smag_coef, low, high))
    sides, up, down = sort_sides(along_z(high, 1), along_z(low, -1))
    side_before, side_after = along_y(up, 1), along_y(down, -1)
    block = pack(velocity, smag_coef)
    before, after = along_y(block, 1), along_y(block, -1)
    wide, snapshots, gram = both_steps(
        snap_code, block, before, after, sides, side_before, side_after
    )
    rows_y, rows_z = velocity.shape[1], velocity.shape[2]
    rows_all = 12 * LANES * count_y * count_z
    pod_modes = project(device_sum(gram), snapshots, rows_all)
    return (unsort(wide, velocity.shape), pod_modes.reshape(RANK, 3, rows_y // 4, rows_z // 4, LANES))


def solution(mesh):
    placed = (P(None, "gy", "gz", None), P("gy", "gz", None), P())
    return jax.shard_map(
        local,
        mesh=mesh,
        in_specs=placed,
        out_specs=(P(None, "gy", "gz", None), P(None, None, "gy", "gz", None)),
        check_vma=False,
    )
```

time: 85 us -> 76.1 us (0.90)
  Pallas kernels: 23.3 us -> 19.8 us
  local copies, waits for them, and re-layouts: 2.5 us -> 0.01 us
  waiting for transfers between devices: 36.5 us -> 35 us
    ppermute x2, waiting for transfers between devices: 7.07 us -> 1.98 us  [along_z(): lax.ppermute(part, 'gz', [(i, (i + step) % count_z) for i in range(count_...]
    pallas_call x1, Pallas kernels: 16.2 us -> 11.2 us  [project(): pl.pallas_call(functools.partial(basis_kernel, rows_all=rows_all), out_sh...]
    ppermute x4, waiting for transfers between devices: 2.6 us -> 5.44 us  [along_y(): lax.ppermute(part, 'gy', [(i, (i + step) % count_y) for i in range(count_...]
    unnamed x6, local copies, waits for them, and re-layouts: 2.47 us -> 0.01 us
    pallas_call x2 -> x5, Pallas kernels: 7.05 us -> 8.58 us  [the longest x1 5.14 us: both_steps(): pl.pallas_call(steps_kernel, out_shape=(f32(3 * rows_y * rows_z, 4 * LANE...]
    ppermute x8, starting transfers between devices: 15.1 us -> 14 us  [device_sum(): lax.ppermute(part, axis, [(i, partner(i)) for i in range(count)])]
  transfers between devices with their start and end apart: 14 -> 14, of which waited for: 11 -> 10; matrix products, arithmetic and copies ran while one was open for 0% -> 0% of each run, Pallas kernels for 0% -> 3%
where the time goes in v3:
time: 76.1 us; the launch traced here: 75.3 us
  waiting for transfers between devices  35 us (46%)
  Pallas kernels  19.8 us (26%)
  starting transfers between devices  19.7 us (26%)
    ppermute x8, waiting for transfers between devices, device_sum(): lax.ppermute(part, axis, [(i, partner(i)) for i in range(count)])  27.6 us
    ppermute x8, starting transfers between devices, device_sum(): lax.ppermute(part, axis, [(i, partner(i)) for i in range(count)])  14 us
    pallas_call x1, Pallas kernels, project(): pl.pallas_call(functools.partial(basis_kernel, rows_all=rows_all), out_sh...  11.2 us
    ppermute x4, waiting for transfers between devices, along_y(): lax.ppermute(part, 'gy', [(i, (i + step) % count_y) for i in range(count_...  5.44 us
    pallas_call x1, Pallas kernels, both_steps(): pl.pallas_call(steps_kernel, out_shape=(f32(3 * rows_y * rows_z, 4 * LANE...  5.14 us
    ppermute x2, starting transfers between devices, along_z(): lax.ppermute(part, 'gz', [(i, (i + step) % count_z) for i in range(count_...  3.31 us
    ppermute x4, starting transfers between devices, along_y(): lax.ppermute(part, 'gy', [(i, (i + step) % count_y) for i in range(count_...  2.38 us
    ppermute x2, waiting for transfers between devices, along_z(): lax.ppermute(part, 'gz', [(i, (i + step) % count_z) for i in range(count_...  1.98 us
  transfers between devices with their start and end apart: 14, of which 10 were waited for; matrix products, arithmetic and copies ran while one was open for 0% of the time, Pallas kernels for 3%

profile of v3, /device:TPU:32, one launch (start us, length us, event | category | flops | bytes accessed | tf_op | source)
XLA Modules:
  0.0 75.3 jit_solution(17649503632500141405)
XLA Ops:
  0.6 1.1 %edges.1 = (f32[4,4,4,512]{3,2,1,0:T(4,128)S(1)}, f32[4,4,4,512]{3,2,1,0:T(4,128)S(1)}) custom-call(f32[3,4,16,512]{3,2,1,0:T(8,128)} %velocity_ref.2, f32[4,16,512]{2,1,0:T(8,128)} %coef_ref.2), custom_call_target="tpu_custom_call" | custom-call | tf_op jit(solution)/shard_map/edges/pallas_call | solution.py:205
  1.7 1.6 %collective-permute-start.2 = (f32[4,4,4,512]{3,2,1,0:T(4,128)S(1)}, f32[4,4,4,512]{3,2,1,0:T(4,128)S(1)}, u32[]{:S(2)}, u32[]{:S(2)}) collective-permute-start(f32[4,4,4,512]{3,2,1,0:T(4,128)S(1)} %get-tuple-element.18), channel_id=1, source_target_pairs={{0,1},{1,2},{2,3},{3,0},{4,5},{5,6},{6,7},{7,4},{8,9},{9,10},{10,1... | collective-permute-start | bytes 393224 | tf_op jit(solution)/shard_map/ppermute | solution.py:522
  3.3 1.7 %collective-permute-start.3 = (f32[4,4,4,512]{3,2,1,0:T(4,128)S(1)}, f32[4,4,4,512]{3,2,1,0:T(4,128)S(1)}, u32[]{:S(2)}, u32[]{:S(2)}) collective-permute-start(f32[4,4,4,512]{3,2,1,0:T(4,128)S(1)} %get-tuple-element.19), channel_id=1, source_target_pairs={{0,3},{1,0},{2,1},{3,2},{4,7},{5,4},{6,5},{7,6},{8,11},{9,8},{10,9... | collective-permute-start | bytes 393224 | tf_op jit(solution)/shard_map/ppermute | solution.py:522
  5.0 0.6 pack.1.block_ref
  5.8 0.5 collective-permute-start
  6.3 2.0 %collective-permute-done.2.low_ref = f32[4,4,4,512]{3,2,1,0:T(4,128)S(1)} collective-permute-done((f32[4,4,4,512]{3,2,1,0:T(4,128)S(1)}, f32[4,4,4,512]{3,2,1,0:T(4,128)S(1)}, u32[]{:S(2)}, u32[]{:S(2)}) %collective-permute-start.2) | collective-permute-done | bytes 131104 | tf_op jit(solution)/shard_map/ppermute | solution.py:522
  8.3 0.5 sides.1
  8.8 1.7 %collective-permute-start.5 = (f32[4,2,4,8,128]{4,3,2,1,0:T(8,128)S(1)}, f32[4,2,4,8,128]{4,3,2,1,0:T(8,128)S(1)}, u32[]{:S(2)}, u32[]{:S(2)}) collective-permute-start(f32[4,2,4,8,128]{4,3,2,1,0:T(8,128)S(1)} %get-tuple-element.22), channel_id=1, source_target_pairs={{0,252},{4,0},{8,4},{12,8},{16,12},{20,16},{24,20},{28,24},{32,28}... | collective-permute-start | bytes 393224 | tf_op jit(solution)/shard_map/ppermute | solution.py:525
  10.6 5.4 %collective-permute-done.4.side_before_ref = f32[4,2,4,8,128]{4,3,2,1,0:T(8,128)S(1)} collective-permute-done((f32[4,2,4,8,128]{4,3,2,1,0:T(8,128)S(1)}, f32[4,2,4,8,128]{4,3,2,1,0:T(8,128)S(1)}, u32[]{:S(2)}, u32[]{:S(2)}) %collective-permute-start.4) | collective-permute-done | bytes 131104 | tf_op jit(solution)/shard_map/ppermute | solution.py:525
  16.0 5.1 %steps.1 = (f32[192,512]{1,0:T(8,128)S(1)}, f32[2048,128]{1,0:T(8,128)S(1)}, f32[72,128]{1,0:T(8,128)S(1)}) custom-call(s32[128]{0:T(128)S(1)} %copy-done.2, f32[4,4,4,16,128]{4,3,2,1,0:T(8,128)S(1)} %pack.1.block_ref, f32[4,4,4,16,128]{4,3,2,1,0:T(8,128)S(1)} %collective-permute-done.before_ref, f32[4,4,4,16,128]{4,3,2,1,0:T(8,128)S(1)} %collective-permute-done.1.after_ref, ...), custom_call_target="tpu_custom_call" | custom-call | tf_op jit(solution)/shard_map/steps/pallas_call | solution.py:472
  21.4 1.1 %collective-permute-done.6 = f32[72,128]{1,0:T(8,128)S(1)} collective-permute-done((f32[72,128]{1,0:T(8,128)S(1)}, f32[72,128]{1,0:T(8,128)S(1)}, u32[]{:S(2)}, u32[]{:S(2)}) %collective-permute-start.6) | collective-permute-done | bytes 36896 | tf_op jit(solution)/shard_map/ppermute | solution.py:514
  22.5 0.4 collective-permute-start.7
  22.9 3.6 %collective-permute-done.7 = f32[72,128]{1,0:T(8,128)S(1)} collective-permute-done((f32[72,128]{1,0:T(8,128)S(1)}, f32[72,128]{1,0:T(8,128)S(1)}, u32[]{:S(2)}, u32[]{:S(2)}) %collective-permute-start.7) | collective-permute-done | bytes 36896 | tf_op jit(solution)/shard_map/ppermute | solution.py:514
  26.4 1.4 %collective-permute-start.8 = (f32[72,128]{1,0:T(8,128)S(1)}, f32[72,128]{1,0:T(8,128)S(1)}, u32[]{:S(2)}, u32[]{:S(2)}) collective-permute-start(f32[72,128]{1,0:T(8,128)S(1)} %add.25), channel_id=1, source_target_pairs={{0,64},{4,68},{8,72},{12,76},{16,80},{20,84},{24,88},{28,92},{32,9... | collective-permute-start | bytes 110600 | tf_op jit(solution)/shard_map/ppermute | solution.py:514
  27.9 2.5 %collective-permute-done.8 = f32[72,128]{1,0:T(8,128)S(1)} collective-permute-done((f32[72,128]{1,0:T(8,128)S(1)}, f32[72,128]{1,0:T(8,128)S(1)}, u32[]{:S(2)}, u32[]{:S(2)}) %collective-permute-start.8) | collective-permute-done | bytes 36896 | tf_op jit(solution)/shard_map/ppermute | solution.py:514
  30.4 10.4 %collective-permute-start.9 = (f32[72,128]{1,0:T(8,128)S(1)}, f32[72,128]{1,0:T(8,128)S(1)}, u32[]{:S(2)}, u32[]{:S(2)}) collective-permute-start(f32[72,128]{1,0:T(8,128)S(1)} %add.26), channel_id=1, source_target_pairs={{0,8},{4,12},{8,0},{12,4},{16,24},{20,28},{24,16},{28,20},{32,40},... | collective-permute-start | bytes 110600 | tf_op jit(solution)/shard_map/ppermute | solution.py:514
  40.8 1.9 %collective-permute-done.9 = f32[72,128]{1,0:T(8,128)S(1)} collective-permute-done((f32[72,128]{1,0:T(8,128)S(1)}, f32[72,128]{1,0:T(8,128)S(1)}, u32[]{:S(2)}, u32[]{:S(2)}) %collective-permute-start.9) | collective-permute-done | bytes 36896 | tf_op jit(solution)/shard_map/ppermute | solution.py:514
  42.7 1.5 %collective-permute-start.10 = (f32[72,128]{1,0:T(8,128)S(1)}, f32[72,128]{1,0:T(8,128)S(1)}, u32[]{:S(2)}, u32[]{:S(2)}) collective-permute-start(f32[72,128]{1,0:T(8,128)S(1)} %add.27), channel_id=1, source_target_pairs={{0,3},{1,2},{2,1},{3,0},{4,7},{5,6},{6,5},{7,4},{8,11},{9,10},{10,... | collective-permute-start | bytes 110600 | tf_op jit(solution)/shard_map/ppermute | solution.py:514
  44.3 3.6 %collective-permute-done.10 = f32[72,128]{1,0:T(8,128)S(1)} collective-permute-done((f32[72,128]{1,0:T(8,128)S(1)}, f32[72,128]{1,0:T(8,128)S(1)}, u32[]{:S(2)}, u32[]{:S(2)}) %collective-permute-start.10) | collective-permute-done | bytes 36896 | tf_op jit(solution)/shard_map/ppermute | solution.py:514
  47.9 5.2 %collective-permute-done.11 = f32[72,128]{1,0:T(8,128)S(1)} collective-permute-done((f32[72,128]{1,0:T(8,128)S(1)}, f32[72,128]{1,0:T(8,128)S(1)}, u32[]{:S(2)}, u32[]{:S(2)}) %collective-permute-start.11) | collective-permute-done | bytes 36896 | tf_op jit(solution)/shard_map/ppermute | solution.py:514
  53.1 4.0 %collective-permute-done.12 = f32[72,128]{1,0:T(8,128)S(1)} collective-permute-done((f32[72,128]{1,0:T(8,128)S(1)}, f32[72,128]{1,0:T(8,128)S(1)}, u32[]{:S(2)}, u32[]{:S(2)}) %collective-permute-start.12) | collective-permute-done | bytes 36896 | tf_op jit(solution)/shard_map/ppermute | solution.py:514
  57.1 1.3 %unsort.1 = f32[3,4,16,512]{3,2,1,0:T(8,128)} custom-call(f32[192,512]{1,0:T(8,128)S(1)} %get-tuple-element.23.wide_ref), custom_call_target="tpu_custom_call" | custom-call | flops 4000000000 | bytes 1000000 | tf_op jit(solution)/shard_map/unsort/pallas_call | solution.py:455
  58.4 5.7 %collective-permute-done.13 = f32[72,128]{1,0:T(8,128)S(1)} collective-permute-done((f32[72,128]{1,0:T(8,128)S(1)}, f32[72,128]{1,0:T(8,128)S(1)}, u32[]{:S(2)}, u32[]{:S(2)}) %collective-permute-start.13) | collective-permute-done | bytes 36896 | tf_op jit(solution)/shard_map/ppermute | solution.py:514
  64.1 11.2 %basis.1 = f32[1344,128]{1,0:T(8,128)} custom-call(f32[72,128]{1,0:T(8,128)S(1)} %add.31.total_ref, f32[2048,128]{1,0:T(8,128)S(1)} %get-tuple-element.25.snap_ref), custom_call_target="tpu_custom_call" | custom-call | tf_op jit(solution)/shard_map/basis/pallas_call | solution.py:163
  (24 shorter events, 0.5 us)
Async XLA Ops:
  0.6 4.4 %copy-start.1 = (f32[4,16,512]{2,1,0:T(8,128)S(1)}, f32[4,16,512]{2,1,0:T(8,128)}, u32[]{:S(2)}) copy-start(f32[4,16,512]{2,1,0:T(8,128)} %coef_ref.2) | copy-start | bytes 393220
  0.6 4.4 %copy-start = (f32[3,4,16,512]{3,2,1,0:T(8,128)S(1)}, f32[3,4,16,512]{3,2,1,0:T(8,128)}, u32[]{:S(2)}) copy-start(f32[3,4,16,512]{3,2,1,0:T(8,128)} %velocity_ref.2) | copy-start | bytes 1179652
  1.7 6.5 %collective-permute-start.2 = (f32[4,4,4,512]{3,2,1,0:T(4,128)S(1)}, f32[4,4,4,512]{3,2,1,0:T(4,128)S(1)}, u32[]{:S(2)}, u32[]{:S(2)}) collective-permute-start(f32[4,4,4,512]{3,2,1,0:T(4,128)S(1)} %get-tuple-element.18), channel_id=1, source_target_pairs={{0,1},{1,2},{2,3},{3,0},{4,5},{5,6},{6,7},{7,4},{8,9},{9,10},{10,1... | collective-permute-start | bytes 393224 | tf_op jit(solution)/shard_map/ppermute | solution.py:522
  3.3 5.0 %collective-permute-start.3 = (f32[4,4,4,512]{3,2,1,0:T(4,128)S(1)}, f32[4,4,4,512]{3,2,1,0:T(4,128)S(1)}, u32[]{:S(2)}, u32[]{:S(2)}) collective-permute-start(f32[4,4,4,512]{3,2,1,0:T(4,128)S(1)} %get-tuple-element.19), channel_id=1, source_target_pairs={{0,3},{1,0},{2,1},{3,2},{4,7},{5,4},{6,5},{7,6},{8,11},{9,8},{10,9... | collective-permute-start | bytes 393224 | tf_op jit(solution)/shard_map/ppermute | solution.py:522
  5.7 10.3 %collective-permute-start.1 = (f32[4,4,4,16,128]{4,3,2,1,0:T(8,128)S(1)}, f32[4,4,4,16,128]{4,3,2,1,0:T(8,128)S(1)}, u32[]{:S(2)}, u32[]{:S(2)}) collective-permute-start(f32[4,4,4,16,128]{4,3,2,1,0:T(8,128)S(1)} %pack.1.block_ref), channel_id=1, source_target_pairs={{0,252},{4,0},{8,4},{12,8},{16,12},{20,16},{24,20},{28,24},{32,28}... | collective-permute-start | bytes 1572872 | tf_op jit(solution)/shard_map/ppermute | solution.py:525
  5.8 10.2 %collective-permute-start = (f32[4,4,4,16,128]{4,3,2,1,0:T(8,128)S(1)}, f32[4,4,4,16,128]{4,3,2,1,0:T(8,128)S(1)}, u32[]{:S(2)}, u32[]{:S(2)}) collective-permute-start(f32[4,4,4,16,128]{4,3,2,1,0:T(8,128)S(1)} %pack.1.block_ref), channel_id=1, source_target_pairs={{0,4},{4,8},{8,12},{12,16},{16,20},{20,24},{24,28},{28,32},{32,36}... | collective-permute-start | bytes 1572872 | tf_op jit(solution)/shard_map/ppermute | solution.py:525
  8.7 7.3 %collective-permute-start.4 = (f32[4,2,4,8,128]{4,3,2,1,0:T(8,128)S(1)}, f32[4,2,4,8,128]{4,3,2,1,0:T(8,128)S(1)}, u32[]{:S(2)}, u32[]{:S(2)}) collective-permute-start(f32[4,2,4,8,128]{4,3,2,1,0:T(8,128)S(1)} %get-tuple-element.21), channel_id=1, source_target_pairs={{0,4},{4,8},{8,12},{12,16},{16,20},{20,24},{24,28},{28,32},{32,36}... | collective-permute-start | bytes 393224 | tf_op jit(solution)/shard_map/ppermute | solution.py:525
  8.8 7.2 %copy-start.2 = (s32[128]{0:T(128)S(1)}, s32[128]{0:T(128)}, u32[]{:S(2)}) copy-start(s32[128]{0:T(128)} %code_ref.1) | copy-start | bytes 1540
  8.8 7.2 %collective-permute-start.5 = (f32[4,2,4,8,128]{4,3,2,1,0:T(8,128)S(1)}, f32[4,2,4,8,128]{4,3,2,1,0:T(8,128)S(1)}, u32[]{:S(2)}, u32[]{:S(2)}) collective-permute-start(f32[4,2,4,8,128]{4,3,2,1,0:T(8,128)S(1)} %get-tuple-element.22), channel_id=1, source_target_pairs={{0,252},{4,0},{8,4},{12,8},{16,12},{20,16},{24,20},{28,24},{32,28}... | collective-permute-start | bytes 393224 | tf_op jit(solution)/shard_map/ppermute | solution.py:525
  21.2 1.3 %collective-permute-start.6 = (f32[72,128]{1,0:T(8,128)S(1)}, f32[72,128]{1,0:T(8,128)S(1)}, u32[]{:S(2)}, u32[]{:S(2)}) collective-permute-start(f32[72,128]{1,0:T(8,128)S(1)} %get-tuple-element.24), channel_id=1, source_target_pairs={{0,4},{4,0},{8,12},{12,8},{16,20},{20,16},{24,28},{28,24},{32,36},... | collective-permute-start | bytes 110600 | tf_op jit(solution)/shard_map/ppermute | solution.py:514
  22.5 4.0 %collective-permute-start.7 = (f32[72,128]{1,0:T(8,128)S(1)}, f32[72,128]{1,0:T(8,128)S(1)}, u32[]{:S(2)}, u32[]{:S(2)}) collective-permute-start(f32[72,128]{1,0:T(8,128)S(1)} %add.24), channel_id=1, source_target_pairs={{0,1},{1,0},{2,3},{3,2},{4,5},{5,4},{6,7},{7,6},{8,9},{9,8},{10,11... | collective-permute-start | bytes 110600 | tf_op jit(solution)/shard_map/ppermute | solution.py:514
  26.4 4.0 %collective-permute-start.8 = (f32[72,128]{1,0:T(8,128)S(1)}, f32[72,128]{1,0:T(8,128)S(1)}, u32[]{:S(2)}, u32[]{:S(2)}) collective-permute-start(f32[72,128]{1,0:T(8,128)S(1)} %add.25), channel_id=1, source_target_pairs={{0,64},{4,68},{8,72},{12,76},{16,80},{20,84},{24,88},{28,92},{32,9... | collective-permute-start | bytes 110600 | tf_op jit(solution)/shard_map/ppermute | solution.py:514
  30.4 12.3 %collective-permute-start.9 = (f32[72,128]{1,0:T(8,128)S(1)}, f32[72,128]{1,0:T(8,128)S(1)}, u32[]{:S(2)}, u32[]{:S(2)}) collective-permute-start(f32[72,128]{1,0:T(8,128)S(1)} %add.26), channel_id=1, source_target_pairs={{0,8},{4,12},{8,0},{12,4},{16,24},{20,28},{24,16},{28,20},{32,40},... | collective-permute-start | bytes 110600 | tf_op jit(solution)/shard_map/ppermute | solution.py:514
  42.7 5.2 %collective-permute-start.10 = (f32[72,128]{1,0:T(8,128)S(1)}, f32[72,128]{1,0:T(8,128)S(1)}, u32[]{:S(2)}, u32[]{:S(2)}) collective-permute-start(f32[72,128]{1,0:T(8,128)S(1)} %add.27), channel_id=1, source_target_pairs={{0,3},{1,2},{2,1},{3,0},{4,7},{5,6},{6,5},{7,4},{8,11},{9,10},{10,... | collective-permute-start | bytes 110600 | tf_op jit(solution)/shard_map/ppermute | solution.py:514
  47.9 5.2 %collective-permute-start.11 = (f32[72,128]{1,0:T(8,128)S(1)}, f32[72,128]{1,0:T(8,128)S(1)}, u32[]{:S(2)}, u32[]{:S(2)}) collective-permute-start(f32[72,128]{1,0:T(8,128)S(1)} %add.28), channel_id=1, source_target_pairs={{0,192},{4,196},{8,200},{12,204},{16,208},{20,212},{24,216},{28,22... | collective-permute-start | bytes 110600 | tf_op jit(solution)/shard_map/ppermute | solution.py:514
  53.1 4.0 %collective-permute-start.12 = (f32[72,128]{1,0:T(8,128)S(1)}, f32[72,128]{1,0:T(8,128)S(1)}, u32[]{:S(2)}, u32[]{:S(2)}) collective-permute-start(f32[72,128]{1,0:T(8,128)S(1)} %add.29), channel_id=1, source_target_pairs={{0,56},{4,60},{8,16},{12,20},{16,8},{20,12},{24,32},{28,36},{32,24... | collective-permute-start | bytes 110600 | tf_op jit(solution)/shard_map/ppermute | solution.py:514
  57.1 7.0 %collective-permute-start.13 = (f32[72,128]{1,0:T(8,128)S(1)}, f32[72,128]{1,0:T(8,128)S(1)}, u32[]{:S(2)}, u32[]{:S(2)}) collective-permute-start(f32[72,128]{1,0:T(8,128)S(1)} %add.30), channel_id=1, source_target_pairs={{0,24},{4,28},{8,48},{12,52},{16,40},{20,44},{24,0},{28,4},{32,56}... | collective-permute-start | bytes 110600 | tf_op jit(solution)/shard_map/ppermute | solution.py:514

commit v4 on v3

--- a/solution.py
+++ b/solution.py
@@ -10,6 +10,7 @@
 RANK = 112
 ITERS = 3
 PANEL = 8
+GROUP = 5
 LANES = 128
 SLOT = 16
 
@@ -71,7 +72,7 @@
             for m in range(j + 2, PANEL):
                 a, b = repeat(cols[j], m), repeat(cols[j + 1], m)
                 below[m] = (below[m] - other_one * a) - other_two * b
-            for m in range(PANEL):
+            for m in range(len(other["cols"])):
                 a, b = repeat(below[j], m), repeat(below[j + 1], m)
                 other["cols"][m] = (other["cols"][m] - other_one * a) - other_two * b
             for n, block in enumerate(blocks):
@@ -96,76 +97,79 @@
     both = jnp.concatenate([inner, wide], axis=1)
     matrix = [both[PANEL * k : PANEL * (k + 1)] for k in range(RANK // PANEL)]
     rows = []
-    for k in range(0, len(matrix), 2):
-        upper = [matrix[k][:, :width], matrix[k][:, width:]]
-        lower = [matrix[k + 1][:, :width], matrix[k + 1][:, width:]]
-        cols = [spread(upper[0], PANEL * k + j) for j in range(PANEL)]
-        other = {
-            "below": [spread(lower[0], PANEL * k + j) for j in range(PANEL)],
-            "cols": [spread(lower[0], PANEL * (k + 1) + j) for j in range(PANEL)],
-            "blocks": lower,
-        }
-        upper_pivots, upper_inverses = eliminate(cols, upper, [other])
-        lower_pivots, lower_inverses = eliminate(other["cols"], lower, [])
-        rows += [upper[1] * lax.rsqrt(upper_pivots), lower[1] * lax.rsqrt(lower_pivots)]
-        if k + 2 < len(matrix):
-            scaled = jnp.concatenate(
-                [
-                    jnp.concatenate([block * upper_inverses for block in upper], axis=1),
-                    jnp.concatenate([block * lower_inverses for block in lower], axis=1),
-                ]
+    for k in range(0, len(matrix), GROUP):
+        group = [[part[:, :width], part[:, width:]] for part in matrix[k : k + GROUP]]
+        cols = [spread(group[0][0], PANEL * k + j) for j in range(PANEL)]
+        scaled = []
+        for n, blocks in enumerate(group):
+            at = PANEL * (k + n)
+            others = []
+            for later, other in enumerate(group[n + 1 :]):
+                below = [spread(other[0], at + j) for j in range(PANEL)]
+                ahead = [spread(other[0], at + PANEL + j) for j in range(PANEL)] if later == 0 else []
+                others.append({"below": below, "cols": ahead, "blocks": other})
+            pivots, inverses = eliminate(cols, blocks, others)
+            rows.append(blocks[1] * lax.rsqrt(pivots))
+            scaled.append(jnp.concatenate([block * inverses for block in blocks], axis=1))
+            if others:
+                cols = others[0]["cols"]
+        if k + GROUP < len(matrix):
+            update = outer_sum(
+                jnp.concatenate([blocks[0] for blocks in group]), jnp.concatenate(scaled)
             )
-            update = outer_sum(jnp.concatenate([upper[0], lower[0]]), scaled)
-            for m in range(k + 2, len(matrix)):
+            for m in range(k + GROUP, len(matrix)):
                 matrix[m] = matrix[m] - update[PANEL * m : PANEL * (m + 1)]
     return jnp.concatenate(rows, axis=0)
 
 
-def basis_kernel(total_ref, snap_ref, out_ref, basis_ref, *, rows_all):
+def deep_left(value):
+    high, middle, low = parts_of(value)
+    return jnp.concatenate([high, high, high, middle, middle, low], axis=1).astype(jnp.bfloat16)
+
+
+def deep_right(value, axis):
+    high, middle, low = parts_of(value)
+    return jnp.concatenate([high, middle, low, high, middle, high], axis=axis).astype(jnp.bfloat16)
+
+
+def basis_kernel(total_ref, snap_ref, out_ref, *, rows_all):
     cols = total_ref.shape[1]
     row_id, col_id = ids((cols, cols))
     identity = jnp.where(row_id == col_id, jnp.float32(ridge), 0.0)
     gram_matrix = unfolded(total_ref[...]) / rows_all + identity
 
-    def sweep(step, carry):
-        @pl.when(step == 0)
-        def _():
-            basis_ref[...] = gram_matrix[:RANK, :]
-
-        @pl.when(step > 0)
-        def _():
-            basis_ref[...] = jnp.dot(
-                basis_ref[...], gram_matrix, precision=highest, preferred_element_type=jnp.float32
-            )
-
-        wide = basis_ref[...]
-        full = jnp.concatenate([wide, jnp.zeros((cols - RANK, cols), jnp.float32)], axis=0)
+    gram_deep = deep_right(gram_matrix, 0)
+    basis = gram_matrix[:RANK]
+    for step in range(ITERS):
+        if step > 0:
+            basis = jnp.dot(deep_left(basis), gram_deep, preferred_element_type=jnp.float32)
+        full = jnp.concatenate([basis, jnp.zeros((cols - RANK, cols), jnp.float32)], axis=0)
         inner = lax.dot_general(
-            wide, full, (((1,), (1,)), ((), ())), precision=highest, preferred_element_type=jnp.float32
-        )
-        basis_ref[...] = orthonormal_rows(inner, wide)
-        return carry
-
-    lax.fori_loop(0, ITERS, sweep, 0)
-    basis = basis_ref[...]
-    blocks, cols = out_ref.shape[0] // RANK, basis.shape[1]
-    for block in range(blocks):
-        out_ref[pl.ds(block, RANK, stride=blocks), :] = jnp.dot(
-            basis,
-            snap_ref[pl.ds(block, cols, stride=SLOT), :],
-            precision=highest,
+            deep_left(basis),
+            deep_right(full, 1),
+            (((1,), (1,)), ((), ())),
             preferred_element_type=jnp.float32,
         )
+        basis = orthonormal_rows(inner, basis)
+    blocks = out_ref.shape[0] // RANK
+    basis_deep = deep_left(basis)
+    for block in range(0, blocks, 2):
+        pair = [snap_ref[pl.ds(block + n, cols, stride=SLOT), :] for n in range(2)]
+        modes = jnp.dot(
+            basis_deep,
+            deep_right(jnp.concatenate(pair, axis=1), 0),
+            preferred_element_type=jnp.float32,
+        )
+        for n in range(2):
+            out_ref[pl.ds(block + n, RANK, stride=blocks), :] = modes[:, LANES * n : LANES * (n + 1)]
 
 
 def project(gram_total, snapshots, rows_all):
-    cols = gram_total.shape[1]
     return pl.pallas_call(
         functools.partial(basis_kernel, rows_all=rows_all),
         out_shape=jax.ShapeDtypeStruct((RANK * 12, LANES), jnp.float32),
         in_specs=[pl.BlockSpec(memory_space=pltpu.VMEM)] * 2,
         out_specs=pl.BlockSpec(memory_space=pltpu.VMEM),
-        scratch_shapes=[pltpu.VMEM((RANK, cols), jnp.float32)],
         compiler_params=pltpu.CompilerParams(vmem_limit_bytes=16 * 2**20),
         name="basis",
     )(gram_total, snapshots)
@@ -236,24 +240,26 @@
     )(velocity, smag_coef)
 
 
-def sides_kernel(low_ref, high_ref, sides_ref, up_ref, down_ref):
+def sides_kernel(low_ref, high_ref, sides_ref, chip_ref, other_ref):
+    odd = lax.axis_index("gy") % 2 == 1
     rows_y, layers, size_x = low_ref.shape[1:]
     rows = jnp.concatenate([high_ref[...], low_ref[...]], axis=2).reshape(-1, size_x)
-    done = exact_dot(rows, sorting(size_x, True))
+    done = exact_dot(rows, sorting(size_x, True)).reshape(4, rows_y, 2 * layers, size_x)
     for c in range(4):
-        for y in range(rows_y):
-            start = 2 * layers * (c * rows_y + y)
-            for o in range(4):
-                part = done[start : start + 2 * layers, LANES * o : LANES * (o + 1)]
-                sides_ref[c, y, o] = part
-                near, far = (0, layers + 2), rows_y - 2
-                for ref, away in ((up_ref, rows_y - 1 - y), (down_ref, y)):
+        for o in range(4):
+            planes = [done[c, y, :, LANES * o : LANES * (o + 1)] for y in range(rows_y)]
+            for y in range(rows_y):
+                sides_ref[c, y, o] = planes[y]
+            for away in range(rows_y - 1):
+                upper, lower = planes[rows_y - 1 - away], planes[away]
+                on_chip, off_chip = jnp.where(odd, lower, upper), jnp.where(odd, upper, lower)
+                for ref, plane in ((chip_ref, on_chip), (other_ref, off_chip)):
                     if away == 0:
-                        ref[c, 0, o] = part
-                    elif away <= far:
-                        for side, begin in enumerate(near):
+                        ref[c, 0, o] = plane
+                    else:
+                        for side, begin in enumerate((0, layers + 2)):
                             to = 4 * (away - 1) + 2 * side
-                            ref[c, 1, o, to : to + 2] = part[begin : begin + 2]
+                            ref[c, 1, o, to : to + 2] = plane[begin : begin + 2]
 
 
 def sort_sides(low, high):
@@ -344,34 +350,41 @@
 
 
 def steps_kernel(
-    code_ref, block_ref, before_ref, after_ref, sides_ref, side_before_ref, side_after_ref,
+    code_ref, block_ref, chip_ref, other_ref, sides_ref, side_chip_ref, side_other_ref,
     wide_ref, snap_ref, gram_ref,
     cells_ref, visc_ref, one_ref, two_ref, all_ref,
 ):
     _, rows_y, _, rows_z, _ = block_ref.shape
     cols = gram_ref.shape[1]
     place_y = lax.axis_index("gy")
-    first, last = place_y == 0, place_y == lax.axis_size("gy") - 1
+    first, last, odd = place_y == 0, place_y == lax.axis_size("gy") - 1, place_y % 2 == 1
+
+    def behind(chip, other):
+        return jnp.where(first, 0.0, jnp.where(odd, chip, other))
+
+    def ahead(chip, other):
+        return jnp.where(last, 0.0, jnp.where(odd, other, chip))
+
     for c in range(4):
         for y in range(rows_y):
             for o in range(4):
                 cells_ref[c, rows_y + y, o, :rows_z] = block_ref[c, y, o]
-                halo = jnp.where(first, 0.0, before_ref[c, y, o])
-                cells_ref[c, y, o, :rows_z] = halo
-                halo = jnp.where(last, 0.0, after_ref[c, y, o])
-                cells_ref[c, 2 * rows_y + y, o, :rows_z] = halo
+                chip, other = chip_ref[c, y, o], other_ref[c, y, o]
+                cells_ref[c, y, o, :rows_z] = behind(chip, other)
+                cells_ref[c, 2 * rows_y + y, o, :rows_z] = ahead(chip, other)
                 side = (slice(rows_z, rows_z + sides_ref.shape[3]),)
                 cells_ref[(c, rows_y + y, o, *side)] = sides_ref[c, y, o]
-                for ref, wall, at, away in (
-                    (side_before_ref, first, y, rows_y - 1 - y),
-                    (side_after_ref, last, 2 * rows_y + y, y),
+                for choose, at, away in (
+                    (behind, y, rows_y - 1 - y),
+                    (ahead, 2 * rows_y + y, y),
                 ):
                     if away == 0:
-                        cells_ref[(c, at, o, *side)] = jnp.where(wall, 0.0, ref[c, 0, o])
+                        halo = choose(side_chip_ref[c, 0, o], side_other_ref[c, 0, o])
+                        cells_ref[(c, at, o, *side)] = halo
                     elif away <= rows_y - 2:
                         for n, begin in enumerate((rows_z, rows_z + sides_ref.shape[3] - 2)):
-                            to = 4 * (away - 1) + 2 * n
-                            halo = jnp.where(wall, 0.0, ref[c, 1, o, to : to + 2])
+                            part = (c, 1, o, slice(4 * (away - 1) + 2 * n, 4 * (away - 1) + 2 * n + 2))
+                            halo = choose(side_chip_ref[part], side_other_ref[part])
                             cells_ref[c, at, o, begin : begin + 2] = halo
 
     @pl.when(first)
@@ -424,13 +437,13 @@
                         piece = ref[c, shift + y, o, pl.ds(z, rows_z // 4, stride=4), :]
                         all_ref[start + 4 * c : start + 4 * c + 4, :] = piece
 
-    def choose(column, carry):
+    def pick(column, carry):
         source = pl.multiple_of(code_ref[column] * SLOT, SLOT)
         target = pl.multiple_of(column * SLOT, SLOT)
         snap_ref[pl.ds(target, SLOT), :] = all_ref[pl.ds(source, SLOT), :]
         return carry
 
-    lax.fori_loop(0, cols, choose, 0, unroll=16)
+    lax.fori_loop(0, cols, pick, 0, unroll=16)
     even, odd = jnp.zeros((cols, cols), jnp.float32), jnp.zeros((cols, cols), jnp.float32)
     across = functools.partial(
         lax.dot_general,
@@ -521,17 +534,19 @@
     def along_z(part, step):
         return lax.ppermute(part, "gz", [(i, (i + step) % count_z) for i in range(count_z)])
 
-    def along_y(part, step):
-        return lax.ppermute(part, "gy", [(i, (i + step) % count_y) for i in range(count_y)])
+    def on_chip(part):
+        return lax.ppermute(part, "gy", [(i, i ^ 1) for i in range(count_y)])
+
+    def off_chip(part):
+        partners = [min(max(((i + 1) ^ 1) - 1, 0), count_y - 1) for i in range(count_y)]
+        return lax.ppermute(part, "gy", list(enumerate(partners)))
 
     low, high = edges(velocity, smag_coef)
     velocity, smag_coef, low, high = lax.optimization_barrier((velocity, smag_coef, low, high))
-    sides, up, down = sort_sides(along_z(high, 1), along_z(low, -1))
-    side_before, side_after = along_y(up, 1), along_y(down, -1)
+    sides, side_chip, side_other = sort_sides(along_z(high, 1), along_z(low, -1))
     block = pack(velocity, smag_coef)
-    before, after = along_y(block, 1), along_y(block, -1)
     wide, snapshots, gram = both_steps(
-        snap_code, block, before, after, sides, side_before, side_after
+        snap_code, block, on_chip(block), off_chip(block), sides, on_chip(side_chip), off_chip(side_other)
     )
     rows_y, rows_z = velocity.shape[1], velocity.shape[2]
     rows_all = 12 * LANES * count_y * count_z

time: 76.1 us -> 71 us (0.933)
  the two profiles are of different devices: /device:TPU:32 before, /device:TPU:24 now
where the time goes in v4:
time: 71 us; the launch traced here: 70.9 us
  waiting for transfers between devices  33.2 us (47%)
  starting transfers between devices  19.4 us (27%)
  Pallas kernels  17.5 us (25%)
  between operations  0.76 us (1%)
    ppermute x8, waiting for transfers between devices, device_sum(): lax.ppermute(part, axis, [(i, partner(i)) for i in range(count)])  28 us
    ppermute x2, starting transfers between devices, off_chip(): return lax.ppermute(part, 'gy', list(enumerate(partners)))  10.1 us
    pallas_call x1, Pallas kernels, project(): pl.pallas_call(functools.partial(basis_kernel, rows_all=rows_all), out_sh...  8.91 us
    ppermute x8, starting transfers between devices, device_sum(): lax.ppermute(part, axis, [(i, partner(i)) for i in range(count)])  5.27 us
    ppermute x2, waiting for transfers between devices, off_chip(): return lax.ppermute(part, 'gy', list(enumerate(partners)))  5.2 us
    pallas_call x1, Pallas kernels, both_steps(): pl.pallas_call(steps_kernel, out_shape=(f32(3 * rows_y * rows_z, 4 * LANE...  5.15 us
    ppermute x2, starting transfers between devices, along_z(): lax.ppermute(part, 'gz', [(i, (i + step) % count_z) for i in range(count_...  3.31 us
  transfers between devices with their start and end apart: 14, of which 9 were waited for; matrix products, arithmetic and copies ran while one was open for 0% of the time, Pallas kernels for 3%

profile of v4, /device:TPU:24, one launch (start us, length us, event | category | flops | bytes accessed | tf_op | source)
XLA Modules:
  0.0 70.9 jit_solution(1858294829416821521)
XLA Ops:
  0.6 1.1 %edges.1 = (f32[4,4,4,512]{3,2,1,0:T(4,128)S(1)}, f32[4,4,4,512]{3,2,1,0:T(4,128)S(1)}) custom-call(f32[3,4,16,512]{3,2,1,0:T(8,128)} %velocity_ref.2, f32[4,16,512]{2,1,0:T(8,128)} %coef_ref.2), custom_call_target="tpu_custom_call" | custom-call | tf_op jit(solution)/shard_map/edges/pallas_call | solution.py:209
  1.7 1.6 %collective-permute-start.2 = (f32[4,4,4,512]{3,2,1,0:T(4,128)S(1)}, f32[4,4,4,512]{3,2,1,0:T(4,128)S(1)}, u32[]{:S(2)}, u32[]{:S(2)}) collective-permute-start(f32[4,4,4,512]{3,2,1,0:T(4,128)S(1)} %get-tuple-element.18), channel_id=1, source_target_pairs={{0,1},{1,2},{2,3},{3,0},{4,5},{5,6},{6,7},{7,4},{8,9},{9,10},{10,1... | collective-permute-start | bytes 393224 | tf_op jit(solution)/shard_map/ppermute | solution.py:535
  3.3 1.7 %collective-permute-start.3 = (f32[4,4,4,512]{3,2,1,0:T(4,128)S(1)}, f32[4,4,4,512]{3,2,1,0:T(4,128)S(1)}, u32[]{:S(2)}, u32[]{:S(2)}) collective-permute-start(f32[4,4,4,512]{3,2,1,0:T(4,128)S(1)} %get-tuple-element.19), channel_id=1, source_target_pairs={{0,3},{1,0},{2,1},{3,2},{4,7},{5,4},{6,5},{7,6},{8,11},{9,8},{10,9... | collective-permute-start | bytes 393224 | tf_op jit(solution)/shard_map/ppermute | solution.py:535
  5.0 0.6 pack.1.block_ref
  5.7 6.8 %collective-permute-start.1 = (f32[4,4,4,16,128]{4,3,2,1,0:T(8,128)S(1)}, f32[4,4,4,16,128]{4,3,2,1,0:T(8,128)S(1)}, u32[]{:S(2)}, u32[]{:S(2)}) collective-permute-start(f32[4,4,4,16,128]{4,3,2,1,0:T(8,128)S(1)} %pack.1.block_ref), channel_id=1, source_target_pairs={{0,0},{4,8},{8,4},{12,16},{16,12},{20,24},{24,20},{28,32},{32,28},... | collective-permute-start | bytes 1572872 | tf_op jit(solution)/shard_map/ppermute | solution.py:542
  12.6 0.5 sides.1
  13.1 0.6 collective-permute-start.4
  13.7 3.3 %collective-permute-start.5 = (f32[4,2,4,8,128]{4,3,2,1,0:T(8,128)S(1)}, f32[4,2,4,8,128]{4,3,2,1,0:T(8,128)S(1)}, u32[]{:S(2)}, u32[]{:S(2)}) collective-permute-start(f32[4,2,4,8,128]{4,3,2,1,0:T(8,128)S(1)} %get-tuple-element.22), channel_id=1, source_target_pairs={{0,0},{4,8},{8,4},{12,16},{16,12},{20,24},{24,20},{28,32},{32,28},... | collective-permute-start | bytes 393224 | tf_op jit(solution)/shard_map/ppermute | solution.py:542
  17.0 5.2 %collective-permute-done.5.side_other_ref = f32[4,2,4,8,128]{4,3,2,1,0:T(8,128)S(1)} collective-permute-done((f32[4,2,4,8,128]{4,3,2,1,0:T(8,128)S(1)}, f32[4,2,4,8,128]{4,3,2,1,0:T(8,128)S(1)}, u32[]{:S(2)}, u32[]{:S(2)}) %collective-permute-start.5) | collective-permute-done | bytes 131104 | tf_op jit(solution)/shard_map/ppermute | solution.py:542
  22.2 5.1 %steps.1 = (f32[192,512]{1,0:T(8,128)S(1)}, f32[2048,128]{1,0:T(8,128)S(1)}, f32[72,128]{1,0:T(8,128)S(1)}) custom-call(s32[128]{0:T(128)S(1)} %copy-done.2, f32[4,4,4,16,128]{4,3,2,1,0:T(8,128)S(1)} %pack.1.block_ref, f32[4,4,4,16,128]{4,3,2,1,0:T(8,128)S(1)} %collective-permute-done.chip_ref, f32[4,4,4,16,128]{4,3,2,1,0:T(8,128)S(1)} %collective-permute-done.1.other_ref, ...), custom_call_target="tpu_custom_call" | custom-call | tf_op jit(solution)/shard_map/steps/pallas_call | solution.py:485
  27.5 1.2 %collective-permute-done.6 = f32[72,128]{1,0:T(8,128)S(1)} collective-permute-done((f32[72,128]{1,0:T(8,128)S(1)}, f32[72,128]{1,0:T(8,128)S(1)}, u32[]{:S(2)}, u32[]{:S(2)}) %collective-permute-start.6) | collective-permute-done | bytes 36896 | tf_op jit(solution)/shard_map/ppermute | solution.py:527
  29.0 3.7 %collective-permute-done.7 = f32[72,128]{1,0:T(8,128)S(1)} collective-permute-done((f32[72,128]{1,0:T(8,128)S(1)}, f32[72,128]{1,0:T(8,128)S(1)}, u32[]{:S(2)}, u32[]{:S(2)}) %collective-permute-start.7) | collective-permute-done | bytes 36896 | tf_op jit(solution)/shard_map/ppermute | solution.py:527
  32.7 0.4 collective-permute-start.8
  33.1 3.5 %collective-permute-done.8 = f32[72,128]{1,0:T(8,128)S(1)} collective-permute-done((f32[72,128]{1,0:T(8,128)S(1)}, f32[72,128]{1,0:T(8,128)S(1)}, u32[]{:S(2)}, u32[]{:S(2)}) %collective-permute-start.8) | collective-permute-done | bytes 36896 | tf_op jit(solution)/shard_map/ppermute | solution.py:527
  36.6 3.9 %collective-permute-done.9 = f32[72,128]{1,0:T(8,128)S(1)} collective-permute-done((f32[72,128]{1,0:T(8,128)S(1)}, f32[72,128]{1,0:T(8,128)S(1)}, u32[]{:S(2)}, u32[]{:S(2)}) %collective-permute-start.9) | collective-permute-done | bytes 36896 | tf_op jit(solution)/shard_map/ppermute | solution.py:527
  40.6 1.5 %collective-permute-start.10 = (f32[72,128]{1,0:T(8,128)S(1)}, f32[72,128]{1,0:T(8,128)S(1)}, u32[]{:S(2)}, u32[]{:S(2)}) collective-permute-start(f32[72,128]{1,0:T(8,128)S(1)} %add.27), channel_id=1, source_target_pairs={{0,3},{1,2},{2,1},{3,0},{4,7},{5,6},{6,5},{7,4},{8,11},{9,10},{10,... | collective-permute-start | bytes 110600 | tf_op jit(solution)/shard_map/ppermute | solution.py:527
  42.1 3.6 %collective-permute-done.10 = f32[72,128]{1,0:T(8,128)S(1)} collective-permute-done((f32[72,128]{1,0:T(8,128)S(1)}, f32[72,128]{1,0:T(8,128)S(1)}, u32[]{:S(2)}, u32[]{:S(2)}) %collective-permute-start.10) | collective-permute-done | bytes 36896 | tf_op jit(solution)/shard_map/ppermute | solution.py:527
  45.8 5.2 %collective-permute-done.11 = f32[72,128]{1,0:T(8,128)S(1)} collective-permute-done((f32[72,128]{1,0:T(8,128)S(1)}, f32[72,128]{1,0:T(8,128)S(1)}, u32[]{:S(2)}, u32[]{:S(2)}) %collective-permute-start.11) | collective-permute-done | bytes 36896 | tf_op jit(solution)/shard_map/ppermute | solution.py:527
  50.9 1.2 %collective-permute-start.12 = (f32[72,128]{1,0:T(8,128)S(1)}, f32[72,128]{1,0:T(8,128)S(1)}, u32[]{:S(2)}, u32[]{:S(2)}) collective-permute-start(f32[72,128]{1,0:T(8,128)S(1)} %add.29), channel_id=1, source_target_pairs={{0,56},{4,60},{8,16},{12,20},{16,8},{20,12},{24,32},{28,36},{32,24... | collective-permute-start | bytes 110600 | tf_op jit(solution)/shard_map/ppermute | solution.py:527
  52.2 3.9 %collective-permute-done.12 = f32[72,128]{1,0:T(8,128)S(1)} collective-permute-done((f32[72,128]{1,0:T(8,128)S(1)}, f32[72,128]{1,0:T(8,128)S(1)}, u32[]{:S(2)}, u32[]{:S(2)}) %collective-permute-start.12) | collective-permute-done | bytes 36896 | tf_op jit(solution)/shard_map/ppermute | solution.py:527
  56.1 1.7 %collective-permute-start.13 = (f32[72,128]{1,0:T(8,128)S(1)}, f32[72,128]{1,0:T(8,128)S(1)}, u32[]{:S(2)}, u32[]{:S(2)}) collective-permute-start(f32[72,128]{1,0:T(8,128)S(1)} %add.30), channel_id=1, source_target_pairs={{0,24},{4,28},{8,48},{12,52},{16,40},{20,44},{24,0},{28,4},{32,56}... | collective-permute-start | bytes 110600 | tf_op jit(solution)/shard_map/ppermute | solution.py:527
  57.8 1.3 %unsort.1 = f32[3,4,16,512]{3,2,1,0:T(8,128)} custom-call(f32[192,512]{1,0:T(8,128)S(1)} %get-tuple-element.23.wide_ref), custom_call_target="tpu_custom_call" | custom-call | flops 4000000000 | bytes 1000000 | tf_op jit(solution)/shard_map/unsort/pallas_call | solution.py:468
  59.1 2.9 %collective-permute-done.13 = f32[72,128]{1,0:T(8,128)S(1)} collective-permute-done((f32[72,128]{1,0:T(8,128)S(1)}, f32[72,128]{1,0:T(8,128)S(1)}, u32[]{:S(2)}, u32[]{:S(2)}) %collective-permute-start.13) | collective-permute-done | bytes 36896 | tf_op jit(solution)/shard_map/ppermute | solution.py:527
  62.0 8.9 %basis.1 = f32[1344,128]{1,0:T(8,128)} custom-call(f32[72,128]{1,0:T(8,128)S(1)} %add.31.total_ref, f32[2048,128]{1,0:T(8,128)S(1)} %get-tuple-element.25.snap_ref), custom_call_target="tpu_custom_call" | custom-call | tf_op jit(solution)/shard_map/basis/pallas_call | solution.py:168
  (24 shorter events, 0.5 us)
Async XLA Ops:
  0.6 4.4 %copy-start.1 = (f32[4,16,512]{2,1,0:T(8,128)S(1)}, f32[4,16,512]{2,1,0:T(8,128)}, u32[]{:S(2)}) copy-start(f32[4,16,512]{2,1,0:T(8,128)} %coef_ref.2) | copy-start | bytes 393220
  0.6 4.4 %copy-start = (f32[3,4,16,512]{3,2,1,0:T(8,128)S(1)}, f32[3,4,16,512]{3,2,1,0:T(8,128)}, u32[]{:S(2)}) copy-start(f32[3,4,16,512]{3,2,1,0:T(8,128)} %velocity_ref.2) | copy-start | bytes 1179652
  1.7 10.9 %collective-permute-start.2 = (f32[4,4,4,512]{3,2,1,0:T(4,128)S(1)}, f32[4,4,4,512]{3,2,1,0:T(4,128)S(1)}, u32[]{:S(2)}, u32[]{:S(2)}) collective-permute-start(f32[4,4,4,512]{3,2,1,0:T(4,128)S(1)} %get-tuple-element.18), channel_id=1, source_target_pairs={{0,1},{1,2},{2,3},{3,0},{4,5},{5,6},{6,7},{7,4},{8,9},{9,10},{10,1... | collective-permute-start | bytes 393224 | tf_op jit(solution)/shard_map/ppermute | solution.py:535
  3.3 9.4 %collective-permute-start.3 = (f32[4,4,4,512]{3,2,1,0:T(4,128)S(1)}, f32[4,4,4,512]{3,2,1,0:T(4,128)S(1)}, u32[]{:S(2)}, u32[]{:S(2)}) collective-permute-start(f32[4,4,4,512]{3,2,1,0:T(4,128)S(1)} %get-tuple-element.19), channel_id=1, source_target_pairs={{0,3},{1,0},{2,1},{3,2},{4,7},{5,4},{6,5},{7,6},{8,11},{9,8},{10,9... | collective-permute-start | bytes 393224 | tf_op jit(solution)/shard_map/ppermute | solution.py:535
  5.7 16.6 %collective-permute-start.1 = (f32[4,4,4,16,128]{4,3,2,1,0:T(8,128)S(1)}, f32[4,4,4,16,128]{4,3,2,1,0:T(8,128)S(1)}, u32[]{:S(2)}, u32[]{:S(2)}) collective-permute-start(f32[4,4,4,16,128]{4,3,2,1,0:T(8,128)S(1)} %pack.1.block_ref), channel_id=1, source_target_pairs={{0,0},{4,8},{8,4},{12,16},{16,12},{20,24},{24,20},{28,32},{32,28},... | collective-permute-start | bytes 1572872 | tf_op jit(solution)/shard_map/ppermute | solution.py:542
  12.5 9.7 %collective-permute-start = (f32[4,4,4,16,128]{4,3,2,1,0:T(8,128)S(1)}, f32[4,4,4,16,128]{4,3,2,1,0:T(8,128)S(1)}, u32[]{:S(2)}, u32[]{:S(2)}) collective-permute-start(f32[4,4,4,16,128]{4,3,2,1,0:T(8,128)S(1)} %pack.1.block_ref), channel_id=1, source_target_pairs={{0,4},{4,0},{8,12},{12,8},{16,20},{20,16},{24,28},{28,24},{32,36},... | collective-permute-start | bytes 1572872 | tf_op jit(solution)/shard_map/ppermute | solution.py:538
  13.1 3.9 %collective-permute-start.4 = (f32[4,2,4,8,128]{4,3,2,1,0:T(8,128)S(1)}, f32[4,2,4,8,128]{4,3,2,1,0:T(8,128)S(1)}, u32[]{:S(2)}, u32[]{:S(2)}) collective-permute-start(f32[4,2,4,8,128]{4,3,2,1,0:T(8,128)S(1)} %get-tuple-element.21), channel_id=1, source_target_pairs={{0,4},{4,0},{8,12},{12,8},{16,20},{20,16},{24,28},{28,24},{32,36},... | collective-permute-start | bytes 393224 | tf_op jit(solution)/shard_map/ppermute | solution.py:538
  13.7 8.5 %copy-start.2 = (s32[128]{0:T(128)S(1)}, s32[128]{0:T(128)}, u32[]{:S(2)}) copy-start(s32[128]{0:T(128)} %code_ref.1) | copy-start | bytes 1540
  13.7 8.5 %collective-permute-start.5 = (f32[4,2,4,8,128]{4,3,2,1,0:T(8,128)S(1)}, f32[4,2,4,8,128]{4,3,2,1,0:T(8,128)S(1)}, u32[]{:S(2)}, u32[]{:S(2)}) collective-permute-start(f32[4,2,4,8,128]{4,3,2,1,0:T(8,128)S(1)} %get-tuple-element.22), channel_id=1, source_target_pairs={{0,0},{4,8},{8,4},{12,16},{16,12},{20,24},{24,20},{28,32},{32,28},... | collective-permute-start | bytes 393224 | tf_op jit(solution)/shard_map/ppermute | solution.py:542
  27.4 1.3 %collective-permute-start.6 = (f32[72,128]{1,0:T(8,128)S(1)}, f32[72,128]{1,0:T(8,128)S(1)}, u32[]{:S(2)}, u32[]{:S(2)}) collective-permute-start(f32[72,128]{1,0:T(8,128)S(1)} %get-tuple-element.24), channel_id=1, source_target_pairs={{0,4},{4,0},{8,12},{12,8},{16,20},{20,16},{24,28},{28,24},{32,36},... | collective-permute-start | bytes 110600 | tf_op jit(solution)/shard_map/ppermute | solution.py:527
  28.7 4.0 %collective-permute-start.7 = (f32[72,128]{1,0:T(8,128)S(1)}, f32[72,128]{1,0:T(8,128)S(1)}, u32[]{:S(2)}, u32[]{:S(2)}) collective-permute-start(f32[72,128]{1,0:T(8,128)S(1)} %add.24), channel_id=1, source_target_pairs={{0,1},{1,0},{2,3},{3,2},{4,5},{5,4},{6,7},{7,6},{8,9},{9,8},{10,11... | collective-permute-start | bytes 110600 | tf_op jit(solution)/shard_map/ppermute | solution.py:527
  32.7 4.0 %collective-permute-start.8 = (f32[72,128]{1,0:T(8,128)S(1)}, f32[72,128]{1,0:T(8,128)S(1)}, u32[]{:S(2)}, u32[]{:S(2)}) collective-permute-start(f32[72,128]{1,0:T(8,128)S(1)} %add.25), channel_id=1, source_target_pairs={{0,64},{4,68},{8,72},{12,76},{16,80},{20,84},{24,88},{28,92},{32,9... | collective-permute-start | bytes 110600 | tf_op jit(solution)/shard_map/ppermute | solution.py:527
  36.6 4.0 %collective-permute-start.9 = (f32[72,128]{1,0:T(8,128)S(1)}, f32[72,128]{1,0:T(8,128)S(1)}, u32[]{:S(2)}, u32[]{:S(2)}) collective-permute-start(f32[72,128]{1,0:T(8,128)S(1)} %add.26), channel_id=1, source_target_pairs={{0,8},{4,12},{8,0},{12,4},{16,24},{20,28},{24,16},{28,20},{32,40},... | collective-permute-start | bytes 110600 | tf_op jit(solution)/shard_map/ppermute | solution.py:527
  40.6 5.2 %collective-permute-start.10 = (f32[72,128]{1,0:T(8,128)S(1)}, f32[72,128]{1,0:T(8,128)S(1)}, u32[]{:S(2)}, u32[]{:S(2)}) collective-permute-start(f32[72,128]{1,0:T(8,128)S(1)} %add.27), channel_id=1, source_target_pairs={{0,3},{1,2},{2,1},{3,0},{4,7},{5,6},{6,5},{7,4},{8,11},{9,10},{10,... | collective-permute-start | bytes 110600 | tf_op jit(solution)/shard_map/ppermute | solution.py:527
  45.8 5.2 %collective-permute-start.11 = (f32[72,128]{1,0:T(8,128)S(1)}, f32[72,128]{1,0:T(8,128)S(1)}, u32[]{:S(2)}, u32[]{:S(2)}) collective-permute-start(f32[72,128]{1,0:T(8,128)S(1)} %add.28), channel_id=1, source_target_pairs={{0,192},{4,196},{8,200},{12,204},{16,208},{20,212},{24,216},{28,22... | collective-permute-start | bytes 110600 | tf_op jit(solution)/shard_map/ppermute | solution.py:527
  50.9 5.2 %collective-permute-start.12 = (f32[72,128]{1,0:T(8,128)S(1)}, f32[72,128]{1,0:T(8,128)S(1)}, u32[]{:S(2)}, u32[]{:S(2)}) collective-permute-start(f32[72,128]{1,0:T(8,128)S(1)} %add.29), channel_id=1, source_target_pairs={{0,56},{4,60},{8,16},{12,20},{16,8},{20,12},{24,32},{28,36},{32,24... | collective-permute-start | bytes 110600 | tf_op jit(solution)/shard_map/ppermute | solution.py:527
  56.1 5.8 %collective-permute-start.13 = (f32[72,128]{1,0:T(8,128)S(1)}, f32[72,128]{1,0:T(8,128)S(1)}, u32[]{:S(2)}, u32[]{:S(2)}) collective-permute-start(f32[72,128]{1,0:T(8,128)S(1)} %add.30), channel_id=1, source_target_pairs={{0,24},{4,28},{8,48},{12,52},{16,40},{20,44},{24,0},{28,4},{32,56}... | collective-permute-start | bytes 110600 | tf_op jit(solution)/shard_map/ppermute | solution.py:527

commit v5 on v4

--- a/solution.py
+++ b/solution.py
@@ -505,26 +505,33 @@
 
 
 def device_sum(part):
-    ring = 8
-    swaps = (lambda z: z ^ 1, lambda z: ((z + 1) ^ 1) - 1, lambda z: 7 - z if z % 4 in (1, 2) else z ^ 3)
-
-    def along_z(swap):
-        return lambda i: i - i // 2 % ring * 2 + swap(i // 2 % ring) % ring * 2
-
-    flip = lambda bits: lambda i: i ^ bits
-    steps = [
-        ("gy", flip(1)),
-        ("gz", flip(1)),
-        ("gy", flip(16)),
-        ("gy", along_z(swaps[0])),
-        ("gz", flip(3)),
-        ("gy", flip(48)),
-        ("gy", along_z(swaps[1])),
-        ("gy", along_z(swaps[2])),
-    ]
-    for axis, partner in steps:
-        count = lax.axis_size(axis)
-        part = part + lax.ppermute(part, axis, [(i, partner(i)) for i in range(count)])
+    axes = ("gy", "gz")
+    size_z, size_x = 8, lax.axis_size("gz")
+    moves = {
+        "core": lambda x, y, z, core: (x, y, z, core ^ 1),
+        "x1": lambda x, y, z, core: (x ^ 1, y, z, core),
+        "x3": lambda x, y, z, core: (x ^ 3, y, z, core),
+        "y1": lambda x, y, z, core: (x, y ^ 1, z, core),
+        "y3": lambda x, y, z, core: (x, y ^ 3, z, core),
+        "za": lambda x, y, z, core: (x, y, z ^ 1, core),
+        "zb": lambda x, y, z, core: (x, y, (((z + 1) ^ 1) - 1) % size_z, core),
+        "zc": lambda x, y, z, core: (x, y, size_z - 1 - z if z % 4 in (1, 2) else z ^ 3, core),
+    }
+    orders = (
+        ("core", "x1", "za", "y1", "zb", "x3", "zc", "y3"),
+        ("core", "za", "x1", "zb", "y1", "zc", "y3", "x3"),
+    )
+
+    def partner(step, device):
+        row, x = divmod(device, size_x)
+        core, z, y = row % 2, row // 2 % size_z, row // (2 * size_z)
+        x, y, z, core = moves[orders[core][step]](x, y, z, core)
+        return ((y * size_z + z) * 2 + core) * size_x + x
+
+    count = lax.axis_size("gy") * size_x
+    for step in range(len(moves)):
+        pairs = [(device, partner(step, device)) for device in range(count)]
+        part = part + lax.ppermute(part, axes, pairs)
     return part
 
 

time: 71 us -> 71.2 us (level)
  no operation moved by 1% of the time
where the time goes in v5:
time: 71.2 us; the launch traced here: 71.1 us
  waiting for transfers between devices  33.5 us (47%)
  starting transfers between devices  19.2 us (27%)
  Pallas kernels  17.5 us (25%)
  between operations  0.76 us (1%)
    ppermute x8, waiting for transfers between devices, device_sum(): part = part + lax.ppermute(part, axes, pairs)  28.3 us
    ppermute x2, starting transfers between devices, off_chip(): return lax.ppermute(part, 'gy', list(enumerate(partners)))  10.1 us
    pallas_call x1, Pallas kernels, project(): pl.pallas_call(functools.partial(basis_kernel, rows_all=rows_all), out_sh...  8.91 us
    ppermute x2, waiting for transfers between devices, off_chip(): return lax.ppermute(part, 'gy', list(enumerate(partners)))  5.2 us
    pallas_call x1, Pallas kernels, both_steps(): pl.pallas_call(steps_kernel, out_shape=(f32(3 * rows_y * rows_z, 4 * LANE...  5.15 us
    ppermute x8, starting transfers between devices, device_sum(): part = part + lax.ppermute(part, axes, pairs)  5.12 us
    ppermute x2, starting transfers between devices, along_z(): lax.ppermute(part, 'gz', [(i, (i + step) % count_z) for i in range(count_...  3.31 us
  transfers between devices with their start and end apart: 14, of which 9 were waited for; matrix products, arithmetic and copies ran while one was open for 0% of the time, Pallas kernels for 3%

profile of v5, /device:TPU:24, one launch (start us, length us, event | category | flops | bytes accessed | tf_op | source)
XLA Modules:
  0.0 71.1 jit_solution(8650056354792638089)
XLA Ops:
  0.6 1.1 %edges.1 = (f32[4,4,4,512]{3,2,1,0:T(4,128)S(1)}, f32[4,4,4,512]{3,2,1,0:T(4,128)S(1)}) custom-call(f32[3,4,16,512]{3,2,1,0:T(8,128)} %velocity_ref.2, f32[4,16,512]{2,1,0:T(8,128)} %coef_ref.2), custom_call_target="tpu_custom_call" | custom-call | tf_op jit(solution)/shard_map/edges/pallas_call | solution.py:209
  1.7 1.6 %collective-permute-start.2 = (f32[4,4,4,512]{3,2,1,0:T(4,128)S(1)}, f32[4,4,4,512]{3,2,1,0:T(4,128)S(1)}, u32[]{:S(2)}, u32[]{:S(2)}) collective-permute-start(f32[4,4,4,512]{3,2,1,0:T(4,128)S(1)} %get-tuple-element.18), channel_id=1, source_target_pairs={{0,1},{1,2},{2,3},{3,0},{4,5},{5,6},{6,7},{7,4},{8,9},{9,10},{10,1... | collective-permute-start | bytes 393224 | tf_op jit(solution)/shard_map/ppermute | solution.py:542
  3.3 1.7 %collective-permute-start.3 = (f32[4,4,4,512]{3,2,1,0:T(4,128)S(1)}, f32[4,4,4,512]{3,2,1,0:T(4,128)S(1)}, u32[]{:S(2)}, u32[]{:S(2)}) collective-permute-start(f32[4,4,4,512]{3,2,1,0:T(4,128)S(1)} %get-tuple-element.19), channel_id=1, source_target_pairs={{0,3},{1,0},{2,1},{3,2},{4,7},{5,4},{6,5},{7,6},{8,11},{9,8},{10,9... | collective-permute-start | bytes 393224 | tf_op jit(solution)/shard_map/ppermute | solution.py:542
  5.0 0.6 pack.1.block_ref
  5.7 6.8 %collective-permute-start.1 = (f32[4,4,4,16,128]{4,3,2,1,0:T(8,128)S(1)}, f32[4,4,4,16,128]{4,3,2,1,0:T(8,128)S(1)}, u32[]{:S(2)}, u32[]{:S(2)}) collective-permute-start(f32[4,4,4,16,128]{4,3,2,1,0:T(8,128)S(1)} %pack.1.block_ref), channel_id=1, source_target_pairs={{0,0},{4,8},{8,4},{12,16},{16,12},{20,24},{24,20},{28,32},{32,28},... | collective-permute-start | bytes 1572872 | tf_op jit(solution)/shard_map/ppermute | solution.py:549
  12.6 0.5 sides.1
  13.1 0.6 collective-permute-start.4
  13.7 3.3 %collective-permute-start.5 = (f32[4,2,4,8,128]{4,3,2,1,0:T(8,128)S(1)}, f32[4,2,4,8,128]{4,3,2,1,0:T(8,128)S(1)}, u32[]{:S(2)}, u32[]{:S(2)}) collective-permute-start(f32[4,2,4,8,128]{4,3,2,1,0:T(8,128)S(1)} %get-tuple-element.22), channel_id=1, source_target_pairs={{0,0},{4,8},{8,4},{12,16},{16,12},{20,24},{24,20},{28,32},{32,28},... | collective-permute-start | bytes 393224 | tf_op jit(solution)/shard_map/ppermute | solution.py:549
  17.0 5.2 %collective-permute-done.5.side_other_ref = f32[4,2,4,8,128]{4,3,2,1,0:T(8,128)S(1)} collective-permute-done((f32[4,2,4,8,128]{4,3,2,1,0:T(8,128)S(1)}, f32[4,2,4,8,128]{4,3,2,1,0:T(8,128)S(1)}, u32[]{:S(2)}, u32[]{:S(2)}) %collective-permute-start.5) | collective-permute-done | bytes 131104 | tf_op jit(solution)/shard_map/ppermute | solution.py:549
  22.2 5.1 %steps.1 = (f32[192,512]{1,0:T(8,128)S(1)}, f32[2048,128]{1,0:T(8,128)S(1)}, f32[72,128]{1,0:T(8,128)S(1)}) custom-call(s32[128]{0:T(128)S(1)} %copy-done.2, f32[4,4,4,16,128]{4,3,2,1,0:T(8,128)S(1)} %pack.1.block_ref, f32[4,4,4,16,128]{4,3,2,1,0:T(8,128)S(1)} %collective-permute-done.chip_ref, f32[4,4,4,16,128]{4,3,2,1,0:T(8,128)S(1)} %collective-permute-done.1.other_ref, ...), custom_call_target="tpu_custom_call" | custom-call | tf_op jit(solution)/shard_map/steps/pallas_call | solution.py:485
  27.5 1.2 %collective-permute-done.6 = f32[72,128]{1,0:T(8,128)S(1)} collective-permute-done((f32[72,128]{1,0:T(8,128)S(1)}, f32[72,128]{1,0:T(8,128)S(1)}, u32[]{:S(2)}, u32[]{:S(2)}) %collective-permute-start.6) | collective-permute-done | bytes 36896 | tf_op jit(solution)/shard_map/ppermute | solution.py:534
  29.0 3.7 %collective-permute-done.7 = f32[72,128]{1,0:T(8,128)S(1)} collective-permute-done((f32[72,128]{1,0:T(8,128)S(1)}, f32[72,128]{1,0:T(8,128)S(1)}, u32[]{:S(2)}, u32[]{:S(2)}) %collective-permute-start.7) | collective-permute-done | bytes 36896 | tf_op jit(solution)/shard_map/ppermute | solution.py:534
  32.7 3.9 %collective-permute-done.8 = f32[72,128]{1,0:T(8,128)S(1)} collective-permute-done((f32[72,128]{1,0:T(8,128)S(1)}, f32[72,128]{1,0:T(8,128)S(1)}, u32[]{:S(2)}, u32[]{:S(2)}) %collective-permute-start.8) | collective-permute-done | bytes 36896 | tf_op jit(solution)/shard_map/ppermute | solution.py:534
  36.6 0.4 collective-permute-start.9
  37.1 3.5 %collective-permute-done.9 = f32[72,128]{1,0:T(8,128)S(1)} collective-permute-done((f32[72,128]{1,0:T(8,128)S(1)}, f32[72,128]{1,0:T(8,128)S(1)}, u32[]{:S(2)}, u32[]{:S(2)}) %collective-permute-start.9) | collective-permute-done | bytes 36896 | tf_op jit(solution)/shard_map/ppermute | solution.py:534
  40.6 1.2 %collective-permute-start.10 = (f32[72,128]{1,0:T(8,128)S(1)}, f32[72,128]{1,0:T(8,128)S(1)}, u32[]{:S(2)}, u32[]{:S(2)}) collective-permute-start(f32[72,128]{1,0:T(8,128)S(1)} %add.27), channel_id=1, source_target_pairs={{0,56},{1,57},{2,58},{3,59},{4,68},{5,69},{6,70},{7,71},{8,16},{9,... | collective-permute-start | bytes 110600 | tf_op jit(solution)/shard_map/ppermute | solution.py:534
  41.8 4.2 %collective-permute-done.10 = f32[72,128]{1,0:T(8,128)S(1)} collective-permute-done((f32[72,128]{1,0:T(8,128)S(1)}, f32[72,128]{1,0:T(8,128)S(1)}, u32[]{:S(2)}, u32[]{:S(2)}) %collective-permute-start.10) | collective-permute-done | bytes 36896 | tf_op jit(solution)/shard_map/ppermute | solution.py:534
  46.0 1.5 %collective-permute-start.11 = (f32[72,128]{1,0:T(8,128)S(1)}, f32[72,128]{1,0:T(8,128)S(1)}, u32[]{:S(2)}, u32[]{:S(2)}) collective-permute-start(f32[72,128]{1,0:T(8,128)S(1)} %add.28), channel_id=1, source_target_pairs={{0,3},{1,2},{2,1},{3,0},{4,28},{5,29},{6,30},{7,31},{8,11},{9,10},... | collective-permute-start | bytes 110600 | tf_op jit(solution)/shard_map/ppermute | solution.py:534
  47.6 3.6 %collective-permute-done.11 = f32[72,128]{1,0:T(8,128)S(1)} collective-permute-done((f32[72,128]{1,0:T(8,128)S(1)}, f32[72,128]{1,0:T(8,128)S(1)}, u32[]{:S(2)}, u32[]{:S(2)}) %collective-permute-start.11) | collective-permute-done | bytes 36896 | tf_op jit(solution)/shard_map/ppermute | solution.py:534
  51.2 1.6 %collective-permute-start.12 = (f32[72,128]{1,0:T(8,128)S(1)}, f32[72,128]{1,0:T(8,128)S(1)}, u32[]{:S(2)}, u32[]{:S(2)}) collective-permute-start(f32[72,128]{1,0:T(8,128)S(1)} %add.29), channel_id=1, source_target_pairs={{0,24},{1,25},{2,26},{3,27},{4,196},{5,197},{6,198},{7,199},{8,48}... | collective-permute-start | bytes 110600 | tf_op jit(solution)/shard_map/ppermute | solution.py:534
  52.8 4.2 %collective-permute-done.12 = f32[72,128]{1,0:T(8,128)S(1)} collective-permute-done((f32[72,128]{1,0:T(8,128)S(1)}, f32[72,128]{1,0:T(8,128)S(1)}, u32[]{:S(2)}, u32[]{:S(2)}) %collective-permute-start.12) | collective-permute-done | bytes 36896 | tf_op jit(solution)/shard_map/ppermute | solution.py:534
  57.0 1.3 %unsort.1 = f32[3,4,16,512]{3,2,1,0:T(8,128)} custom-call(f32[192,512]{1,0:T(8,128)S(1)} %get-tuple-element.23.wide_ref), custom_call_target="tpu_custom_call" | custom-call | flops 4000000000 | bytes 1000000 | tf_op jit(solution)/shard_map/unsort/pallas_call | solution.py:468
  58.3 3.9 %collective-permute-done.13 = f32[72,128]{1,0:T(8,128)S(1)} collective-permute-done((f32[72,128]{1,0:T(8,128)S(1)}, f32[72,128]{1,0:T(8,128)S(1)}, u32[]{:S(2)}, u32[]{:S(2)}) %collective-permute-start.13) | collective-permute-done | bytes 36896 | tf_op jit(solution)/shard_map/ppermute | solution.py:534
  62.2 8.9 %basis.1 = f32[1344,128]{1,0:T(8,128)} custom-call(f32[72,128]{1,0:T(8,128)S(1)} %add.31.total_ref, f32[2048,128]{1,0:T(8,128)S(1)} %get-tuple-element.25.snap_ref), custom_call_target="tpu_custom_call" | custom-call | tf_op jit(solution)/shard_map/basis/pallas_call | solution.py:168
  (24 shorter events, 0.5 us)
Async XLA Ops:
  0.6 4.4 %copy-start.1 = (f32[4,16,512]{2,1,0:T(8,128)S(1)}, f32[4,16,512]{2,1,0:T(8,128)}, u32[]{:S(2)}) copy-start(f32[4,16,512]{2,1,0:T(8,128)} %coef_ref.2) | copy-start | bytes 393220
  0.6 4.4 %copy-start = (f32[3,4,16,512]{3,2,1,0:T(8,128)S(1)}, f32[3,4,16,512]{3,2,1,0:T(8,128)}, u32[]{:S(2)}) copy-start(f32[3,4,16,512]{3,2,1,0:T(8,128)} %velocity_ref.2) | copy-start | bytes 1179652
  1.7 10.9 %collective-permute-start.2 = (f32[4,4,4,512]{3,2,1,0:T(4,128)S(1)}, f32[4,4,4,512]{3,2,1,0:T(4,128)S(1)}, u32[]{:S(2)}, u32[]{:S(2)}) collective-permute-start(f32[4,4,4,512]{3,2,1,0:T(4,128)S(1)} %get-tuple-element.18), channel_id=1, source_target_pairs={{0,1},{1,2},{2,3},{3,0},{4,5},{5,6},{6,7},{7,4},{8,9},{9,10},{10,1... | collective-permute-start | bytes 393224 | tf_op jit(solution)/shard_map/ppermute | solution.py:542
  3.3 9.4 %collective-permute-start.3 = (f32[4,4,4,512]{3,2,1,0:T(4,128)S(1)}, f32[4,4,4,512]{3,2,1,0:T(4,128)S(1)}, u32[]{:S(2)}, u32[]{:S(2)}) collective-permute-start(f32[4,4,4,512]{3,2,1,0:T(4,128)S(1)} %get-tuple-element.19), channel_id=1, source_target_pairs={{0,3},{1,0},{2,1},{3,2},{4,7},{5,4},{6,5},{7,6},{8,11},{9,8},{10,9... | collective-permute-start | bytes 393224 | tf_op jit(solution)/shard_map/ppermute | solution.py:542
  5.7 16.6 %collective-permute-start.1 = (f32[4,4,4,16,128]{4,3,2,1,0:T(8,128)S(1)}, f32[4,4,4,16,128]{4,3,2,1,0:T(8,128)S(1)}, u32[]{:S(2)}, u32[]{:S(2)}) collective-permute-start(f32[4,4,4,16,128]{4,3,2,1,0:T(8,128)S(1)} %pack.1.block_ref), channel_id=1, source_target_pairs={{0,0},{4,8},{8,4},{12,16},{16,12},{20,24},{24,20},{28,32},{32,28},... | collective-permute-start | bytes 1572872 | tf_op jit(solution)/shard_map/ppermute | solution.py:549
  12.5 9.7 %collective-permute-start = (f32[4,4,4,16,128]{4,3,2,1,0:T(8,128)S(1)}, f32[4,4,4,16,128]{4,3,2,1,0:T(8,128)S(1)}, u32[]{:S(2)}, u32[]{:S(2)}) collective-permute-start(f32[4,4,4,16,128]{4,3,2,1,0:T(8,128)S(1)} %pack.1.block_ref), channel_id=1, source_target_pairs={{0,4},{4,0},{8,12},{12,8},{16,20},{20,16},{24,28},{28,24},{32,36},... | collective-permute-start | bytes 1572872 | tf_op jit(solution)/shard_map/ppermute | solution.py:545
  13.1 3.9 %collective-permute-start.4 = (f32[4,2,4,8,128]{4,3,2,1,0:T(8,128)S(1)}, f32[4,2,4,8,128]{4,3,2,1,0:T(8,128)S(1)}, u32[]{:S(2)}, u32[]{:S(2)}) collective-permute-start(f32[4,2,4,8,128]{4,3,2,1,0:T(8,128)S(1)} %get-tuple-element.21), channel_id=1, source_target_pairs={{0,4},{4,0},{8,12},{12,8},{16,20},{20,16},{24,28},{28,24},{32,36},... | collective-permute-start | bytes 393224 | tf_op jit(solution)/shard_map/ppermute | solution.py:545
  13.7 8.5 %copy-start.2 = (s32[128]{0:T(128)S(1)}, s32[128]{0:T(128)}, u32[]{:S(2)}) copy-start(s32[128]{0:T(128)} %code_ref.1) | copy-start | bytes 1540
  13.7 8.5 %collective-permute-start.5 = (f32[4,2,4,8,128]{4,3,2,1,0:T(8,128)S(1)}, f32[4,2,4,8,128]{4,3,2,1,0:T(8,128)S(1)}, u32[]{:S(2)}, u32[]{:S(2)}) collective-permute-start(f32[4,2,4,8,128]{4,3,2,1,0:T(8,128)S(1)} %get-tuple-element.22), channel_id=1, source_target_pairs={{0,0},{4,8},{8,4},{12,16},{16,12},{20,24},{24,20},{28,32},{32,28},... | collective-permute-start | bytes 393224 | tf_op jit(solution)/shard_map/ppermute | solution.py:549
  27.4 1.3 %collective-permute-start.6 = (f32[72,128]{1,0:T(8,128)S(1)}, f32[72,128]{1,0:T(8,128)S(1)}, u32[]{:S(2)}, u32[]{:S(2)}) collective-permute-start(f32[72,128]{1,0:T(8,128)S(1)} %get-tuple-element.24), channel_id=1, source_target_pairs={{0,4},{1,5},{2,6},{3,7},{4,0},{5,1},{6,2},{7,3},{8,12},{9,13},{10,... | collective-permute-start | bytes 110600 | tf_op jit(solution)/shard_map/ppermute | solution.py:534
  28.7 4.0 %collective-permute-start.7 = (f32[72,128]{1,0:T(8,128)S(1)}, f32[72,128]{1,0:T(8,128)S(1)}, u32[]{:S(2)}, u32[]{:S(2)}) collective-permute-start(f32[72,128]{1,0:T(8,128)S(1)} %add.24), channel_id=1, source_target_pairs={{0,1},{1,0},{2,3},{3,2},{4,12},{5,13},{6,14},{7,15},{8,9},{9,8},{1... | collective-permute-start | bytes 110600 | tf_op jit(solution)/shard_map/ppermute | solution.py:534
  32.7 4.0 %collective-permute-start.8 = (f32[72,128]{1,0:T(8,128)S(1)}, f32[72,128]{1,0:T(8,128)S(1)}, u32[]{:S(2)}, u32[]{:S(2)}) collective-permute-start(f32[72,128]{1,0:T(8,128)S(1)} %add.25), channel_id=1, source_target_pairs={{0,8},{1,9},{2,10},{3,11},{4,5},{5,4},{6,7},{7,6},{8,0},{9,1},{10,... | collective-permute-start | bytes 110600 | tf_op jit(solution)/shard_map/ppermute | solution.py:534
  36.6 4.0 %collective-permute-start.9 = (f32[72,128]{1,0:T(8,128)S(1)}, f32[72,128]{1,0:T(8,128)S(1)}, u32[]{:S(2)}, u32[]{:S(2)}) collective-permute-start(f32[72,128]{1,0:T(8,128)S(1)} %add.26), channel_id=1, source_target_pairs={{0,64},{1,65},{2,66},{3,67},{4,60},{5,61},{6,62},{7,63},{8,72},{9,... | collective-permute-start | bytes 110600 | tf_op jit(solution)/shard_map/ppermute | solution.py:534
  40.6 5.4 %collective-permute-start.10 = (f32[72,128]{1,0:T(8,128)S(1)}, f32[72,128]{1,0:T(8,128)S(1)}, u32[]{:S(2)}, u32[]{:S(2)}) collective-permute-start(f32[72,128]{1,0:T(8,128)S(1)} %add.27), channel_id=1, source_target_pairs={{0,56},{1,57},{2,58},{3,59},{4,68},{5,69},{6,70},{7,71},{8,16},{9,... | collective-permute-start | bytes 110600 | tf_op jit(solution)/shard_map/ppermute | solution.py:534
  46.0 5.2 %collective-permute-start.11 = (f32[72,128]{1,0:T(8,128)S(1)}, f32[72,128]{1,0:T(8,128)S(1)}, u32[]{:S(2)}, u32[]{:S(2)}) collective-permute-start(f32[72,128]{1,0:T(8,128)S(1)} %add.28), channel_id=1, source_target_pairs={{0,3},{1,2},{2,1},{3,0},{4,28},{5,29},{6,30},{7,31},{8,11},{9,10},... | collective-permute-start | bytes 110600 | tf_op jit(solution)/shard_map/ppermute | solution.py:534
  51.2 5.8 %collective-permute-start.12 = (f32[72,128]{1,0:T(8,128)S(1)}, f32[72,128]{1,0:T(8,128)S(1)}, u32[]{:S(2)}, u32[]{:S(2)}) collective-permute-start(f32[72,128]{1,0:T(8,128)S(1)} %add.29), channel_id=1, source_target_pairs={{0,24},{1,25},{2,26},{3,27},{4,196},{5,197},{6,198},{7,199},{8,48}... | collective-permute-start | bytes 110600 | tf_op jit(solution)/shard_map/ppermute | solution.py:534
  57.0 5.2 %collective-permute-start.13 = (f32[72,128]{1,0:T(8,128)S(1)}, f32[72,128]{1,0:T(8,128)S(1)}, u32[]{:S(2)}, u32[]{:S(2)}) collective-permute-start(f32[72,128]{1,0:T(8,128)S(1)} %add.30), channel_id=1, source_target_pairs={{0,192},{1,193},{2,194},{3,195},{4,7},{5,6},{6,5},{7,4},{8,200},{9... | collective-permute-start | bytes 110600 | tf_op jit(solution)/shard_map/ppermute | solution.py:534

commit v6 on v5

--- a/solution.py
+++ b/solution.py
@@ -507,31 +507,26 @@
 def device_sum(part):
     axes = ("gy", "gz")
     size_z, size_x = 8, lax.axis_size("gz")
-    moves = {
-        "core": lambda x, y, z, core: (x, y, z, core ^ 1),
-        "x1": lambda x, y, z, core: (x ^ 1, y, z, core),
-        "x3": lambda x, y, z, core: (x ^ 3, y, z, core),
-        "y1": lambda x, y, z, core: (x, y ^ 1, z, core),
-        "y3": lambda x, y, z, core: (x, y ^ 3, z, core),
-        "za": lambda x, y, z, core: (x, y, z ^ 1, core),
-        "zb": lambda x, y, z, core: (x, y, (((z + 1) ^ 1) - 1) % size_z, core),
-        "zc": lambda x, y, z, core: (x, y, size_z - 1 - z if z % 4 in (1, 2) else z ^ 3, core),
-    }
-    orders = (
-        ("core", "x1", "za", "y1", "zb", "x3", "zc", "y3"),
-        ("core", "za", "x1", "zb", "y1", "zc", "y3", "x3"),
+    rounds = (
+        [lambda x, y, z, core: (x, y, z, core ^ 1)],
+        [lambda x, y, z, core, bits=bits: (x ^ bits, y, z, core) for bits in (1, 2, 3)],
+        [lambda x, y, z, core, bits=bits: (x, y ^ bits, z, core) for bits in (1, 2, 3)],
+        [lambda x, y, z, core, bits=bits: (x, y, z ^ bits, core) for bits in (1, 2, 3)],
+        [lambda x, y, z, core: (x, y, size_z - 1 - z, core)],
     )
 
-    def partner(step, device):
+    def partner(move, device):
         row, x = divmod(device, size_x)
-        core, z, y = row % 2, row // 2 % size_z, row // (2 * size_z)
-        x, y, z, core = moves[orders[core][step]](x, y, z, core)
+        x, y, z, core = move(x, row // (2 * size_z), row // 2 % size_z, row % 2)
         return ((y * size_z + z) * 2 + core) * size_x + x
 
     count = lax.axis_size("gy") * size_x
-    for step in range(len(moves)):
-        pairs = [(device, partner(step, device)) for device in range(count)]
-        part = part + lax.ppermute(part, axes, pairs)
+    for moves in rounds:
+        others = [
+            lax.ppermute(part, axes, [(device, partner(move, device)) for device in range(count)])
+            for move in moves
+        ]
+        part = part + sum(others[1:], others[0])
     return part
 
 

time: 71.2 us -> 67.1 us (0.942)
  the two profiles are of different devices: /device:TPU:24 before, /device:TPU:32 now
where the time goes in v6:
time: 67.1 us; the launch traced here: 67 us
  starting transfers between devices  28.2 us (42%)
  waiting for transfers between devices  20.5 us (31%)
  Pallas kernels  17.5 us (26%)
  between operations  0.72 us (1%)
    ppermute x11, starting transfers between devices, device_sum(): lax.ppermute(part, axes, [(device, partner(move, device)) for device in r...  18.5 us
    ppermute x11, waiting for transfers between devices, device_sum(): lax.ppermute(part, axes, [(device, partner(move, device)) for device in r...  15.4 us
    pallas_call x1, Pallas kernels, project(): pl.pallas_call(functools.partial(basis_kernel, rows_all=rows_all), out_sh...  8.91 us
    pallas_call x1, Pallas kernels, both_steps(): pl.pallas_call(steps_kernel, out_shape=(f32(3 * rows_y * rows_z, 4 * LANE...  5.15 us
    ppermute x2, waiting for transfers between devices, off_chip(): return lax.ppermute(part, 'gy', list(enumerate(partners)))  5.01 us
    ppermute x2, starting transfers between devices, off_chip(): return lax.ppermute(part, 'gy', list(enumerate(partners)))  4.16 us
    ppermute x2, starting transfers between devices, along_z(): lax.ppermute(part, 'gz', [(i, (i + step) % count_z) for i in range(count_...  3.31 us
    ppermute x2, starting transfers between devices, on_chip(): return lax.ppermute(part, 'gy', [(i, i ^ 1) for i in range(count_y)])  2.21 us
  transfers between devices with their start and end apart: 17, of which 9 were waited for; matrix products, arithmetic and copies ran while one was open for 0% of the time, Pallas kernels for 4%

profile of v6, /device:TPU:32, one launch (start us, length us, event | category | flops | bytes accessed | tf_op | source)
XLA Modules:
  0.0 67.0 jit_solution(9244480693880566581)
XLA Ops:
  0.6 1.1 %edges.1 = (f32[4,4,4,512]{3,2,1,0:T(4,128)S(1)}, f32[4,4,4,512]{3,2,1,0:T(4,128)S(1)}) custom-call(f32[3,4,16,512]{3,2,1,0:T(8,128)} %velocity_ref.2, f32[4,16,512]{2,1,0:T(8,128)} %coef_ref.2), custom_call_target="tpu_custom_call" | custom-call | tf_op jit(solution)/shard_map/edges/pallas_call | solution.py:209
  1.7 1.6 %collective-permute-start.2 = (f32[4,4,4,512]{3,2,1,0:T(4,128)S(1)}, f32[4,4,4,512]{3,2,1,0:T(4,128)S(1)}, u32[]{:S(2)}, u32[]{:S(2)}) collective-permute-start(f32[4,4,4,512]{3,2,1,0:T(4,128)S(1)} %get-tuple-element.18), channel_id=1, source_target_pairs={{0,1},{1,2},{2,3},{3,0},{4,5},{5,6},{6,7},{7,4},{8,9},{9,10},{10,1... | collective-permute-start | bytes 393224 | tf_op jit(solution)/shard_map/ppermute | solution.py:537
  3.3 1.7 %collective-permute-start.3 = (f32[4,4,4,512]{3,2,1,0:T(4,128)S(1)}, f32[4,4,4,512]{3,2,1,0:T(4,128)S(1)}, u32[]{:S(2)}, u32[]{:S(2)}) collective-permute-start(f32[4,4,4,512]{3,2,1,0:T(4,128)S(1)} %get-tuple-element.19), channel_id=1, source_target_pairs={{0,3},{1,0},{2,1},{3,2},{4,7},{5,4},{6,5},{7,6},{8,11},{9,8},{10,9... | collective-permute-start | bytes 393224 | tf_op jit(solution)/shard_map/ppermute | solution.py:537
  5.7 1.9 %collective-permute-start.1 = (f32[4,4,4,16,128]{4,3,2,1,0:T(8,128)S(1)}, f32[4,4,4,16,128]{4,3,2,1,0:T(8,128)S(1)}, u32[]{:S(2)}, u32[]{:S(2)}) collective-permute-start(f32[4,4,4,16,128]{4,3,2,1,0:T(8,128)S(1)} %pack.1.block_ref), channel_id=1, source_target_pairs={{0,0},{4,8},{8,4},{12,16},{16,12},{20,24},{24,20},{28,32},{32,28},... | collective-permute-start | bytes 1572872 | tf_op jit(solution)/shard_map/ppermute | solution.py:544
  7.6 2.1 %collective-permute-start = (f32[4,4,4,16,128]{4,3,2,1,0:T(8,128)S(1)}, f32[4,4,4,16,128]{4,3,2,1,0:T(8,128)S(1)}, u32[]{:S(2)}, u32[]{:S(2)}) collective-permute-start(f32[4,4,4,16,128]{4,3,2,1,0:T(8,128)S(1)} %pack.1.block_ref), channel_id=1, source_target_pairs={{0,4},{4,0},{8,12},{12,8},{16,20},{20,16},{24,28},{28,24},{32,36},... | collective-permute-start | bytes 1572872 | tf_op jit(solution)/shard_map/ppermute | solution.py:540
  10.3 2.2 %collective-permute-start.5 = (f32[4,2,4,8,128]{4,3,2,1,0:T(8,128)S(1)}, f32[4,2,4,8,128]{4,3,2,1,0:T(8,128)S(1)}, u32[]{:S(2)}, u32[]{:S(2)}) collective-permute-start(f32[4,2,4,8,128]{4,3,2,1,0:T(8,128)S(1)} %get-tuple-element.22), channel_id=1, source_target_pairs={{0,0},{4,8},{8,4},{12,16},{16,12},{20,24},{24,20},{28,32},{32,28},... | collective-permute-start | bytes 393224 | tf_op jit(solution)/shard_map/ppermute | solution.py:544
  12.6 5.0 %collective-permute-done.5.side_other_ref = f32[4,2,4,8,128]{4,3,2,1,0:T(8,128)S(1)} collective-permute-done((f32[4,2,4,8,128]{4,3,2,1,0:T(8,128)S(1)}, f32[4,2,4,8,128]{4,3,2,1,0:T(8,128)S(1)}, u32[]{:S(2)}, u32[]{:S(2)}) %collective-permute-start.5) | collective-permute-done | bytes 131104 | tf_op jit(solution)/shard_map/ppermute | solution.py:544
  17.6 5.1 %steps.1 = (f32[192,512]{1,0:T(8,128)S(1)}, f32[2048,128]{1,0:T(8,128)S(1)}, f32[72,128]{1,0:T(8,128)S(1)}) custom-call(s32[128]{0:T(128)S(1)} %copy-done.2, f32[4,4,4,16,128]{4,3,2,1,0:T(8,128)S(1)} %pack.1.block_ref, f32[4,4,4,16,128]{4,3,2,1,0:T(8,128)S(1)} %collective-permute-done.chip_ref, f32[4,4,4,16,128]{4,3,2,1,0:T(8,128)S(1)} %collective-permute-done.1.other_ref, ...), custom_call_target="tpu_custom_call" | custom-call | tf_op jit(solution)/shard_map/steps/pallas_call | solution.py:485
  23.1 0.9 %collective-permute-done.6 = f32[72,128]{1,0:T(8,128)S(1)} collective-permute-done((f32[72,128]{1,0:T(8,128)S(1)}, f32[72,128]{1,0:T(8,128)S(1)}, u32[]{:S(2)}, u32[]{:S(2)}) %collective-permute-start.6) | collective-permute-done | bytes 36896 | tf_op jit(solution)/shard_map/ppermute | solution.py:526
  24.1 1.6 %collective-permute-start.9 = (f32[72,128]{1,0:T(8,128)S(1)}, f32[72,128]{1,0:T(8,128)S(1)}, u32[]{:S(2)}, u32[]{:S(2)}) collective-permute-start(f32[72,128]{1,0:T(8,128)S(1)} %add.33), channel_id=1, source_target_pairs={{0,3},{1,2},{2,1},{3,0},{4,7},{5,6},{6,5},{7,4},{8,11},{9,10},{10,... | collective-permute-start | bytes 110600 | tf_op jit(solution)/shard_map/ppermute | solution.py:526
  26.4 1.7 %collective-permute-start.7 = (f32[72,128]{1,0:T(8,128)S(1)}, f32[72,128]{1,0:T(8,128)S(1)}, u32[]{:S(2)}, u32[]{:S(2)}) collective-permute-start(f32[72,128]{1,0:T(8,128)S(1)} %add.33), channel_id=1, source_target_pairs={{0,1},{1,0},{2,3},{3,2},{4,5},{5,4},{6,7},{7,6},{8,9},{9,8},{10,11... | collective-permute-start | bytes 110600 | tf_op jit(solution)/shard_map/ppermute | solution.py:526
  28.2 1.1 %collective-permute-done.9 = f32[72,128]{1,0:T(8,128)S(1)} collective-permute-done((f32[72,128]{1,0:T(8,128)S(1)}, f32[72,128]{1,0:T(8,128)S(1)}, u32[]{:S(2)}, u32[]{:S(2)}) %collective-permute-start.9) | collective-permute-done | bytes 36896 | tf_op jit(solution)/shard_map/ppermute | solution.py:526
  29.2 1.8 %collective-permute-done.8 = f32[72,128]{1,0:T(8,128)S(1)} collective-permute-done((f32[72,128]{1,0:T(8,128)S(1)}, f32[72,128]{1,0:T(8,128)S(1)}, u32[]{:S(2)}, u32[]{:S(2)}) %collective-permute-start.8) | collective-permute-done | bytes 36896 | tf_op jit(solution)/shard_map/ppermute | solution.py:526
  31.1 3.6 %collective-permute-start.12 = (f32[72,128]{1,0:T(8,128)S(1)}, f32[72,128]{1,0:T(8,128)S(1)}, u32[]{:S(2)}, u32[]{:S(2)}) collective-permute-start(f32[72,128]{1,0:T(8,128)S(1)} %add_add_fusion.2), channel_id=1, source_target_pairs={{0,192},{1,193},{2,194},{3,195},{4,196},{5,197},{6,198},{7,199},{8... | collective-permute-start | bytes 110600 | tf_op jit(solution)/shard_map/ppermute | solution.py:526
  35.7 1.0 %collective-permute-done.12 = f32[72,128]{1,0:T(8,128)S(1)} collective-permute-done((f32[72,128]{1,0:T(8,128)S(1)}, f32[72,128]{1,0:T(8,128)S(1)}, u32[]{:S(2)}, u32[]{:S(2)}) %collective-permute-start.12) | collective-permute-done | bytes 36896 | tf_op jit(solution)/shard_map/ppermute | solution.py:526
  36.7 3.5 %collective-permute-done.11 = f32[72,128]{1,0:T(8,128)S(1)} collective-permute-done((f32[72,128]{1,0:T(8,128)S(1)}, f32[72,128]{1,0:T(8,128)S(1)}, u32[]{:S(2)}, u32[]{:S(2)}) %collective-permute-start.11) | collective-permute-done | bytes 36896 | tf_op jit(solution)/shard_map/ppermute | solution.py:526
  40.2 1.8 %collective-permute-start.15 = (f32[72,128]{1,0:T(8,128)S(1)}, f32[72,128]{1,0:T(8,128)S(1)}, u32[]{:S(2)}, u32[]{:S(2)}) collective-permute-start(f32[72,128]{1,0:T(8,128)S(1)} %add_add_fusion.1), channel_id=1, source_target_pairs={{0,24},{1,25},{2,26},{3,27},{4,28},{5,29},{6,30},{7,31},{8,16},{9,... | collective-permute-start | bytes 110600 | tf_op jit(solution)/shard_map/ppermute | solution.py:526
  42.0 4.8 %collective-permute-start.14 = (f32[72,128]{1,0:T(8,128)S(1)}, f32[72,128]{1,0:T(8,128)S(1)}, u32[]{:S(2)}, u32[]{:S(2)}) collective-permute-start(f32[72,128]{1,0:T(8,128)S(1)} %add_add_fusion.1), channel_id=1, source_target_pairs={{0,16},{1,17},{2,18},{3,19},{4,20},{5,21},{6,22},{7,23},{8,24},{9,... | collective-permute-start | bytes 110600 | tf_op jit(solution)/shard_map/ppermute | solution.py:526
  46.9 2.3 %collective-permute-done.14 = f32[72,128]{1,0:T(8,128)S(1)} collective-permute-done((f32[72,128]{1,0:T(8,128)S(1)}, f32[72,128]{1,0:T(8,128)S(1)}, u32[]{:S(2)}, u32[]{:S(2)}) %collective-permute-start.14) | collective-permute-done | bytes 36896 | tf_op jit(solution)/shard_map/ppermute | solution.py:526
  49.2 1.6 %collective-permute-done.13 = f32[72,128]{1,0:T(8,128)S(1)} collective-permute-done((f32[72,128]{1,0:T(8,128)S(1)}, f32[72,128]{1,0:T(8,128)S(1)}, u32[]{:S(2)}, u32[]{:S(2)}) %collective-permute-start.13) | collective-permute-done | bytes 36896 | tf_op jit(solution)/shard_map/ppermute | solution.py:526
  50.8 2.8 %collective-permute-start.16 = (f32[72,128]{1,0:T(8,128)S(1)}, f32[72,128]{1,0:T(8,128)S(1)}, u32[]{:S(2)}, u32[]{:S(2)}) collective-permute-start(f32[72,128]{1,0:T(8,128)S(1)} %add_add_fusion), channel_id=1, source_target_pairs={{0,56},{1,57},{2,58},{3,59},{4,60},{5,61},{6,62},{7,63},{8,48},{9,... | collective-permute-start | bytes 110600 | tf_op jit(solution)/shard_map/ppermute | solution.py:526
  53.7 1.3 %unsort.1 = f32[3,4,16,512]{3,2,1,0:T(8,128)} custom-call(f32[192,512]{1,0:T(8,128)S(1)} %get-tuple-element.23.wide_ref), custom_call_target="tpu_custom_call" | custom-call | flops 4000000000 | bytes 1000000 | tf_op jit(solution)/shard_map/unsort/pallas_call | solution.py:468
  54.9 3.1 %collective-permute-done.16 = f32[72,128]{1,0:T(8,128)S(1)} collective-permute-done((f32[72,128]{1,0:T(8,128)S(1)}, f32[72,128]{1,0:T(8,128)S(1)}, u32[]{:S(2)}, u32[]{:S(2)}) %collective-permute-start.16) | collective-permute-done | bytes 36896 | tf_op jit(solution)/shard_map/ppermute | solution.py:526
  58.1 8.9 %basis.1 = f32[1344,128]{1,0:T(8,128)} custom-call(f32[72,128]{1,0:T(8,128)S(1)} %add.43.total_ref, f32[2048,128]{1,0:T(8,128)S(1)} %get-tuple-element.25.snap_ref), custom_call_target="tpu_custom_call" | custom-call | tf_op jit(solution)/shard_map/basis/pallas_call | solution.py:168
  (27 shorter events, 3.5 us)
Async XLA Ops:
  0.6 4.4 %copy-start.1 = (f32[4,16,512]{2,1,0:T(8,128)S(1)}, f32[4,16,512]{2,1,0:T(8,128)}, u32[]{:S(2)}) copy-start(f32[4,16,512]{2,1,0:T(8,128)} %coef_ref.2) | copy-start | bytes 393220
  0.6 4.4 %copy-start = (f32[3,4,16,512]{3,2,1,0:T(8,128)S(1)}, f32[3,4,16,512]{3,2,1,0:T(8,128)}, u32[]{:S(2)}) copy-start(f32[3,4,16,512]{3,2,1,0:T(8,128)} %velocity_ref.2) | copy-start | bytes 1179652
  1.7 8.0 %collective-permute-start.2 = (f32[4,4,4,512]{3,2,1,0:T(4,128)S(1)}, f32[4,4,4,512]{3,2,1,0:T(4,128)S(1)}, u32[]{:S(2)}, u32[]{:S(2)}) collective-permute-start(f32[4,4,4,512]{3,2,1,0:T(4,128)S(1)} %get-tuple-element.18), channel_id=1, source_target_pairs={{0,1},{1,2},{2,3},{3,0},{4,5},{5,6},{6,7},{7,4},{8,9},{9,10},{10,1... | collective-permute-start | bytes 393224 | tf_op jit(solution)/shard_map/ppermute | solution.py:537
  3.3 6.4 %collective-permute-start.3 = (f32[4,4,4,512]{3,2,1,0:T(4,128)S(1)}, f32[4,4,4,512]{3,2,1,0:T(4,128)S(1)}, u32[]{:S(2)}, u32[]{:S(2)}) collective-permute-start(f32[4,4,4,512]{3,2,1,0:T(4,128)S(1)} %get-tuple-element.19), channel_id=1, source_target_pairs={{0,3},{1,0},{2,1},{3,2},{4,7},{5,4},{6,5},{7,6},{8,11},{9,8},{10,9... | collective-permute-start | bytes 393224 | tf_op jit(solution)/shard_map/ppermute | solution.py:537
  5.7 11.9 %collective-permute-start.1 = (f32[4,4,4,16,128]{4,3,2,1,0:T(8,128)S(1)}, f32[4,4,4,16,128]{4,3,2,1,0:T(8,128)S(1)}, u32[]{:S(2)}, u32[]{:S(2)}) collective-permute-start(f32[4,4,4,16,128]{4,3,2,1,0:T(8,128)S(1)} %pack.1.block_ref), channel_id=1, source_target_pairs={{0,0},{4,8},{8,4},{12,16},{16,12},{20,24},{24,20},{28,32},{32,28},... | collective-permute-start | bytes 1572872 | tf_op jit(solution)/shard_map/ppermute | solution.py:544
  7.6 10.0 %collective-permute-start = (f32[4,4,4,16,128]{4,3,2,1,0:T(8,128)S(1)}, f32[4,4,4,16,128]{4,3,2,1,0:T(8,128)S(1)}, u32[]{:S(2)}, u32[]{:S(2)}) collective-permute-start(f32[4,4,4,16,128]{4,3,2,1,0:T(8,128)S(1)} %pack.1.block_ref), channel_id=1, source_target_pairs={{0,4},{4,0},{8,12},{12,8},{16,20},{20,16},{24,28},{28,24},{32,36},... | collective-permute-start | bytes 1572872 | tf_op jit(solution)/shard_map/ppermute | solution.py:540
  10.2 2.4 %collective-permute-start.4 = (f32[4,2,4,8,128]{4,3,2,1,0:T(8,128)S(1)}, f32[4,2,4,8,128]{4,3,2,1,0:T(8,128)S(1)}, u32[]{:S(2)}, u32[]{:S(2)}) collective-permute-start(f32[4,2,4,8,128]{4,3,2,1,0:T(8,128)S(1)} %get-tuple-element.21), channel_id=1, source_target_pairs={{0,4},{4,0},{8,12},{12,8},{16,20},{20,16},{24,28},{28,24},{32,36},... | collective-permute-start | bytes 393224 | tf_op jit(solution)/shard_map/ppermute | solution.py:540
  10.3 7.3 %copy-start.2 = (s32[128]{0:T(128)S(1)}, s32[128]{0:T(128)}, u32[]{:S(2)}) copy-start(s32[128]{0:T(128)} %code_ref.1) | copy-start | bytes 1540
  10.3 7.3 %collective-permute-start.5 = (f32[4,2,4,8,128]{4,3,2,1,0:T(8,128)S(1)}, f32[4,2,4,8,128]{4,3,2,1,0:T(8,128)S(1)}, u32[]{:S(2)}, u32[]{:S(2)}) collective-permute-start(f32[4,2,4,8,128]{4,3,2,1,0:T(8,128)S(1)} %get-tuple-element.22), channel_id=1, source_target_pairs={{0,0},{4,8},{8,4},{12,16},{16,12},{20,24},{24,20},{28,32},{32,28},... | collective-permute-start | bytes 393224 | tf_op jit(solution)/shard_map/ppermute | solution.py:544
  22.8 1.3 %collective-permute-start.6 = (f32[72,128]{1,0:T(8,128)S(1)}, f32[72,128]{1,0:T(8,128)S(1)}, u32[]{:S(2)}, u32[]{:S(2)}) collective-permute-start(f32[72,128]{1,0:T(8,128)S(1)} %get-tuple-element.24), channel_id=1, source_target_pairs={{0,4},{1,5},{2,6},{3,7},{4,0},{5,1},{6,2},{7,3},{8,12},{9,13},{10,... | collective-permute-start | bytes 110600 | tf_op jit(solution)/shard_map/ppermute | solution.py:526
  24.1 5.2 %collective-permute-start.9 = (f32[72,128]{1,0:T(8,128)S(1)}, f32[72,128]{1,0:T(8,128)S(1)}, u32[]{:S(2)}, u32[]{:S(2)}) collective-permute-start(f32[72,128]{1,0:T(8,128)S(1)} %add.33), channel_id=1, source_target_pairs={{0,3},{1,2},{2,1},{3,0},{4,7},{5,6},{6,5},{7,4},{8,11},{9,10},{10,... | collective-permute-start | bytes 110600 | tf_op jit(solution)/shard_map/ppermute | solution.py:526
  25.6 5.5 %collective-permute-start.8 = (f32[72,128]{1,0:T(8,128)S(1)}, f32[72,128]{1,0:T(8,128)S(1)}, u32[]{:S(2)}, u32[]{:S(2)}) collective-permute-start(f32[72,128]{1,0:T(8,128)S(1)} %add.33), channel_id=1, source_target_pairs={{0,2},{1,3},{2,0},{3,1},{4,6},{5,7},{6,4},{7,5},{8,10},{9,11},{10,... | collective-permute-start | bytes 110600 | tf_op jit(solution)/shard_map/ppermute | solution.py:526
  26.4 4.7 %collective-permute-start.7 = (f32[72,128]{1,0:T(8,128)S(1)}, f32[72,128]{1,0:T(8,128)S(1)}, u32[]{:S(2)}, u32[]{:S(2)}) collective-permute-start(f32[72,128]{1,0:T(8,128)S(1)} %add.33), channel_id=1, source_target_pairs={{0,1},{1,0},{2,3},{3,2},{4,5},{5,4},{6,7},{7,6},{8,9},{9,8},{10,11... | collective-permute-start | bytes 110600 | tf_op jit(solution)/shard_map/ppermute | solution.py:526
  31.1 5.6 %collective-permute-start.12 = (f32[72,128]{1,0:T(8,128)S(1)}, f32[72,128]{1,0:T(8,128)S(1)}, u32[]{:S(2)}, u32[]{:S(2)}) collective-permute-start(f32[72,128]{1,0:T(8,128)S(1)} %add_add_fusion.2), channel_id=1, source_target_pairs={{0,192},{1,193},{2,194},{3,195},{4,196},{5,197},{6,198},{7,199},{8... | collective-permute-start | bytes 110600 | tf_op jit(solution)/shard_map/ppermute | solution.py:526
  34.7 5.5 %collective-permute-start.11 = (f32[72,128]{1,0:T(8,128)S(1)}, f32[72,128]{1,0:T(8,128)S(1)}, u32[]{:S(2)}, u32[]{:S(2)}) collective-permute-start(f32[72,128]{1,0:T(8,128)S(1)} %add_add_fusion.2), channel_id=1, source_target_pairs={{0,128},{1,129},{2,130},{3,131},{4,132},{5,133},{6,134},{7,135},{8... | collective-permute-start | bytes 110600 | tf_op jit(solution)/shard_map/ppermute | solution.py:526
  35.1 5.1 %collective-permute-start.10 = (f32[72,128]{1,0:T(8,128)S(1)}, f32[72,128]{1,0:T(8,128)S(1)}, u32[]{:S(2)}, u32[]{:S(2)}) collective-permute-start(f32[72,128]{1,0:T(8,128)S(1)} %add_add_fusion.2), channel_id=1, source_target_pairs={{0,64},{1,65},{2,66},{3,67},{4,68},{5,69},{6,70},{7,71},{8,72},{9,... | collective-permute-start | bytes 110600 | tf_op jit(solution)/shard_map/ppermute | solution.py:526
  40.2 6.7 %collective-permute-start.15 = (f32[72,128]{1,0:T(8,128)S(1)}, f32[72,128]{1,0:T(8,128)S(1)}, u32[]{:S(2)}, u32[]{:S(2)}) collective-permute-start(f32[72,128]{1,0:T(8,128)S(1)} %add_add_fusion.1), channel_id=1, source_target_pairs={{0,24},{1,25},{2,26},{3,27},{4,28},{5,29},{6,30},{7,31},{8,16},{9,... | collective-permute-start | bytes 110600 | tf_op jit(solution)/shard_map/ppermute | solution.py:526
  42.0 7.1 %collective-permute-start.14 = (f32[72,128]{1,0:T(8,128)S(1)}, f32[72,128]{1,0:T(8,128)S(1)}, u32[]{:S(2)}, u32[]{:S(2)}) collective-permute-start(f32[72,128]{1,0:T(8,128)S(1)} %add_add_fusion.1), channel_id=1, source_target_pairs={{0,16},{1,17},{2,18},{3,19},{4,20},{5,21},{6,22},{7,23},{8,24},{9,... | collective-permute-start | bytes 110600 | tf_op jit(solution)/shard_map/ppermute | solution.py:526
  46.9 4.0 %collective-permute-start.13 = (f32[72,128]{1,0:T(8,128)S(1)}, f32[72,128]{1,0:T(8,128)S(1)}, u32[]{:S(2)}, u32[]{:S(2)}) collective-permute-start(f32[72,128]{1,0:T(8,128)S(1)} %add_add_fusion.1), channel_id=1, source_target_pairs={{0,8},{1,9},{2,10},{3,11},{4,12},{5,13},{6,14},{7,15},{8,0},{9,1},... | collective-permute-start | bytes 110600 | tf_op jit(solution)/shard_map/ppermute | solution.py:526
  50.8 7.2 %collective-permute-start.16 = (f32[72,128]{1,0:T(8,128)S(1)}, f32[72,128]{1,0:T(8,128)S(1)}, u32[]{:S(2)}, u32[]{:S(2)}) collective-permute-start(f32[72,128]{1,0:T(8,128)S(1)} %add_add_fusion), channel_id=1, source_target_pairs={{0,56},{1,57},{2,58},{3,59},{4,60},{5,61},{6,62},{7,63},{8,48},{9,... | collective-permute-start | bytes 110600 | tf_op jit(solution)/shard_map/ppermute | solution.py:526

commit v7 on v6

--- a/solution.py
+++ b/solution.py
@@ -13,6 +13,7 @@
 GROUP = 5
 LANES = 128
 SLOT = 16
+EDGE = 8
 
 
 nu_limit = 0.125
@@ -276,23 +277,37 @@
     )(low, high)
 
 
+def around_z(ref, index):
+    return ref[(*index, slice(EDGE + 1, EDGE + 25))], ref[(*index, slice(EDGE - 1, EDGE + 23))]
+
+
+def at(ref, *index):
+    return ref[(*index, slice(EDGE, EDGE + 24))]
+
+
+def put(ref, index, plane):
+    ref[(*index, slice(EDGE, EDGE + 24))] = plane
+    close(ref, index, plane)
+
+
+def close(ref, index, plane):
+    ref[(*index, slice(EDGE - 1, EDGE))] = plane[23:24]
+    ref[(*index, slice(EDGE + 24, EDGE + 25))] = plane[:1]
+
+
 def around_x(ref, index, o):
-    ahead = ref[(*index, o + 1)] if o < 3 else pltpu.roll(ref[(*index, 0)], LANES - 1, 1)
-    behind = ref[(*index, o - 1)] if o > 0 else pltpu.roll(ref[(*index, 3)], 1, 1)
+    ahead = at(ref, *index, o + 1) if o < 3 else pltpu.roll(at(ref, *index, 0), LANES - 1, 1)
+    behind = at(ref, *index, o - 1) if o > 0 else pltpu.roll(at(ref, *index, 3), 1, 1)
     return ahead, behind
-
-
-def around_z(plane):
-    return pltpu.roll(plane, plane.shape[0] - 1, 0), pltpu.roll(plane, 1, 0)
 
 
 def half_viscosity(cells_ref, y, o, coefficient):
     jump = []
     for c in range(3):
         x_ahead, x_behind = around_x(cells_ref, (c, y), o)
-        z_ahead, z_behind = around_z(cells_ref[c, y, o])
+        z_ahead, z_behind = around_z(cells_ref, (c, y, o))
         jump.append(
-            (x_ahead - x_behind, cells_ref[c, y + 1, o] - cells_ref[c, y - 1, o], z_ahead - z_behind)
+            (x_ahead - x_behind, at(cells_ref, c, y + 1, o) - at(cells_ref, c, y - 1, o), z_ahead - z_behind)
         )
     total = jump[0][0] ** 2 + jump[1][1] ** 2 + jump[2][2] ** 2
     total = total + total
@@ -303,17 +318,22 @@
 
 
 def stepped(cells_ref, y, visc_ref, v, o):
-    here = visc_ref[v, o]
-    visc = [*around_x(visc_ref, (v,), o), visc_ref[v + 1, o], visc_ref[v - 1, o], *around_z(here)]
+    here = at(visc_ref, v, o)
+    visc = [
+        *around_x(visc_ref, (v,), o),
+        at(visc_ref, v + 1, o),
+        at(visc_ref, v - 1, o),
+        *around_z(visc_ref, (v, o)),
+    ]
     visc = [here + other for other in visc]
     result = []
     for c in range(3):
-        centre = cells_ref[c, y, o]
+        centre = at(cells_ref, c, y, o)
         cells = [
             *around_x(cells_ref, (c, y), o),
-            cells_ref[c, y + 1, o],
-            cells_ref[c, y - 1, o],
-            *around_z(centre),
+            at(cells_ref, c, y + 1, o),
+            at(cells_ref, c, y - 1, o),
+            *around_z(cells_ref, (c, y, o)),
         ]
         change = visc[0] * (cells[0] - centre)
         for n in range(1, 6):
@@ -365,27 +385,29 @@
     def ahead(chip, other):
         return jnp.where(last, 0.0, jnp.where(odd, other, chip))
 
+    own_rows, layers = slice(EDGE, EDGE + rows_z), sides_ref.shape[3]
+    side = slice(EDGE + rows_z, EDGE + rows_z + layers)
     for c in range(4):
         for y in range(rows_y):
             for o in range(4):
-                cells_ref[c, rows_y + y, o, :rows_z] = block_ref[c, y, o]
+                own, below, above = (c, rows_y + y, o), (c, y, o), (c, 2 * rows_y + y, o)
+                cells_ref[(*own, own_rows)] = block_ref[c, y, o]
                 chip, other = chip_ref[c, y, o], other_ref[c, y, o]
-                cells_ref[c, y, o, :rows_z] = behind(chip, other)
-                cells_ref[c, 2 * rows_y + y, o, :rows_z] = ahead(chip, other)
-                side = (slice(rows_z, rows_z + sides_ref.shape[3]),)
-                cells_ref[(c, rows_y + y, o, *side)] = sides_ref[c, y, o]
-                for choose, at, away in (
-                    (behind, y, rows_y - 1 - y),
-                    (ahead, 2 * rows_y + y, y),
-                ):
+                cells_ref[(*below, own_rows)] = behind(chip, other)
+                cells_ref[(*above, own_rows)] = ahead(chip, other)
+                cells_ref[(*own, side)] = sides_ref[c, y, o]
+                for choose, place, away in ((behind, below, rows_y - 1 - y), (ahead, above, y)):
                     if away == 0:
                         halo = choose(side_chip_ref[c, 0, o], side_other_ref[c, 0, o])
-                        cells_ref[(c, at, o, *side)] = halo
+                        cells_ref[(*place, side)] = halo
                     elif away <= rows_y - 2:
-                        for n, begin in enumerate((rows_z, rows_z + sides_ref.shape[3] - 2)):
+                        for n, begin in enumerate((rows_z, rows_z + layers - 2)):
                             part = (c, 1, o, slice(4 * (away - 1) + 2 * n, 4 * (away - 1) + 2 * n + 2))
                             halo = choose(side_chip_ref[part], side_other_ref[part])
-                            cells_ref[c, at, o, begin : begin + 2] = halo
+                            cells_ref[(*place, slice(EDGE + begin, EDGE + begin + 2))] = halo
+                if c < 3:
+                    for place in (own, below, above):
+                        close(cells_ref, place, at(cells_ref, *place))
 
     @pl.when(first)
     def _():
@@ -399,7 +421,7 @@
 
     def visc_one(y, carry):
         for o in range(4):
-            visc_ref[y, o] = half_viscosity(cells_ref, y, o, cells_ref[3, y, o])
+            put(visc_ref, (y, o), half_viscosity(cells_ref, y, o, at(cells_ref, 3, y, o)))
         return carry
 
     lax.fori_loop(1, 3 * rows_y - 1, visc_one, 0)
@@ -410,14 +432,14 @@
         )
         for o in range(4):
             for c, cells in enumerate(stepped(cells_ref, y, visc_ref, y, o)):
-                one_ref[c, y, o] = jnp.where(outside, 0.0, cells)
+                put(one_ref, (c, y, o), jnp.where(outside, 0.0, cells))
         return carry
 
     lax.fori_loop(2, 3 * rows_y - 2, step_one, 0)
 
     def visc_two(y, carry):
         for o in range(4):
-            visc_ref[y, o] = half_viscosity(one_ref, y, o, cells_ref[3, y, o])
+            put(visc_ref, (y, o), half_viscosity(one_ref, y, o, at(cells_ref, 3, y, o)))
         return carry
 
     lax.fori_loop(rows_y - 1, 2 * rows_y + 1, visc_two, 0)
@@ -428,13 +450,14 @@
                 two_ref[c, y, o] = cells[:rows_z]
                 start = (c * rows_y + y) * rows_z
                 wide_ref[start : start + rows_z, LANES * o : LANES * (o + 1)] = cells[:rows_z]
-    for state, (ref, shift) in enumerate(((block_ref, 0), (one_ref, rows_y), (two_ref, 0))):
+    states = ((block_ref, 0, 0), (one_ref, rows_y, EDGE), (two_ref, 0, 0))
+    for state, (ref, shift, edge) in enumerate(states):
         for y in range(rows_y):
             for z in range(4):
                 for o in range(4):
                     start = SLOT * (64 * state + 16 * y + 4 * z + o)
                     for c in range(3):
-                        piece = ref[c, shift + y, o, pl.ds(z, rows_z // 4, stride=4), :]
+                        piece = ref[c, shift + y, o, pl.ds(edge + z, rows_z // 4, stride=4), :]
                         all_ref[start + 4 * c : start + 4 * c + 4, :] = piece
 
     def pick(column, carry):
@@ -481,7 +504,7 @@
     cols = snap_code.shape[0]
     f32 = lambda *shape: jax.ShapeDtypeStruct(shape, jnp.float32)
     scratch = lambda *shape: pltpu.VMEM(shape, jnp.float32)
-    depth = rows_z + 8
+    depth = EDGE + rows_z + 16
     return pl.pallas_call(
         steps_kernel,
         out_shape=(
@@ -508,11 +531,14 @@
     axes = ("gy", "gz")
     size_z, size_x = 8, lax.axis_size("gz")
     rounds = (
-        [lambda x, y, z, core: (x, y, z, core ^ 1)],
+        [
+            lambda x, y, z, core: (x, y, z, core ^ 1),
+            lambda x, y, z, core: (x, y, z ^ 1, core),
+            lambda x, y, z, core: (x, y, z ^ 1, core ^ 1),
+        ],
         [lambda x, y, z, core, bits=bits: (x ^ bits, y, z, core) for bits in (1, 2, 3)],
         [lambda x, y, z, core, bits=bits: (x, y ^ bits, z, core) for bits in (1, 2, 3)],
-        [lambda x, y, z, core, bits=bits: (x, y, z ^ bits, core) for bits in (1, 2, 3)],
-        [lambda x, y, z, core: (x, y, size_z - 1 - z, core)],
+        [lambda x, y, z, core, far=far: (x, y, (z + far) % size_z, core) for far in (2, -2, 4)],
     )
 
     def partner(move, device):

time: 67.1 us -> 67.6 us (level); the launches traced: 67 us -> 66.4 us
  waiting for transfers between devices: 20.5 us -> 19.1 us
  starting transfers between devices: 28.2 us -> 29.1 us
    ppermute x11 -> x12, waiting for transfers between devices: 15.4 us -> 14.1 us  [device_sum(): lax.ppermute(part, axes, [(device, partner(move, device)) for device in r...]
    ppermute x11 -> x12, starting transfers between devices: 18.5 us -> 19.4 us  [device_sum(): lax.ppermute(part, axes, [(device, partner(move, device)) for device in r...]
  transfers between devices with their start and end apart: 17 -> 18, of which waited for: 9 -> 9; matrix products, arithmetic and copies ran while one was open for 0% -> 0% of each run, Pallas kernels for 4% -> 4%
where the time goes in v7:
time: 67.6 us; the launch traced here: 66.4 us
  starting transfers between devices  29.1 us (43%)
  waiting for transfers between devices  19.1 us (28%)
  Pallas kernels  17.4 us (26%)
  between operations  0.73 us (1%)
    ppermute x12, starting transfers between devices, device_sum(): lax.ppermute(part, axes, [(device, partner(move, device)) for device in r...  19.4 us
    ppermute x12, waiting for transfers between devices, device_sum(): lax.ppermute(part, axes, [(device, partner(move, device)) for device in r...  14.1 us
    pallas_call x1, Pallas kernels, project(): pl.pallas_call(functools.partial(basis_kernel, rows_all=rows_all), out_sh...  8.92 us
    pallas_call x1, Pallas kernels, both_steps(): pl.pallas_call(steps_kernel, out_shape=(f32(3 * rows_y * rows_z, 4 * LANE...  5.05 us
    ppermute x2, waiting for transfers between devices, off_chip(): return lax.ppermute(part, 'gy', list(enumerate(partners)))  5.01 us
    ppermute x2, starting transfers between devices, off_chip(): return lax.ppermute(part, 'gy', list(enumerate(partners)))  4.16 us
    ppermute x2, starting transfers between devices, along_z(): lax.ppermute(part, 'gz', [(i, (i + step) % count_z) for i in range(count_...  3.31 us
    ppermute x2, starting transfers between devices, on_chip(): return lax.ppermute(part, 'gy', [(i, i ^ 1) for i in range(count_y)])  2.21 us
  transfers between devices with their start and end apart: 18, of which 9 were waited for; matrix products, arithmetic and copies ran while one was open for 0% of the time, Pallas kernels for 4%

profile of v7, /device:TPU:32, one launch (start us, length us, event | category | flops | bytes accessed | tf_op | source)
XLA Modules:
  0.0 66.4 jit_solution(5381835545677140636)
XLA Ops:
  0.6 1.1 %edges.1 = (f32[4,4,4,512]{3,2,1,0:T(4,128)S(1)}, f32[4,4,4,512]{3,2,1,0:T(4,128)S(1)}) custom-call(f32[3,4,16,512]{3,2,1,0:T(8,128)} %velocity_ref.2, f32[4,16,512]{2,1,0:T(8,128)} %coef_ref.2), custom_call_target="tpu_custom_call" | custom-call | tf_op jit(solution)/shard_map/edges/pallas_call | solution.py:210
  1.7 1.6 %collective-permute-start.2 = (f32[4,4,4,512]{3,2,1,0:T(4,128)S(1)}, f32[4,4,4,512]{3,2,1,0:T(4,128)S(1)}, u32[]{:S(2)}, u32[]{:S(2)}) collective-permute-start(f32[4,4,4,512]{3,2,1,0:T(4,128)S(1)} %get-tuple-element.18), channel_id=1, source_target_pairs={{0,1},{1,2},{2,3},{3,0},{4,5},{5,6},{6,7},{7,4},{8,9},{9,10},{10,1... | collective-permute-start | bytes 393224 | tf_op jit(solution)/shard_map/ppermute | solution.py:563
  3.3 1.7 %collective-permute-start.3 = (f32[4,4,4,512]{3,2,1,0:T(4,128)S(1)}, f32[4,4,4,512]{3,2,1,0:T(4,128)S(1)}, u32[]{:S(2)}, u32[]{:S(2)}) collective-permute-start(f32[4,4,4,512]{3,2,1,0:T(4,128)S(1)} %get-tuple-element.19), channel_id=1, source_target_pairs={{0,3},{1,0},{2,1},{3,2},{4,7},{5,4},{6,5},{7,6},{8,11},{9,8},{10,9... | collective-permute-start | bytes 393224 | tf_op jit(solution)/shard_map/ppermute | solution.py:563
  5.7 1.9 %collective-permute-start.1 = (f32[4,4,4,16,128]{4,3,2,1,0:T(8,128)S(1)}, f32[4,4,4,16,128]{4,3,2,1,0:T(8,128)S(1)}, u32[]{:S(2)}, u32[]{:S(2)}) collective-permute-start(f32[4,4,4,16,128]{4,3,2,1,0:T(8,128)S(1)} %pack.1.block_ref), channel_id=1, source_target_pairs={{0,0},{4,8},{8,4},{12,16},{16,12},{20,24},{24,20},{28,32},{32,28},... | collective-permute-start | bytes 1572872 | tf_op jit(solution)/shard_map/ppermute | solution.py:570
  7.6 2.1 %collective-permute-start = (f32[4,4,4,16,128]{4,3,2,1,0:T(8,128)S(1)}, f32[4,4,4,16,128]{4,3,2,1,0:T(8,128)S(1)}, u32[]{:S(2)}, u32[]{:S(2)}) collective-permute-start(f32[4,4,4,16,128]{4,3,2,1,0:T(8,128)S(1)} %pack.1.block_ref), channel_id=1, source_target_pairs={{0,4},{4,0},{8,12},{12,8},{16,20},{20,16},{24,28},{28,24},{32,36},... | collective-permute-start | bytes 1572872 | tf_op jit(solution)/shard_map/ppermute | solution.py:566
  10.3 2.2 %collective-permute-start.5 = (f32[4,2,4,8,128]{4,3,2,1,0:T(8,128)S(1)}, f32[4,2,4,8,128]{4,3,2,1,0:T(8,128)S(1)}, u32[]{:S(2)}, u32[]{:S(2)}) collective-permute-start(f32[4,2,4,8,128]{4,3,2,1,0:T(8,128)S(1)} %get-tuple-element.22), channel_id=1, source_target_pairs={{0,0},{4,8},{8,4},{12,16},{16,12},{20,24},{24,20},{28,32},{32,28},... | collective-permute-start | bytes 393224 | tf_op jit(solution)/shard_map/ppermute | solution.py:570
  12.6 5.0 %collective-permute-done.5.side_other_ref = f32[4,2,4,8,128]{4,3,2,1,0:T(8,128)S(1)} collective-permute-done((f32[4,2,4,8,128]{4,3,2,1,0:T(8,128)S(1)}, f32[4,2,4,8,128]{4,3,2,1,0:T(8,128)S(1)}, u32[]{:S(2)}, u32[]{:S(2)}) %collective-permute-start.5) | collective-permute-done | bytes 131104 | tf_op jit(solution)/shard_map/ppermute | solution.py:570
  17.6 5.1 %steps.1 = (f32[192,512]{1,0:T(8,128)S(1)}, f32[2048,128]{1,0:T(8,128)S(1)}, f32[72,128]{1,0:T(8,128)S(1)}) custom-call(s32[128]{0:T(128)S(1)} %copy-done.2, f32[4,4,4,16,128]{4,3,2,1,0:T(8,128)S(1)} %pack.1.block_ref, f32[4,4,4,16,128]{4,3,2,1,0:T(8,128)S(1)} %collective-permute-done.chip_ref, f32[4,4,4,16,128]{4,3,2,1,0:T(8,128)S(1)} %collective-permute-done.1.other_ref, ...), custom_call_target="tpu_custom_call" | custom-call | tf_op jit(solution)/shard_map/steps/pallas_call | solution.py:508
  22.8 1.9 %collective-permute-start.7 = (f32[72,128]{1,0:T(8,128)S(1)}, f32[72,128]{1,0:T(8,128)S(1)}, u32[]{:S(2)}, u32[]{:S(2)}) collective-permute-start(f32[72,128]{1,0:T(8,128)S(1)} %get-tuple-element.24), channel_id=1, source_target_pairs={{0,8},{1,9},{2,10},{3,11},{4,12},{5,13},{6,14},{7,15},{8,0},{9,1},... | collective-permute-start | bytes 110600 | tf_op jit(solution)/shard_map/ppermute | solution.py:552
  24.7 1.5 %collective-permute-done.8 = f32[72,128]{1,0:T(8,128)S(1)} collective-permute-done((f32[72,128]{1,0:T(8,128)S(1)}, f32[72,128]{1,0:T(8,128)S(1)}, u32[]{:S(2)}, u32[]{:S(2)}) %collective-permute-start.8) | collective-permute-done | bytes 36896 | tf_op jit(solution)/shard_map/ppermute | solution.py:552
  26.2 1.2 %collective-permute-done.7 = f32[72,128]{1,0:T(8,128)S(1)} collective-permute-done((f32[72,128]{1,0:T(8,128)S(1)}, f32[72,128]{1,0:T(8,128)S(1)}, u32[]{:S(2)}, u32[]{:S(2)}) %collective-permute-start.7) | collective-permute-done | bytes 36896 | tf_op jit(solution)/shard_map/ppermute | solution.py:552
  27.4 2.0 %collective-permute-start.11 = (f32[72,128]{1,0:T(8,128)S(1)}, f32[72,128]{1,0:T(8,128)S(1)}, u32[]{:S(2)}, u32[]{:S(2)}) collective-permute-start(f32[72,128]{1,0:T(8,128)S(1)} %add_add_fusion.3), channel_id=1, source_target_pairs={{0,3},{1,2},{2,1},{3,0},{4,7},{5,6},{6,5},{7,4},{8,11},{9,10},{10,... | collective-permute-start | bytes 110600 | tf_op jit(solution)/shard_map/ppermute | solution.py:552
  29.8 1.7 %collective-permute-start.9 = (f32[72,128]{1,0:T(8,128)S(1)}, f32[72,128]{1,0:T(8,128)S(1)}, u32[]{:S(2)}, u32[]{:S(2)}) collective-permute-start(f32[72,128]{1,0:T(8,128)S(1)} %add_add_fusion.3), channel_id=1, source_target_pairs={{0,1},{1,0},{2,3},{3,2},{4,5},{5,4},{6,7},{7,6},{8,9},{9,8},{10,11... | collective-permute-start | bytes 110600 | tf_op jit(solution)/shard_map/ppermute | solution.py:552
  31.5 1.5 %collective-permute-done.11 = f32[72,128]{1,0:T(8,128)S(1)} collective-permute-done((f32[72,128]{1,0:T(8,128)S(1)}, f32[72,128]{1,0:T(8,128)S(1)}, u32[]{:S(2)}, u32[]{:S(2)}) %collective-permute-start.11) | collective-permute-done | bytes 36896 | tf_op jit(solution)/shard_map/ppermute | solution.py:552
  33.0 1.8 %collective-permute-done.10 = f32[72,128]{1,0:T(8,128)S(1)} collective-permute-done((f32[72,128]{1,0:T(8,128)S(1)}, f32[72,128]{1,0:T(8,128)S(1)}, u32[]{:S(2)}, u32[]{:S(2)}) %collective-permute-start.10) | collective-permute-done | bytes 36896 | tf_op jit(solution)/shard_map/ppermute | solution.py:552
  34.8 5.5 %collective-permute-start.14 = (f32[72,128]{1,0:T(8,128)S(1)}, f32[72,128]{1,0:T(8,128)S(1)}, u32[]{:S(2)}, u32[]{:S(2)}) collective-permute-start(f32[72,128]{1,0:T(8,128)S(1)} %add_add_fusion.2), channel_id=1, source_target_pairs={{0,192},{1,193},{2,194},{3,195},{4,196},{5,197},{6,198},{7,199},{8... | collective-permute-start | bytes 110600 | tf_op jit(solution)/shard_map/ppermute | solution.py:552
  41.3 1.0 %collective-permute-done.14 = f32[72,128]{1,0:T(8,128)S(1)} collective-permute-done((f32[72,128]{1,0:T(8,128)S(1)}, f32[72,128]{1,0:T(8,128)S(1)}, u32[]{:S(2)}, u32[]{:S(2)}) %collective-permute-start.14) | collective-permute-done | bytes 36896 | tf_op jit(solution)/shard_map/ppermute | solution.py:552
  42.3 3.5 %collective-permute-done.13 = f32[72,128]{1,0:T(8,128)S(1)} collective-permute-done((f32[72,128]{1,0:T(8,128)S(1)}, f32[72,128]{1,0:T(8,128)S(1)}, u32[]{:S(2)}, u32[]{:S(2)}) %collective-permute-start.13) | collective-permute-done | bytes 36896 | tf_op jit(solution)/shard_map/ppermute | solution.py:552
  45.8 3.9 %collective-permute-start.17 = (f32[72,128]{1,0:T(8,128)S(1)}, f32[72,128]{1,0:T(8,128)S(1)}, u32[]{:S(2)}, u32[]{:S(2)}) collective-permute-start(f32[72,128]{1,0:T(8,128)S(1)} %add_add_fusion.1), channel_id=1, source_target_pairs={{0,32},{1,33},{2,34},{3,35},{4,36},{5,37},{6,38},{7,39},{8,40},{9,... | collective-permute-start | bytes 110600 | tf_op jit(solution)/shard_map/ppermute | solution.py:552
  49.7 1.7 %collective-permute-start.16 = (f32[72,128]{1,0:T(8,128)S(1)}, f32[72,128]{1,0:T(8,128)S(1)}, u32[]{:S(2)}, u32[]{:S(2)}) collective-permute-start(f32[72,128]{1,0:T(8,128)S(1)} %add_add_fusion.1), channel_id=1, source_target_pairs={{0,48},{1,49},{2,50},{3,51},{4,52},{5,53},{6,54},{7,55},{8,56},{9,... | collective-permute-start | bytes 110600 | tf_op jit(solution)/shard_map/ppermute | solution.py:552
  51.4 1.2 %collective-permute-start.15 = (f32[72,128]{1,0:T(8,128)S(1)}, f32[72,128]{1,0:T(8,128)S(1)}, u32[]{:S(2)}, u32[]{:S(2)}) collective-permute-start(f32[72,128]{1,0:T(8,128)S(1)} %add_add_fusion.1), channel_id=1, source_target_pairs={{0,16},{1,17},{2,18},{3,19},{4,20},{5,21},{6,22},{7,23},{8,24},{9,... | collective-permute-start | bytes 110600 | tf_op jit(solution)/shard_map/ppermute | solution.py:552
  52.6 1.3 %unsort.1 = f32[3,4,16,512]{3,2,1,0:T(8,128)} custom-call(f32[192,512]{1,0:T(8,128)S(1)} %get-tuple-element.23.wide_ref), custom_call_target="tpu_custom_call" | custom-call | flops 4000000000 | bytes 1000000 | tf_op jit(solution)/shard_map/unsort/pallas_call | solution.py:491
  54.6 2.9 %collective-permute-done.15 = f32[72,128]{1,0:T(8,128)S(1)} collective-permute-done((f32[72,128]{1,0:T(8,128)S(1)}, f32[72,128]{1,0:T(8,128)S(1)}, u32[]{:S(2)}, u32[]{:S(2)}) %collective-permute-start.15) | collective-permute-done | bytes 36896 | tf_op jit(solution)/shard_map/ppermute | solution.py:552
  57.5 8.9 %basis.1 = f32[1344,128]{1,0:T(8,128)} custom-call(f32[72,128]{1,0:T(8,128)S(1)} %add_add_fusion.total_ref, f32[2048,128]{1,0:T(8,128)S(1)} %get-tuple-element.25.snap_ref), custom_call_target="tpu_custom_call" | custom-call | tf_op jit(solution)/shard_map/basis/pallas_call | solution.py:169
  (28 shorter events, 3.5 us)
Async XLA Ops:
  0.6 4.4 %copy-start.1 = (f32[4,16,512]{2,1,0:T(8,128)S(1)}, f32[4,16,512]{2,1,0:T(8,128)}, u32[]{:S(2)}) copy-start(f32[4,16,512]{2,1,0:T(8,128)} %coef_ref.2) | copy-start | bytes 393220
  0.6 4.4 %copy-start = (f32[3,4,16,512]{3,2,1,0:T(8,128)S(1)}, f32[3,4,16,512]{3,2,1,0:T(8,128)}, u32[]{:S(2)}) copy-start(f32[3,4,16,512]{3,2,1,0:T(8,128)} %velocity_ref.2) | copy-start | bytes 1179652
  1.7 8.0 %collective-permute-start.2 = (f32[4,4,4,512]{3,2,1,0:T(4,128)S(1)}, f32[4,4,4,512]{3,2,1,0:T(4,128)S(1)}, u32[]{:S(2)}, u32[]{:S(2)}) collective-permute-start(f32[4,4,4,512]{3,2,1,0:T(4,128)S(1)} %get-tuple-element.18), channel_id=1, source_target_pairs={{0,1},{1,2},{2,3},{3,0},{4,5},{5,6},{6,7},{7,4},{8,9},{9,10},{10,1... | collective-permute-start | bytes 393224 | tf_op jit(solution)/shard_map/ppermute | solution.py:563
  3.3 6.4 %collective-permute-start.3 = (f32[4,4,4,512]{3,2,1,0:T(4,128)S(1)}, f32[4,4,4,512]{3,2,1,0:T(4,128)S(1)}, u32[]{:S(2)}, u32[]{:S(2)}) collective-permute-start(f32[4,4,4,512]{3,2,1,0:T(4,128)S(1)} %get-tuple-element.19), channel_id=1, source_target_pairs={{0,3},{1,0},{2,1},{3,2},{4,7},{5,4},{6,5},{7,6},{8,11},{9,8},{10,9... | collective-permute-start | bytes 393224 | tf_op jit(solution)/shard_map/ppermute | solution.py:563
  5.7 11.9 %collective-permute-start.1 = (f32[4,4,4,16,128]{4,3,2,1,0:T(8,128)S(1)}, f32[4,4,4,16,128]{4,3,2,1,0:T(8,128)S(1)}, u32[]{:S(2)}, u32[]{:S(2)}) collective-permute-start(f32[4,4,4,16,128]{4,3,2,1,0:T(8,128)S(1)} %pack.1.block_ref), channel_id=1, source_target_pairs={{0,0},{4,8},{8,4},{12,16},{16,12},{20,24},{24,20},{28,32},{32,28},... | collective-permute-start | bytes 1572872 | tf_op jit(solution)/shard_map/ppermute | solution.py:570
  7.6 10.0 %collective-permute-start = (f32[4,4,4,16,128]{4,3,2,1,0:T(8,128)S(1)}, f32[4,4,4,16,128]{4,3,2,1,0:T(8,128)S(1)}, u32[]{:S(2)}, u32[]{:S(2)}) collective-permute-start(f32[4,4,4,16,128]{4,3,2,1,0:T(8,128)S(1)} %pack.1.block_ref), channel_id=1, source_target_pairs={{0,4},{4,0},{8,12},{12,8},{16,20},{20,16},{24,28},{28,24},{32,36},... | collective-permute-start | bytes 1572872 | tf_op jit(solution)/shard_map/ppermute | solution.py:566
  10.2 2.4 %collective-permute-start.4 = (f32[4,2,4,8,128]{4,3,2,1,0:T(8,128)S(1)}, f32[4,2,4,8,128]{4,3,2,1,0:T(8,128)S(1)}, u32[]{:S(2)}, u32[]{:S(2)}) collective-permute-start(f32[4,2,4,8,128]{4,3,2,1,0:T(8,128)S(1)} %get-tuple-element.21), channel_id=1, source_target_pairs={{0,4},{4,0},{8,12},{12,8},{16,20},{20,16},{24,28},{28,24},{32,36},... | collective-permute-start | bytes 393224 | tf_op jit(solution)/shard_map/ppermute | solution.py:566
  10.3 7.3 %copy-start.2 = (s32[128]{0:T(128)S(1)}, s32[128]{0:T(128)}, u32[]{:S(2)}) copy-start(s32[128]{0:T(128)} %code_ref.1) | copy-start | bytes 1540
  10.3 7.3 %collective-permute-start.5 = (f32[4,2,4,8,128]{4,3,2,1,0:T(8,128)S(1)}, f32[4,2,4,8,128]{4,3,2,1,0:T(8,128)S(1)}, u32[]{:S(2)}, u32[]{:S(2)}) collective-permute-start(f32[4,2,4,8,128]{4,3,2,1,0:T(8,128)S(1)} %get-tuple-element.22), channel_id=1, source_target_pairs={{0,0},{4,8},{8,4},{12,16},{16,12},{20,24},{24,20},{28,32},{32,28},... | collective-permute-start | bytes 393224 | tf_op jit(solution)/shard_map/ppermute | solution.py:570
  22.7 3.5 %collective-permute-start.8 = (f32[72,128]{1,0:T(8,128)S(1)}, f32[72,128]{1,0:T(8,128)S(1)}, u32[]{:S(2)}, u32[]{:S(2)}) collective-permute-start(f32[72,128]{1,0:T(8,128)S(1)} %get-tuple-element.24), channel_id=1, source_target_pairs={{0,12},{1,13},{2,14},{3,15},{4,8},{5,9},{6,10},{7,11},{8,4},{9,5},... | collective-permute-start | bytes 110600 | tf_op jit(solution)/shard_map/ppermute | solution.py:552
  22.8 4.6 %collective-permute-start.7 = (f32[72,128]{1,0:T(8,128)S(1)}, f32[72,128]{1,0:T(8,128)S(1)}, u32[]{:S(2)}, u32[]{:S(2)}) collective-permute-start(f32[72,128]{1,0:T(8,128)S(1)} %get-tuple-element.24), channel_id=1, source_target_pairs={{0,8},{1,9},{2,10},{3,11},{4,12},{5,13},{6,14},{7,15},{8,0},{9,1},... | collective-permute-start | bytes 110600 | tf_op jit(solution)/shard_map/ppermute | solution.py:552
  24.7 2.7 %collective-permute-start.6 = (f32[72,128]{1,0:T(8,128)S(1)}, f32[72,128]{1,0:T(8,128)S(1)}, u32[]{:S(2)}, u32[]{:S(2)}) collective-permute-start(f32[72,128]{1,0:T(8,128)S(1)} %get-tuple-element.24), channel_id=1, source_target_pairs={{0,4},{1,5},{2,6},{3,7},{4,0},{5,1},{6,2},{7,3},{8,12},{9,13},{10,... | collective-permute-start | bytes 110600 | tf_op jit(solution)/shard_map/ppermute | solution.py:552
  27.4 5.7 %collective-permute-start.11 = (f32[72,128]{1,0:T(8,128)S(1)}, f32[72,128]{1,0:T(8,128)S(1)}, u32[]{:S(2)}, u32[]{:S(2)}) collective-permute-start(f32[72,128]{1,0:T(8,128)S(1)} %add_add_fusion.3), channel_id=1, source_target_pairs={{0,3},{1,2},{2,1},{3,0},{4,7},{5,6},{6,5},{7,4},{8,11},{9,10},{10,... | collective-permute-start | bytes 110600 | tf_op jit(solution)/shard_map/ppermute | solution.py:552
  29.4 5.5 %collective-permute-start.10 = (f32[72,128]{1,0:T(8,128)S(1)}, f32[72,128]{1,0:T(8,128)S(1)}, u32[]{:S(2)}, u32[]{:S(2)}) collective-permute-start(f32[72,128]{1,0:T(8,128)S(1)} %add_add_fusion.3), channel_id=1, source_target_pairs={{0,2},{1,3},{2,0},{3,1},{4,6},{5,7},{6,4},{7,5},{8,10},{9,11},{10,... | collective-permute-start | bytes 110600 | tf_op jit(solution)/shard_map/ppermute | solution.py:552
  29.8 5.0 %collective-permute-start.9 = (f32[72,128]{1,0:T(8,128)S(1)}, f32[72,128]{1,0:T(8,128)S(1)}, u32[]{:S(2)}, u32[]{:S(2)}) collective-permute-start(f32[72,128]{1,0:T(8,128)S(1)} %add_add_fusion.3), channel_id=1, source_target_pairs={{0,1},{1,0},{2,3},{3,2},{4,5},{5,4},{6,7},{7,6},{8,9},{9,8},{10,11... | collective-permute-start | bytes 110600 | tf_op jit(solution)/shard_map/ppermute | solution.py:552
  34.8 7.4 %collective-permute-start.14 = (f32[72,128]{1,0:T(8,128)S(1)}, f32[72,128]{1,0:T(8,128)S(1)}, u32[]{:S(2)}, u32[]{:S(2)}) collective-permute-start(f32[72,128]{1,0:T(8,128)S(1)} %add_add_fusion.2), channel_id=1, source_target_pairs={{0,192},{1,193},{2,194},{3,195},{4,196},{5,197},{6,198},{7,199},{8... | collective-permute-start | bytes 110600 | tf_op jit(solution)/shard_map/ppermute | solution.py:552
  40.3 5.5 %collective-permute-start.13 = (f32[72,128]{1,0:T(8,128)S(1)}, f32[72,128]{1,0:T(8,128)S(1)}, u32[]{:S(2)}, u32[]{:S(2)}) collective-permute-start(f32[72,128]{1,0:T(8,128)S(1)} %add_add_fusion.2), channel_id=1, source_target_pairs={{0,128},{1,129},{2,130},{3,131},{4,132},{5,133},{6,134},{7,135},{8... | collective-permute-start | bytes 110600 | tf_op jit(solution)/shard_map/ppermute | solution.py:552
  40.7 5.1 %collective-permute-start.12 = (f32[72,128]{1,0:T(8,128)S(1)}, f32[72,128]{1,0:T(8,128)S(1)}, u32[]{:S(2)}, u32[]{:S(2)}) collective-permute-start(f32[72,128]{1,0:T(8,128)S(1)} %add_add_fusion.2), channel_id=1, source_target_pairs={{0,64},{1,65},{2,66},{3,67},{4,68},{5,69},{6,70},{7,71},{8,72},{9,... | collective-permute-start | bytes 110600 | tf_op jit(solution)/shard_map/ppermute | solution.py:552
  45.8 8.1 %collective-permute-start.17 = (f32[72,128]{1,0:T(8,128)S(1)}, f32[72,128]{1,0:T(8,128)S(1)}, u32[]{:S(2)}, u32[]{:S(2)}) collective-permute-start(f32[72,128]{1,0:T(8,128)S(1)} %add_add_fusion.1), channel_id=1, source_target_pairs={{0,32},{1,33},{2,34},{3,35},{4,36},{5,37},{6,38},{7,39},{8,40},{9,... | collective-permute-start | bytes 110600 | tf_op jit(solution)/shard_map/ppermute | solution.py:552
  49.7 4.9 %collective-permute-start.16 = (f32[72,128]{1,0:T(8,128)S(1)}, f32[72,128]{1,0:T(8,128)S(1)}, u32[]{:S(2)}, u32[]{:S(2)}) collective-permute-start(f32[72,128]{1,0:T(8,128)S(1)} %add_add_fusion.1), channel_id=1, source_target_pairs={{0,48},{1,49},{2,50},{3,51},{4,52},{5,53},{6,54},{7,55},{8,56},{9,... | collective-permute-start | bytes 110600 | tf_op jit(solution)/shard_map/ppermute | solution.py:552
  51.4 6.1 %collective-permute-start.15 = (f32[72,128]{1,0:T(8,128)S(1)}, f32[72,128]{1,0:T(8,128)S(1)}, u32[]{:S(2)}, u32[]{:S(2)}) collective-permute-start(f32[72,128]{1,0:T(8,128)S(1)} %add_add_fusion.1), channel_id=1, source_target_pairs={{0,16},{1,17},{2,18},{3,19},{4,20},{5,21},{6,22},{7,23},{8,24},{9,... | collective-permute-start | bytes 110600 | tf_op jit(solution)/shard_map/ppermute | solution.py:552

commit v8 on v7

--- a/solution.py
+++ b/solution.py
@@ -189,7 +189,7 @@
     return jnp.where(place == spot, 1.0, 0.0).astype(jnp.bfloat16)
 
 
-def edges_kernel(velocity_ref, coef_ref, low_ref, high_ref, arrived):
+def edges_kernel(velocity_ref, coef_ref, low_ref, high_ref, far_low_ref, far_high_ref, arrived):
     layers, rows_z = low_ref.shape[2], coef_ref.shape[1]
     copies = []
     for n, (edge_ref, start) in enumerate(((low_ref, 0), (high_ref, rows_z - layers))):
@@ -202,16 +202,28 @@
         copy.start()
     for copy in copies:
         copy.wait()
+    odd = lax.axis_index("gy") % 2 == 1
+    rows_y = coef_ref.shape[0]
+    for c in range(4):
+        for away in range(rows_y - 1):
+            low = jnp.where(odd, low_ref[c, rows_y - 1 - away], low_ref[c, away])
+            high = jnp.where(odd, high_ref[c, rows_y - 1 - away], high_ref[c, away])
+            if away == 0:
+                far_low_ref[c, :layers], far_high_ref[c, :layers] = low, high
+            else:
+                rows = slice(layers + 2 * (away - 1), layers + 2 * away)
+                far_low_ref[c, rows], far_high_ref[c, rows] = low[:2], high[2:]
 
 
 def edges(velocity, smag_coef):
     rows_y, _, size_x = smag_coef.shape
     edge = jax.ShapeDtypeStruct((4, rows_y, 4, size_x), jnp.float32)
+    far = jax.ShapeDtypeStruct((4, 8, size_x), jnp.float32)
     return pl.pallas_call(
         edges_kernel,
-        out_shape=(edge, edge),
+        out_shape=(edge, edge, far, far),
         in_specs=[pl.BlockSpec(memory_space=pltpu.HBM)] * 2,
-        out_specs=[pl.BlockSpec(memory_space=pltpu.VMEM)] * 2,
+        out_specs=[pl.BlockSpec(memory_space=pltpu.VMEM)] * 4,
         scratch_shapes=[pltpu.SemaphoreType.DMA((4,))],
         compiler_params=pltpu.CompilerParams(vmem_limit_bytes=2 * 2**20),
         name="edges",
@@ -241,7 +253,7 @@
     )(velocity, smag_coef)
 
 
-def sides_kernel(low_ref, high_ref, sides_ref, chip_ref, other_ref):
+def sides_kernel(low_ref, high_ref, sides_ref, chip_ref):
     odd = lax.axis_index("gy") % 2 == 1
     rows_y, layers, size_x = low_ref.shape[1:]
     rows = jnp.concatenate([high_ref[...], low_ref[...]], axis=2).reshape(-1, size_x)
@@ -252,15 +264,13 @@
             for y in range(rows_y):
                 sides_ref[c, y, o] = planes[y]
             for away in range(rows_y - 1):
-                upper, lower = planes[rows_y - 1 - away], planes[away]
-                on_chip, off_chip = jnp.where(odd, lower, upper), jnp.where(odd, upper, lower)
-                for ref, plane in ((chip_ref, on_chip), (other_ref, off_chip)):
-                    if away == 0:
-                        ref[c, 0, o] = plane
-                    else:
-                        for side, begin in enumerate((0, layers + 2)):
-                            to = 4 * (away - 1) + 2 * side
-                            ref[c, 1, o, to : to + 2] = plane[begin : begin + 2]
+                plane = jnp.where(odd, planes[away], planes[rows_y - 1 - away])
+                if away == 0:
+                    chip_ref[c, 0, o] = plane
+                else:
+                    for side, begin in enumerate((0, layers + 2)):
+                        to = 4 * (away - 1) + 2 * side
+                        chip_ref[c, 1, o, to : to + 2] = plane[begin : begin + 2]
 
 
 def sort_sides(low, high):
@@ -268,12 +278,37 @@
     shape = lambda rows: jax.ShapeDtypeStruct((4, rows, 4, 2 * layers, LANES), jnp.float32)
     return pl.pallas_call(
         sides_kernel,
-        out_shape=(shape(rows_y), shape(2), shape(2)),
+        out_shape=(shape(rows_y), shape(2)),
         in_specs=[pl.BlockSpec(memory_space=pltpu.VMEM)] * 2,
-        out_specs=[pl.BlockSpec(memory_space=pltpu.VMEM)] * 3,
+        out_specs=[pl.BlockSpec(memory_space=pltpu.VMEM)] * 2,
         compiler_params=pltpu.CompilerParams(vmem_limit_bytes=12 * 2**20),
         cost_estimate=pl.CostEstimate(flops=2 * 10**10, bytes_accessed=10**6, transcendentals=0),
         name="sides",
+    )(low, high)
+
+
+def corners_kernel(low_ref, high_ref, other_ref):
+    size_x = low_ref.shape[-1]
+    low, high = low_ref[...], high_ref[...]
+    near = jnp.concatenate([high[:, :4], low[:, :4]], axis=1)
+    away = jnp.concatenate([high[:, 4:6], low[:, 4:6], high[:, 6:8], low[:, 6:8]], axis=1)
+    rows = jnp.concatenate([near.reshape(-1, size_x), away.reshape(-1, size_x)])
+    done = exact_dot(rows, sorting(size_x, True)).reshape(2, 4, 8, size_x)
+    for c in range(4):
+        for tile in range(2):
+            for o in range(4):
+                other_ref[c, tile, o] = done[tile, c, :, LANES * o : LANES * (o + 1)]
+
+
+def sort_corners(low, high):
+    return pl.pallas_call(
+        corners_kernel,
+        out_shape=jax.ShapeDtypeStruct((4, 2, 4, 8, LANES), jnp.float32),
+        in_specs=[pl.BlockSpec(memory_space=pltpu.VMEM)] * 2,
+        out_specs=pl.BlockSpec(memory_space=pltpu.VMEM),
+        compiler_params=pltpu.CompilerParams(vmem_limit_bytes=12 * 2**20),
+        cost_estimate=pl.CostEstimate(flops=15 * 10**9, bytes_accessed=10**6, transcendentals=0),
+        name="corners",
     )(low, high)
 
 
@@ -531,14 +566,11 @@
     axes = ("gy", "gz")
     size_z, size_x = 8, lax.axis_size("gz")
     rounds = (
-        [
-            lambda x, y, z, core: (x, y, z, core ^ 1),
-            lambda x, y, z, core: (x, y, z ^ 1, core),
-            lambda x, y, z, core: (x, y, z ^ 1, core ^ 1),
-        ],
+        [lambda x, y, z, core: (x, y, z, core ^ 1)],
         [lambda x, y, z, core, bits=bits: (x ^ bits, y, z, core) for bits in (1, 2, 3)],
         [lambda x, y, z, core, bits=bits: (x, y ^ bits, z, core) for bits in (1, 2, 3)],
-        [lambda x, y, z, core, far=far: (x, y, (z + far) % size_z, core) for far in (2, -2, 4)],
+        [lambda x, y, z, core, bits=bits: (x, y, z ^ bits, core) for bits in (1, 2, 3)],
+        [lambda x, y, z, core: (x, y, size_z - 1 - z, core)],
     )
 
     def partner(move, device):
@@ -565,16 +597,23 @@
     def on_chip(part):
         return lax.ppermute(part, "gy", [(i, i ^ 1) for i in range(count_y)])
 
-    def off_chip(part):
-        partners = [min(max(((i + 1) ^ 1) - 1, 0), count_y - 1) for i in range(count_y)]
-        return lax.ppermute(part, "gy", list(enumerate(partners)))
-
-    low, high = edges(velocity, smag_coef)
-    velocity, smag_coef, low, high = lax.optimization_barrier((velocity, smag_coef, low, high))
-    sides, side_chip, side_other = sort_sides(along_z(high, 1), along_z(low, -1))
+    def off_chip(part, step=0):
+        pairs = [
+            (y * count_z + z, min(max(((y + 1) ^ 1) - 1, 0), count_y - 1) * count_z + (z + step) % count_z)
+            for y in range(count_y)
+            for z in range(count_z)
+        ]
+        return lax.ppermute(part, ("gy", "gz"), pairs)
+
+    low, high, far_low, far_high = edges(velocity, smag_coef)
+    velocity, smag_coef, low, high, far_low, far_high = lax.optimization_barrier(
+        (velocity, smag_coef, low, high, far_low, far_high)
+    )
+    sides, side_chip = sort_sides(along_z(high, 1), along_z(low, -1))
+    side_other = sort_corners(off_chip(far_high, 1), off_chip(far_low, -1))
     block = pack(velocity, smag_coef)
     wide, snapshots, gram = both_steps(
-        snap_code, block, on_chip(block), off_chip(block), sides, on_chip(side_chip), off_chip(side_other)
+        snap_code, block, on_chip(block), off_chip(block), sides, on_chip(side_chip), side_other
     )
     rows_y, rows_z = velocity.shape[1], velocity.shape[2]
     rows_all = 12 * LANES * count_y * count_z

time: 67.6 us -> 68.7 us (1.016); the launches traced: 66.4 us -> 68.5 us
  waiting for transfers between devices: 19.1 us -> 19.8 us
    ppermute x12 -> x11, waiting for transfers between devices: 14.1 us -> 15.9 us  [device_sum(): lax.ppermute(part, axes, [(device, partner(move, device)) for device in r...]
    ppermute x2 -> x3, starting transfers between devices: 4.16 us -> 5.78 us  [off_chip(): return lax.ppermute(part, ('gy', 'gz'), pairs)]
    ppermute x12 -> x11, starting transfers between devices: 19.4 us -> 18 us  [device_sum(): lax.ppermute(part, axes, [(device, partner(move, device)) for device in r...]
    ppermute x2 -> x3, waiting for transfers between devices: 5.01 us -> 3.87 us  [off_chip(): return lax.ppermute(part, ('gy', 'gz'), pairs)]
    pallas_call x2 -> x3, Pallas kernels: 1.54 us -> 2.01 us  [the longest x1 1.09 us: edges(): pl.pallas_call(edges_kernel, out_shape=(edge, edge, far, far), in_specs=[...]
where the time goes in v8:
time: 68.7 us; the launch traced here: 68.5 us
  starting transfers between devices  29.4 us (43%)
  waiting for transfers between devices  19.8 us (29%)
  Pallas kernels  17.9 us (26%)
  between operations  0.74 us (1%)
    ppermute x11, starting transfers between devices, device_sum(): lax.ppermute(part, axes, [(device, partner(move, device)) for device in r...  18 us
    ppermute x11, waiting for transfers between devices, device_sum(): lax.ppermute(part, axes, [(device, partner(move, device)) for device in r...  15.9 us
    pallas_call x1, Pallas kernels, project(): pl.pallas_call(functools.partial(basis_kernel, rows_all=rows_all), out_sh...  8.91 us
    ppermute x3, starting transfers between devices, off_chip(): return lax.ppermute(part, ('gy', 'gz'), pairs)  5.78 us
    pallas_call x1, Pallas kernels, both_steps(): pl.pallas_call(steps_kernel, out_shape=(f32(3 * rows_y * rows_z, 4 * LANE...  5.05 us
    ppermute x3, waiting for transfers between devices, off_chip(): return lax.ppermute(part, ('gy', 'gz'), pairs)  3.87 us
    ppermute x2, starting transfers between devices, along_z(): lax.ppermute(part, 'gz', [(i, (i + step) % count_z) for i in range(count_...  3.31 us
    ppermute x2, starting transfers between devices, on_chip(): return lax.ppermute(part, 'gy', [(i, i ^ 1) for i in range(count_y)])  2.28 us
  transfers between devices with their start and end apart: 18, of which 9 were waited for; matrix products, arithmetic and copies ran while one was open for 0% of the time, Pallas kernels for 4%

profile of v8, /device:TPU:32, one launch (start us, length us, event | category | flops | bytes accessed | tf_op | source)
XLA Modules:
  0.0 68.5 jit_solution(12431191353819741600)
XLA Ops:
  0.6 1.1 %edges.1 = (f32[4,4,4,512]{3,2,1,0:T(4,128)S(1)}, f32[4,4,4,512]{3,2,1,0:T(4,128)S(1)}, f32[4,8,512]{2,1,0:T(8,128)S(1)}, f32[4,8,512]{2,1,0:T(8,128)S(1)}) custom-call(f32[3,4,16,512]{3,2,1,0:T(8,128)} %velocity_ref.2, f32[4,16,512]{2,1,0:T(8,128)} %coef_ref.2), custom_call_target="tpu_custom_call" | custom-call | tf_op jit(solution)/shard_map/edges/pallas_call | solution.py:222
  1.7 1.6 %collective-permute-start.2 = (f32[4,4,4,512]{3,2,1,0:T(4,128)S(1)}, f32[4,4,4,512]{3,2,1,0:T(4,128)S(1)}, u32[]{:S(2)}, u32[]{:S(2)}) collective-permute-start(f32[4,4,4,512]{3,2,1,0:T(4,128)S(1)} %get-tuple-element.23), channel_id=1, source_target_pairs={{0,1},{1,2},{2,3},{3,0},{4,5},{5,6},{6,7},{7,4},{8,9},{9,10},{10,1... | collective-permute-start | bytes 393224 | tf_op jit(solution)/shard_map/ppermute | solution.py:595
  3.3 1.7 %collective-permute-start.3 = (f32[4,4,4,512]{3,2,1,0:T(4,128)S(1)}, f32[4,4,4,512]{3,2,1,0:T(4,128)S(1)}, u32[]{:S(2)}, u32[]{:S(2)}) collective-permute-start(f32[4,4,4,512]{3,2,1,0:T(4,128)S(1)} %get-tuple-element.24), channel_id=1, source_target_pairs={{0,3},{1,0},{2,1},{3,2},{4,7},{5,4},{6,5},{7,6},{8,11},{9,8},{10,9... | collective-permute-start | bytes 393224 | tf_op jit(solution)/shard_map/ppermute | solution.py:595
  5.7 1.9 %collective-permute-start.1 = (f32[4,4,4,16,128]{4,3,2,1,0:T(8,128)S(1)}, f32[4,4,4,16,128]{4,3,2,1,0:T(8,128)S(1)}, u32[]{:S(2)}, u32[]{:S(2)}) collective-permute-start(f32[4,4,4,16,128]{4,3,2,1,0:T(8,128)S(1)} %pack.1.block_ref), channel_id=1, source_target_pairs={{0,0},{1,1},{2,2},{3,3},{4,8},{5,9},{6,10},{7,11},{8,4},{9,5},{10,... | collective-permute-start | bytes 1572872 | tf_op jit(solution)/shard_map/ppermute | solution.py:606
  7.7 2.1 %collective-permute-start = (f32[4,4,4,16,128]{4,3,2,1,0:T(8,128)S(1)}, f32[4,4,4,16,128]{4,3,2,1,0:T(8,128)S(1)}, u32[]{:S(2)}, u32[]{:S(2)}) collective-permute-start(f32[4,4,4,16,128]{4,3,2,1,0:T(8,128)S(1)} %pack.1.block_ref), channel_id=1, source_target_pairs={{0,4},{4,0},{8,12},{12,8},{16,20},{20,16},{24,28},{28,24},{32,36},... | collective-permute-start | bytes 1572872 | tf_op jit(solution)/shard_map/ppermute | solution.py:598
  9.8 3.9 %collective-permute-start.6 = (f32[4,8,512]{2,1,0:T(8,128)S(1)}, f32[4,8,512]{2,1,0:T(8,128)S(1)}, u32[]{:S(2)}, u32[]{:S(2)}) collective-permute-start(f32[4,8,512]{2,1,0:T(8,128)S(1)} %get-tuple-element.28), channel_id=1, source_target_pairs={{0,3},{1,0},{2,1},{3,2},{4,11},{5,8},{6,9},{7,10},{8,7},{9,4},{10,... | collective-permute-start | bytes 196616 | tf_op jit(solution)/shard_map/ppermute | solution.py:606
  14.3 3.9 %collective-permute-done.5.low_ref = f32[4,8,512]{2,1,0:T(8,128)S(1)} collective-permute-done((f32[4,8,512]{2,1,0:T(8,128)S(1)}, f32[4,8,512]{2,1,0:T(8,128)S(1)}, u32[]{:S(2)}, u32[]{:S(2)}) %collective-permute-start.5) | collective-permute-done | bytes 65568 | tf_op jit(solution)/shard_map/ppermute | solution.py:606
  19.3 5.0 %steps.1 = (f32[192,512]{1,0:T(8,128)S(1)}, f32[2048,128]{1,0:T(8,128)S(1)}, f32[72,128]{1,0:T(8,128)S(1)}) custom-call(s32[128]{0:T(128)S(1)} %copy-done.2, f32[4,4,4,16,128]{4,3,2,1,0:T(8,128)S(1)} %pack.1.block_ref, f32[4,4,4,16,128]{4,3,2,1,0:T(8,128)S(1)} %collective-permute-done.chip_ref, f32[4,4,4,16,128]{4,3,2,1,0:T(8,128)S(1)} %collective-permute-done.1.other_ref, ...), custom_call_target="tpu_custom_call" | custom-call | tf_op jit(solution)/shard_map/steps/pallas_call | solution.py:543
  24.7 0.9 %collective-permute-done.7 = f32[72,128]{1,0:T(8,128)S(1)} collective-permute-done((f32[72,128]{1,0:T(8,128)S(1)}, f32[72,128]{1,0:T(8,128)S(1)}, u32[]{:S(2)}, u32[]{:S(2)}) %collective-permute-start.7) | collective-permute-done | bytes 36896 | tf_op jit(solution)/shard_map/ppermute | solution.py:584
  25.6 2.4 %collective-permute-start.10 = (f32[72,128]{1,0:T(8,128)S(1)}, f32[72,128]{1,0:T(8,128)S(1)}, u32[]{:S(2)}, u32[]{:S(2)}) collective-permute-start(f32[72,128]{1,0:T(8,128)S(1)} %add.33), channel_id=1, source_target_pairs={{0,3},{1,2},{2,1},{3,0},{4,7},{5,6},{6,5},{7,4},{8,11},{9,10},{10,... | collective-permute-start | bytes 110600 | tf_op jit(solution)/shard_map/ppermute | solution.py:584
  28.6 1.1 %collective-permute-start.8 = (f32[72,128]{1,0:T(8,128)S(1)}, f32[72,128]{1,0:T(8,128)S(1)}, u32[]{:S(2)}, u32[]{:S(2)}) collective-permute-start(f32[72,128]{1,0:T(8,128)S(1)} %add.33), channel_id=1, source_target_pairs={{0,1},{1,0},{2,3},{3,2},{4,5},{5,4},{6,7},{7,6},{8,9},{9,8},{10,11... | collective-permute-start | bytes 110600 | tf_op jit(solution)/shard_map/ppermute | solution.py:584
  29.7 1.1 %collective-permute-done.10 = f32[72,128]{1,0:T(8,128)S(1)} collective-permute-done((f32[72,128]{1,0:T(8,128)S(1)}, f32[72,128]{1,0:T(8,128)S(1)}, u32[]{:S(2)}, u32[]{:S(2)}) %collective-permute-start.10) | collective-permute-done | bytes 36896 | tf_op jit(solution)/shard_map/ppermute | solution.py:584
  30.8 2.7 %collective-permute-done.9 = f32[72,128]{1,0:T(8,128)S(1)} collective-permute-done((f32[72,128]{1,0:T(8,128)S(1)}, f32[72,128]{1,0:T(8,128)S(1)}, u32[]{:S(2)}, u32[]{:S(2)}) %collective-permute-start.9) | collective-permute-done | bytes 36896 | tf_op jit(solution)/shard_map/ppermute | solution.py:584
  33.5 4.1 %collective-permute-start.13 = (f32[72,128]{1,0:T(8,128)S(1)}, f32[72,128]{1,0:T(8,128)S(1)}, u32[]{:S(2)}, u32[]{:S(2)}) collective-permute-start(f32[72,128]{1,0:T(8,128)S(1)} %add_add_fusion.2), channel_id=1, source_target_pairs={{0,192},{1,193},{2,194},{3,195},{4,196},{5,197},{6,198},{7,199},{8... | collective-permute-start | bytes 110600 | tf_op jit(solution)/shard_map/ppermute | solution.py:584
  38.5 1.0 %collective-permute-done.13 = f32[72,128]{1,0:T(8,128)S(1)} collective-permute-done((f32[72,128]{1,0:T(8,128)S(1)}, f32[72,128]{1,0:T(8,128)S(1)}, u32[]{:S(2)}, u32[]{:S(2)}) %collective-permute-start.13) | collective-permute-done | bytes 36896 | tf_op jit(solution)/shard_map/ppermute | solution.py:584
  39.5 3.5 %collective-permute-done.12 = f32[72,128]{1,0:T(8,128)S(1)} collective-permute-done((f32[72,128]{1,0:T(8,128)S(1)}, f32[72,128]{1,0:T(8,128)S(1)}, u32[]{:S(2)}, u32[]{:S(2)}) %collective-permute-start.12) | collective-permute-done | bytes 36896 | tf_op jit(solution)/shard_map/ppermute | solution.py:584
  43.0 1.7 %collective-permute-start.16 = (f32[72,128]{1,0:T(8,128)S(1)}, f32[72,128]{1,0:T(8,128)S(1)}, u32[]{:S(2)}, u32[]{:S(2)}) collective-permute-start(f32[72,128]{1,0:T(8,128)S(1)} %add_add_fusion.1), channel_id=1, source_target_pairs={{0,24},{1,25},{2,26},{3,27},{4,28},{5,29},{6,30},{7,31},{8,16},{9,... | collective-permute-start | bytes 110600 | tf_op jit(solution)/shard_map/ppermute | solution.py:584
  44.7 3.9 %collective-permute-start.15 = (f32[72,128]{1,0:T(8,128)S(1)}, f32[72,128]{1,0:T(8,128)S(1)}, u32[]{:S(2)}, u32[]{:S(2)}) collective-permute-start(f32[72,128]{1,0:T(8,128)S(1)} %add_add_fusion.1), channel_id=1, source_target_pairs={{0,16},{1,17},{2,18},{3,19},{4,20},{5,21},{6,22},{7,23},{8,24},{9,... | collective-permute-start | bytes 110600 | tf_op jit(solution)/shard_map/ppermute | solution.py:584
  48.6 2.3 %collective-permute-done.15 = f32[72,128]{1,0:T(8,128)S(1)} collective-permute-done((f32[72,128]{1,0:T(8,128)S(1)}, f32[72,128]{1,0:T(8,128)S(1)}, u32[]{:S(2)}, u32[]{:S(2)}) %collective-permute-start.15) | collective-permute-done | bytes 36896 | tf_op jit(solution)/shard_map/ppermute | solution.py:584
  50.9 1.6 %collective-permute-done.14 = f32[72,128]{1,0:T(8,128)S(1)} collective-permute-done((f32[72,128]{1,0:T(8,128)S(1)}, f32[72,128]{1,0:T(8,128)S(1)}, u32[]{:S(2)}, u32[]{:S(2)}) %collective-permute-start.14) | collective-permute-done | bytes 36896 | tf_op jit(solution)/shard_map/ppermute | solution.py:584
  52.5 3.0 %collective-permute-start.17 = (f32[72,128]{1,0:T(8,128)S(1)}, f32[72,128]{1,0:T(8,128)S(1)}, u32[]{:S(2)}, u32[]{:S(2)}) collective-permute-start(f32[72,128]{1,0:T(8,128)S(1)} %add_add_fusion), channel_id=1, source_target_pairs={{0,56},{1,57},{2,58},{3,59},{4,60},{5,61},{6,62},{7,63},{8,48},{9,... | collective-permute-start | bytes 110600 | tf_op jit(solution)/shard_map/ppermute | solution.py:584
  55.5 1.3 %unsort.1 = f32[3,4,16,512]{3,2,1,0:T(8,128)} custom-call(f32[192,512]{1,0:T(8,128)S(1)} %get-tuple-element.29.wide_ref), custom_call_target="tpu_custom_call" | custom-call | flops 4000000000 | bytes 1000000 | tf_op jit(solution)/shard_map/unsort/pallas_call | solution.py:526
  56.8 2.8 %collective-permute-done.17 = f32[72,128]{1,0:T(8,128)S(1)} collective-permute-done((f32[72,128]{1,0:T(8,128)S(1)}, f32[72,128]{1,0:T(8,128)S(1)}, u32[]{:S(2)}, u32[]{:S(2)}) %collective-permute-start.17) | collective-permute-done | bytes 36896 | tf_op jit(solution)/shard_map/ppermute | solution.py:584
  59.6 8.9 %basis.1 = f32[1344,128]{1,0:T(8,128)} custom-call(f32[72,128]{1,0:T(8,128)S(1)} %add.43.total_ref, f32[2048,128]{1,0:T(8,128)S(1)} %get-tuple-element.31.snap_ref), custom_call_target="tpu_custom_call" | custom-call | tf_op jit(solution)/shard_map/basis/pallas_call | solution.py:169
  (30 shorter events, 4.4 us)
Async XLA Ops:
  0.6 4.4 %copy-start.1 = (f32[4,16,512]{2,1,0:T(8,128)S(1)}, f32[4,16,512]{2,1,0:T(8,128)}, u32[]{:S(2)}) copy-start(f32[4,16,512]{2,1,0:T(8,128)} %coef_ref.2) | copy-start | bytes 393220
  0.6 4.4 %copy-start = (f32[3,4,16,512]{3,2,1,0:T(8,128)S(1)}, f32[3,4,16,512]{3,2,1,0:T(8,128)}, u32[]{:S(2)}) copy-start(f32[3,4,16,512]{3,2,1,0:T(8,128)} %velocity_ref.2) | copy-start | bytes 1179652
  1.7 8.0 %collective-permute-start.2 = (f32[4,4,4,512]{3,2,1,0:T(4,128)S(1)}, f32[4,4,4,512]{3,2,1,0:T(4,128)S(1)}, u32[]{:S(2)}, u32[]{:S(2)}) collective-permute-start(f32[4,4,4,512]{3,2,1,0:T(4,128)S(1)} %get-tuple-element.23), channel_id=1, source_target_pairs={{0,1},{1,2},{2,3},{3,0},{4,5},{5,6},{6,7},{7,4},{8,9},{9,10},{10,1... | collective-permute-start | bytes 393224 | tf_op jit(solution)/shard_map/ppermute | solution.py:595
  3.3 10.3 %collective-permute-start.3 = (f32[4,4,4,512]{3,2,1,0:T(4,128)S(1)}, f32[4,4,4,512]{3,2,1,0:T(4,128)S(1)}, u32[]{:S(2)}, u32[]{:S(2)}) collective-permute-start(f32[4,4,4,512]{3,2,1,0:T(4,128)S(1)} %get-tuple-element.24), channel_id=1, source_target_pairs={{0,3},{1,0},{2,1},{3,2},{4,7},{5,4},{6,5},{7,6},{8,11},{9,8},{10,9... | collective-permute-start | bytes 393224 | tf_op jit(solution)/shard_map/ppermute | solution.py:595
  5.7 12.9 %collective-permute-start.1 = (f32[4,4,4,16,128]{4,3,2,1,0:T(8,128)S(1)}, f32[4,4,4,16,128]{4,3,2,1,0:T(8,128)S(1)}, u32[]{:S(2)}, u32[]{:S(2)}) collective-permute-start(f32[4,4,4,16,128]{4,3,2,1,0:T(8,128)S(1)} %pack.1.block_ref), channel_id=1, source_target_pairs={{0,0},{1,1},{2,2},{3,3},{4,8},{5,9},{6,10},{7,11},{8,4},{9,5},{10,... | collective-permute-start | bytes 1572872 | tf_op jit(solution)/shard_map/ppermute | solution.py:606
  7.7 11.0 %collective-permute-start = (f32[4,4,4,16,128]{4,3,2,1,0:T(8,128)S(1)}, f32[4,4,4,16,128]{4,3,2,1,0:T(8,128)S(1)}, u32[]{:S(2)}, u32[]{:S(2)}) collective-permute-start(f32[4,4,4,16,128]{4,3,2,1,0:T(8,128)S(1)} %pack.1.block_ref), channel_id=1, source_target_pairs={{0,4},{4,0},{8,12},{12,8},{16,20},{20,16},{24,28},{28,24},{32,36},... | collective-permute-start | bytes 1572872 | tf_op jit(solution)/shard_map/ppermute | solution.py:598
  9.8 8.4 %collective-permute-start.5 = (f32[4,8,512]{2,1,0:T(8,128)S(1)}, f32[4,8,512]{2,1,0:T(8,128)S(1)}, u32[]{:S(2)}, u32[]{:S(2)}) collective-permute-start(f32[4,8,512]{2,1,0:T(8,128)S(1)} %get-tuple-element.27), channel_id=1, source_target_pairs={{0,1},{1,2},{2,3},{3,0},{4,9},{5,10},{6,11},{7,8},{8,5},{9,6},{10,... | collective-permute-start | bytes 196616 | tf_op jit(solution)/shard_map/ppermute | solution.py:606
  9.8 8.4 %collective-permute-start.6 = (f32[4,8,512]{2,1,0:T(8,128)S(1)}, f32[4,8,512]{2,1,0:T(8,128)S(1)}, u32[]{:S(2)}, u32[]{:S(2)}) collective-permute-start(f32[4,8,512]{2,1,0:T(8,128)S(1)} %get-tuple-element.28), channel_id=1, source_target_pairs={{0,3},{1,0},{2,1},{3,2},{4,11},{5,8},{6,9},{7,10},{8,7},{9,4},{10,... | collective-permute-start | bytes 196616 | tf_op jit(solution)/shard_map/ppermute | solution.py:606
  14.1 4.5 %collective-permute-start.4 = (f32[4,2,4,8,128]{4,3,2,1,0:T(8,128)S(1)}, f32[4,2,4,8,128]{4,3,2,1,0:T(8,128)S(1)}, u32[]{:S(2)}, u32[]{:S(2)}) collective-permute-start(f32[4,2,4,8,128]{4,3,2,1,0:T(8,128)S(1)} %get-tuple-element.26), channel_id=1, source_target_pairs={{0,4},{4,0},{8,12},{12,8},{16,20},{20,16},{24,28},{28,24},{32,36},... | collective-permute-start | bytes 393224 | tf_op jit(solution)/shard_map/ppermute | solution.py:598
  18.6 0.7 copy-start.2
  24.3 1.3 %collective-permute-start.7 = (f32[72,128]{1,0:T(8,128)S(1)}, f32[72,128]{1,0:T(8,128)S(1)}, u32[]{:S(2)}, u32[]{:S(2)}) collective-permute-start(f32[72,128]{1,0:T(8,128)S(1)} %get-tuple-element.30), channel_id=1, source_target_pairs={{0,4},{1,5},{2,6},{3,7},{4,0},{5,1},{6,2},{7,3},{8,12},{9,13},{10,... | collective-permute-start | bytes 110600 | tf_op jit(solution)/shard_map/ppermute | solution.py:584
  25.6 5.2 %collective-permute-start.10 = (f32[72,128]{1,0:T(8,128)S(1)}, f32[72,128]{1,0:T(8,128)S(1)}, u32[]{:S(2)}, u32[]{:S(2)}) collective-permute-start(f32[72,128]{1,0:T(8,128)S(1)} %add.33), channel_id=1, source_target_pairs={{0,3},{1,2},{2,1},{3,0},{4,7},{5,6},{6,5},{7,4},{8,11},{9,10},{10,... | collective-permute-start | bytes 110600 | tf_op jit(solution)/shard_map/ppermute | solution.py:584
  28.0 5.5 %collective-permute-start.9 = (f32[72,128]{1,0:T(8,128)S(1)}, f32[72,128]{1,0:T(8,128)S(1)}, u32[]{:S(2)}, u32[]{:S(2)}) collective-permute-start(f32[72,128]{1,0:T(8,128)S(1)} %add.33), channel_id=1, source_target_pairs={{0,2},{1,3},{2,0},{3,1},{4,6},{5,7},{6,4},{7,5},{8,10},{9,11},{10,... | collective-permute-start | bytes 110600 | tf_op jit(solution)/shard_map/ppermute | solution.py:584
  28.6 4.9 %collective-permute-start.8 = (f32[72,128]{1,0:T(8,128)S(1)}, f32[72,128]{1,0:T(8,128)S(1)}, u32[]{:S(2)}, u32[]{:S(2)}) collective-permute-start(f32[72,128]{1,0:T(8,128)S(1)} %add.33), channel_id=1, source_target_pairs={{0,1},{1,0},{2,3},{3,2},{4,5},{5,4},{6,7},{7,6},{8,9},{9,8},{10,11... | collective-permute-start | bytes 110600 | tf_op jit(solution)/shard_map/ppermute | solution.py:584
  33.5 6.0 %collective-permute-start.13 = (f32[72,128]{1,0:T(8,128)S(1)}, f32[72,128]{1,0:T(8,128)S(1)}, u32[]{:S(2)}, u32[]{:S(2)}) collective-permute-start(f32[72,128]{1,0:T(8,128)S(1)} %add_add_fusion.2), channel_id=1, source_target_pairs={{0,192},{1,193},{2,194},{3,195},{4,196},{5,197},{6,198},{7,199},{8... | collective-permute-start | bytes 110600 | tf_op jit(solution)/shard_map/ppermute | solution.py:584
  37.6 5.5 %collective-permute-start.12 = (f32[72,128]{1,0:T(8,128)S(1)}, f32[72,128]{1,0:T(8,128)S(1)}, u32[]{:S(2)}, u32[]{:S(2)}) collective-permute-start(f32[72,128]{1,0:T(8,128)S(1)} %add_add_fusion.2), channel_id=1, source_target_pairs={{0,128},{1,129},{2,130},{3,131},{4,132},{5,133},{6,134},{7,135},{8... | collective-permute-start | bytes 110600 | tf_op jit(solution)/shard_map/ppermute | solution.py:584
  38.2 4.8 %collective-permute-start.11 = (f32[72,128]{1,0:T(8,128)S(1)}, f32[72,128]{1,0:T(8,128)S(1)}, u32[]{:S(2)}, u32[]{:S(2)}) collective-permute-start(f32[72,128]{1,0:T(8,128)S(1)} %add_add_fusion.2), channel_id=1, source_target_pairs={{0,64},{1,65},{2,66},{3,67},{4,68},{5,69},{6,70},{7,71},{8,72},{9,... | collective-permute-start | bytes 110600 | tf_op jit(solution)/shard_map/ppermute | solution.py:584
  43.0 5.5 %collective-permute-start.16 = (f32[72,128]{1,0:T(8,128)S(1)}, f32[72,128]{1,0:T(8,128)S(1)}, u32[]{:S(2)}, u32[]{:S(2)}) collective-permute-start(f32[72,128]{1,0:T(8,128)S(1)} %add_add_fusion.1), channel_id=1, source_target_pairs={{0,24},{1,25},{2,26},{3,27},{4,28},{5,29},{6,30},{7,31},{8,16},{9,... | collective-permute-start | bytes 110600 | tf_op jit(solution)/shard_map/ppermute | solution.py:584
  44.7 6.2 %collective-permute-start.15 = (f32[72,128]{1,0:T(8,128)S(1)}, f32[72,128]{1,0:T(8,128)S(1)}, u32[]{:S(2)}, u32[]{:S(2)}) collective-permute-start(f32[72,128]{1,0:T(8,128)S(1)} %add_add_fusion.1), channel_id=1, source_target_pairs={{0,16},{1,17},{2,18},{3,19},{4,20},{5,21},{6,22},{7,23},{8,24},{9,... | collective-permute-start | bytes 110600 | tf_op jit(solution)/shard_map/ppermute | solution.py:584
  48.6 4.0 %collective-permute-start.14 = (f32[72,128]{1,0:T(8,128)S(1)}, f32[72,128]{1,0:T(8,128)S(1)}, u32[]{:S(2)}, u32[]{:S(2)}) collective-permute-start(f32[72,128]{1,0:T(8,128)S(1)} %add_add_fusion.1), channel_id=1, source_target_pairs={{0,8},{1,9},{2,10},{3,11},{4,12},{5,13},{6,14},{7,15},{8,0},{9,1},... | collective-permute-start | bytes 110600 | tf_op jit(solution)/shard_map/ppermute | solution.py:584
  52.5 7.1 %collective-permute-start.17 = (f32[72,128]{1,0:T(8,128)S(1)}, f32[72,128]{1,0:T(8,128)S(1)}, u32[]{:S(2)}, u32[]{:S(2)}) collective-permute-start(f32[72,128]{1,0:T(8,128)S(1)} %add_add_fusion), channel_id=1, source_target_pairs={{0,56},{1,57},{2,58},{3,59},{4,60},{5,61},{6,62},{7,63},{8,48},{9,... | collective-permute-start | bytes 110600 | tf_op jit(solution)/shard_map/ppermute | solution.py:584

commit v9 on v7

--- a/solution.py
+++ b/solution.py
@@ -218,7 +218,8 @@
     )(*(pltpu.with_memory_space_constraint(a, pltpu.HBM) for a in (velocity, smag_coef)))
 
 
-def pack_kernel(velocity_ref, coef_ref, block_ref):
+def pack_kernel(velocity_ref, coef_ref, block_ref, off_ref):
+    odd = lax.axis_index("gy") % 2 == 1
     rows_y, rows_z, size_x = coef_ref.shape
     rows = [velocity_ref[c].reshape(-1, size_x) for c in range(3)] + [coef_ref[...].reshape(-1, size_x)]
     done = exact_dot(jnp.concatenate(rows), sorting(size_x, True))
@@ -226,16 +227,25 @@
         for y in range(rows_y):
             start = (c * rows_y + y) * rows_z
             for o in range(4):
-                block_ref[c, y, o] = done[start : start + rows_z, LANES * o : LANES * (o + 1)]
+                plane = done[start : start + rows_z, LANES * o : LANES * (o + 1)]
+                block_ref[c, y, o] = plane
+                if c < 3:
+                    off_ref[c * rows_y + y, o] = plane
+                elif y < rows_y - 1:
+                    above = done[start + rows_z : start + 2 * rows_z, LANES * o : LANES * (o + 1)]
+                    off_ref[c * rows_y + y, o] = jnp.where(odd, above, plane)
 
 
 def pack(velocity, smag_coef):
     rows_y, rows_z, _ = smag_coef.shape
     return pl.pallas_call(
         pack_kernel,
-        out_shape=jax.ShapeDtypeStruct((4, rows_y, 4, rows_z, LANES), jnp.float32),
+        out_shape=(
+            jax.ShapeDtypeStruct((4, rows_y, 4, rows_z, LANES), jnp.float32),
+            jax.ShapeDtypeStruct((4 * rows_y - 1, 4, rows_z, LANES), jnp.float32),
+        ),
         in_specs=[pl.BlockSpec(memory_space=pltpu.VMEM)] * 2,
-        out_specs=pl.BlockSpec(memory_space=pltpu.VMEM),
+        out_specs=[pl.BlockSpec(memory_space=pltpu.VMEM)] * 2,
         compiler_params=pltpu.CompilerParams(vmem_limit_bytes=12 * 2**20),
         name="pack",
     )(velocity, smag_coef)
@@ -392,9 +402,10 @@
             for o in range(4):
                 own, below, above = (c, rows_y + y, o), (c, y, o), (c, 2 * rows_y + y, o)
                 cells_ref[(*own, own_rows)] = block_ref[c, y, o]
-                chip, other = chip_ref[c, y, o], other_ref[c, y, o]
-                cells_ref[(*below, own_rows)] = behind(chip, other)
-                cells_ref[(*above, own_rows)] = ahead(chip, other)
+                chip, plane = chip_ref[c, y, o], c * rows_y + y
+                under, upper = (plane, plane) if c < 3 else (plane - min(y, 1), min(plane, 4 * rows_y - 2))
+                cells_ref[(*below, own_rows)] = behind(chip, other_ref[under, o])
+                cells_ref[(*above, own_rows)] = ahead(chip, other_ref[upper, o])
                 cells_ref[(*own, side)] = sides_ref[c, y, o]
                 for choose, place, away in ((behind, below, rows_y - 1 - y), (ahead, above, y)):
                     if away == 0:
@@ -531,14 +542,11 @@
     axes = ("gy", "gz")
     size_z, size_x = 8, lax.axis_size("gz")
     rounds = (
-        [
-            lambda x, y, z, core: (x, y, z, core ^ 1),
-            lambda x, y, z, core: (x, y, z ^ 1, core),
-            lambda x, y, z, core: (x, y, z ^ 1, core ^ 1),
-        ],
+        [lambda x, y, z, core: (x, y, z, core ^ 1)],
         [lambda x, y, z, core, bits=bits: (x ^ bits, y, z, core) for bits in (1, 2, 3)],
         [lambda x, y, z, core, bits=bits: (x, y ^ bits, z, core) for bits in (1, 2, 3)],
-        [lambda x, y, z, core, far=far: (x, y, (z + far) % size_z, core) for far in (2, -2, 4)],
+        [lambda x, y, z, core, bits=bits: (x, y, z ^ bits, core) for bits in (1, 2, 3)],
+        [lambda x, y, z, core: (x, y, size_z - 1 - z, core)],
     )
 
     def partner(move, device):
@@ -572,9 +580,9 @@
     low, high = edges(velocity, smag_coef)
     velocity, smag_coef, low, high = lax.optimization_barrier((velocity, smag_coef, low, high))
     sides, side_chip, side_other = sort_sides(along_z(high, 1), along_z(low, -1))
-    block = pack(velocity, smag_coef)
+    block, off = pack(velocity, smag_coef)
     wide, snapshots, gram = both_steps(
-        snap_code, block, on_chip(block), off_chip(block), sides, on_chip(side_chip), off_chip(side_other)
+        snap_code, block, on_chip(block), off_chip(off), sides, on_chip(side_chip), off_chip(side_other)
     )
     rows_y, rows_z = velocity.shape[1], velocity.shape[2]
     rows_all = 12 * LANES * count_y * count_z

time: 67.6 us -> 67 us (level); the launches traced: 66.4 us -> 66.9 us
  waiting for transfers between devices: 19.1 us -> 20.1 us
    ppermute x12 -> x11, waiting for transfers between devices: 14.1 us -> 15.5 us  [device_sum(): lax.ppermute(part, axes, [(device, partner(move, device)) for device in r...]
    ppermute x12 -> x11, starting transfers between devices: 19.4 us -> 18.9 us  [device_sum(): lax.ppermute(part, axes, [(device, partner(move, device)) for device in r...]
  transfers between devices with their start and end apart: 18 -> 17, of which waited for: 9 -> 9; matrix products, arithmetic and copies ran while one was open for 0% -> 0% of each run, Pallas kernels for 4% -> 4%
where the time goes in v9:
time: 67 us; the launch traced here: 66.9 us
  starting transfers between devices  28.6 us (43%)
  waiting for transfers between devices  20.1 us (30%)
  Pallas kernels  17.4 us (26%)
  between operations  0.72 us (1%)
    ppermute x11, starting transfers between devices, device_sum(): lax.ppermute(part, axes, [(device, partner(move, device)) for device in r...  18.9 us
    ppermute x11, waiting for transfers between devices, device_sum(): lax.ppermute(part, axes, [(device, partner(move, device)) for device in r...  15.5 us
    pallas_call x1, Pallas kernels, project(): pl.pallas_call(functools.partial(basis_kernel, rows_all=rows_all), out_sh...  8.91 us
    pallas_call x1, Pallas kernels, both_steps(): pl.pallas_call(steps_kernel, out_shape=(f32(3 * rows_y * rows_z, 4 * LANE...  5.05 us
    ppermute x2, waiting for transfers between devices, off_chip(): return lax.ppermute(part, 'gy', list(enumerate(partners)))  4.66 us
    ppermute x2, starting transfers between devices, off_chip(): return lax.ppermute(part, 'gy', list(enumerate(partners)))  4.16 us
    ppermute x2, starting transfers between devices, along_z(): lax.ppermute(part, 'gz', [(i, (i + step) % count_z) for i in range(count_...  3.31 us
    ppermute x2, starting transfers between devices, on_chip(): return lax.ppermute(part, 'gy', [(i, i ^ 1) for i in range(count_y)])  2.21 us
  transfers between devices with their start and end apart: 17, of which 9 were waited for; matrix products, arithmetic and copies ran while one was open for 0% of the time, Pallas kernels for 4%

profile of v9, /device:TPU:32, one launch (start us, length us, event | category | flops | bytes accessed | tf_op | source)
XLA Modules:
  0.0 66.9 jit_solution(12811874165291057216)
XLA Ops:
  0.6 1.1 %edges.1 = (f32[4,4,4,512]{3,2,1,0:T(4,128)S(1)}, f32[4,4,4,512]{3,2,1,0:T(4,128)S(1)}) custom-call(f32[3,4,16,512]{3,2,1,0:T(8,128)} %velocity_ref.2, f32[4,16,512]{2,1,0:T(8,128)} %coef_ref.2), custom_call_target="tpu_custom_call" | custom-call | tf_op jit(solution)/shard_map/edges/pallas_call | solution.py:210
  1.7 1.6 %collective-permute-start.2 = (f32[4,4,4,512]{3,2,1,0:T(4,128)S(1)}, f32[4,4,4,512]{3,2,1,0:T(4,128)S(1)}, u32[]{:S(2)}, u32[]{:S(2)}) collective-permute-start(f32[4,4,4,512]{3,2,1,0:T(4,128)S(1)} %get-tuple-element.22), channel_id=1, source_target_pairs={{0,1},{1,2},{2,3},{3,0},{4,5},{5,6},{6,7},{7,4},{8,9},{9,10},{10,1... | collective-permute-start | bytes 393224 | tf_op jit(solution)/shard_map/ppermute | solution.py:571
  3.3 1.7 %collective-permute-start.3 = (f32[4,4,4,512]{3,2,1,0:T(4,128)S(1)}, f32[4,4,4,512]{3,2,1,0:T(4,128)S(1)}, u32[]{:S(2)}, u32[]{:S(2)}) collective-permute-start(f32[4,4,4,512]{3,2,1,0:T(4,128)S(1)} %get-tuple-element.23), channel_id=1, source_target_pairs={{0,3},{1,0},{2,1},{3,2},{4,7},{5,4},{6,5},{7,6},{8,11},{9,8},{10,9... | collective-permute-start | bytes 393224 | tf_op jit(solution)/shard_map/ppermute | solution.py:571
  5.7 1.9 %collective-permute-start.1 = (f32[15,4,16,128]{3,2,1,0:T(8,128)S(1)}, f32[15,4,16,128]{3,2,1,0:T(8,128)S(1)}, u32[]{:S(2)}, u32[]{:S(2)}) collective-permute-start(f32[15,4,16,128]{3,2,1,0:T(8,128)S(1)} %get-tuple-element.21), channel_id=1, source_target_pairs={{0,0},{4,8},{8,4},{12,16},{16,12},{20,24},{24,20},{28,32},{32,28},... | collective-permute-start | bytes 1474568 | tf_op jit(solution)/shard_map/ppermute | solution.py:578
  7.6 2.1 %collective-permute-start = (f32[4,4,4,16,128]{4,3,2,1,0:T(8,128)S(1)}, f32[4,4,4,16,128]{4,3,2,1,0:T(8,128)S(1)}, u32[]{:S(2)}, u32[]{:S(2)}) collective-permute-start(f32[4,4,4,16,128]{4,3,2,1,0:T(8,128)S(1)} %get-tuple-element.20.block_ref), channel_id=1, source_target_pairs={{0,4},{4,0},{8,12},{12,8},{16,20},{20,16},{24,28},{28,24},{32,36},... | collective-permute-start | bytes 1572872 | tf_op jit(solution)/shard_map/ppermute | solution.py:574
  10.3 2.2 %collective-permute-start.5 = (f32[4,2,4,8,128]{4,3,2,1,0:T(8,128)S(1)}, f32[4,2,4,8,128]{4,3,2,1,0:T(8,128)S(1)}, u32[]{:S(2)}, u32[]{:S(2)}) collective-permute-start(f32[4,2,4,8,128]{4,3,2,1,0:T(8,128)S(1)} %get-tuple-element.26), channel_id=1, source_target_pairs={{0,0},{4,8},{8,4},{12,16},{16,12},{20,24},{24,20},{28,32},{32,28},... | collective-permute-start | bytes 393224 | tf_op jit(solution)/shard_map/ppermute | solution.py:578
  12.6 4.7 %collective-permute-done.5.side_other_ref = f32[4,2,4,8,128]{4,3,2,1,0:T(8,128)S(1)} collective-permute-done((f32[4,2,4,8,128]{4,3,2,1,0:T(8,128)S(1)}, f32[4,2,4,8,128]{4,3,2,1,0:T(8,128)S(1)}, u32[]{:S(2)}, u32[]{:S(2)}) %collective-permute-start.5) | collective-permute-done | bytes 131104 | tf_op jit(solution)/shard_map/ppermute | solution.py:578
  17.3 5.1 %steps.1 = (f32[192,512]{1,0:T(8,128)S(1)}, f32[2048,128]{1,0:T(8,128)S(1)}, f32[72,128]{1,0:T(8,128)S(1)}) custom-call(s32[128]{0:T(128)S(1)} %copy-done.2, f32[4,4,4,16,128]{4,3,2,1,0:T(8,128)S(1)} %get-tuple-element.20.block_ref, f32[4,4,4,16,128]{4,3,2,1,0:T(8,128)S(1)} %collective-permute-done.chip_ref, ...), custom_call_target="tpu_custom_call" | custom-call | tf_op jit(solution)/shard_map/steps/pallas_call | solution.py:519
  22.7 0.9 %collective-permute-done.6 = f32[72,128]{1,0:T(8,128)S(1)} collective-permute-done((f32[72,128]{1,0:T(8,128)S(1)}, f32[72,128]{1,0:T(8,128)S(1)}, u32[]{:S(2)}, u32[]{:S(2)}) %collective-permute-start.6) | collective-permute-done | bytes 36896 | tf_op jit(solution)/shard_map/ppermute | solution.py:560
  23.6 1.6 %collective-permute-start.9 = (f32[72,128]{1,0:T(8,128)S(1)}, f32[72,128]{1,0:T(8,128)S(1)}, u32[]{:S(2)}, u32[]{:S(2)}) collective-permute-start(f32[72,128]{1,0:T(8,128)S(1)} %add.33), channel_id=1, source_target_pairs={{0,3},{1,2},{2,1},{3,0},{4,7},{5,6},{6,5},{7,4},{8,11},{9,10},{10,... | collective-permute-start | bytes 110600 | tf_op jit(solution)/shard_map/ppermute | solution.py:560
  26.0 1.7 %collective-permute-start.7 = (f32[72,128]{1,0:T(8,128)S(1)}, f32[72,128]{1,0:T(8,128)S(1)}, u32[]{:S(2)}, u32[]{:S(2)}) collective-permute-start(f32[72,128]{1,0:T(8,128)S(1)} %add.33), channel_id=1, source_target_pairs={{0,1},{1,0},{2,3},{3,2},{4,5},{5,4},{6,7},{7,6},{8,9},{9,8},{10,11... | collective-permute-start | bytes 110600 | tf_op jit(solution)/shard_map/ppermute | solution.py:560
  27.7 1.1 %collective-permute-done.9 = f32[72,128]{1,0:T(8,128)S(1)} collective-permute-done((f32[72,128]{1,0:T(8,128)S(1)}, f32[72,128]{1,0:T(8,128)S(1)}, u32[]{:S(2)}, u32[]{:S(2)}) %collective-permute-start.9) | collective-permute-done | bytes 36896 | tf_op jit(solution)/shard_map/ppermute | solution.py:560
  28.8 1.8 %collective-permute-done.8 = f32[72,128]{1,0:T(8,128)S(1)} collective-permute-done((f32[72,128]{1,0:T(8,128)S(1)}, f32[72,128]{1,0:T(8,128)S(1)}, u32[]{:S(2)}, u32[]{:S(2)}) %collective-permute-start.8) | collective-permute-done | bytes 36896 | tf_op jit(solution)/shard_map/ppermute | solution.py:560
  30.7 4.0 %collective-permute-start.12 = (f32[72,128]{1,0:T(8,128)S(1)}, f32[72,128]{1,0:T(8,128)S(1)}, u32[]{:S(2)}, u32[]{:S(2)}) collective-permute-start(f32[72,128]{1,0:T(8,128)S(1)} %add_add_fusion.2), channel_id=1, source_target_pairs={{0,192},{1,193},{2,194},{3,195},{4,196},{5,197},{6,198},{7,199},{8... | collective-permute-start | bytes 110600 | tf_op jit(solution)/shard_map/ppermute | solution.py:560
  35.6 1.0 %collective-permute-done.12 = f32[72,128]{1,0:T(8,128)S(1)} collective-permute-done((f32[72,128]{1,0:T(8,128)S(1)}, f32[72,128]{1,0:T(8,128)S(1)}, u32[]{:S(2)}, u32[]{:S(2)}) %collective-permute-start.12) | collective-permute-done | bytes 36896 | tf_op jit(solution)/shard_map/ppermute | solution.py:560
  36.6 3.5 %collective-permute-done.11 = f32[72,128]{1,0:T(8,128)S(1)} collective-permute-done((f32[72,128]{1,0:T(8,128)S(1)}, f32[72,128]{1,0:T(8,128)S(1)}, u32[]{:S(2)}, u32[]{:S(2)}) %collective-permute-start.11) | collective-permute-done | bytes 36896 | tf_op jit(solution)/shard_map/ppermute | solution.py:560
  40.1 1.8 %collective-permute-start.15 = (f32[72,128]{1,0:T(8,128)S(1)}, f32[72,128]{1,0:T(8,128)S(1)}, u32[]{:S(2)}, u32[]{:S(2)}) collective-permute-start(f32[72,128]{1,0:T(8,128)S(1)} %add_add_fusion.1), channel_id=1, source_target_pairs={{0,24},{1,25},{2,26},{3,27},{4,28},{5,29},{6,30},{7,31},{8,16},{9,... | collective-permute-start | bytes 110600 | tf_op jit(solution)/shard_map/ppermute | solution.py:560
  42.0 4.8 %collective-permute-start.14 = (f32[72,128]{1,0:T(8,128)S(1)}, f32[72,128]{1,0:T(8,128)S(1)}, u32[]{:S(2)}, u32[]{:S(2)}) collective-permute-start(f32[72,128]{1,0:T(8,128)S(1)} %add_add_fusion.1), channel_id=1, source_target_pairs={{0,16},{1,17},{2,18},{3,19},{4,20},{5,21},{6,22},{7,23},{8,24},{9,... | collective-permute-start | bytes 110600 | tf_op jit(solution)/shard_map/ppermute | solution.py:560
  46.8 2.3 %collective-permute-done.14 = f32[72,128]{1,0:T(8,128)S(1)} collective-permute-done((f32[72,128]{1,0:T(8,128)S(1)}, f32[72,128]{1,0:T(8,128)S(1)}, u32[]{:S(2)}, u32[]{:S(2)}) %collective-permute-start.14) | collective-permute-done | bytes 36896 | tf_op jit(solution)/shard_map/ppermute | solution.py:560
  49.1 1.6 %collective-permute-done.13 = f32[72,128]{1,0:T(8,128)S(1)} collective-permute-done((f32[72,128]{1,0:T(8,128)S(1)}, f32[72,128]{1,0:T(8,128)S(1)}, u32[]{:S(2)}, u32[]{:S(2)}) %collective-permute-start.13) | collective-permute-done | bytes 36896 | tf_op jit(solution)/shard_map/ppermute | solution.py:560
  50.7 2.8 %collective-permute-start.16 = (f32[72,128]{1,0:T(8,128)S(1)}, f32[72,128]{1,0:T(8,128)S(1)}, u32[]{:S(2)}, u32[]{:S(2)}) collective-permute-start(f32[72,128]{1,0:T(8,128)S(1)} %add_add_fusion), channel_id=1, source_target_pairs={{0,56},{1,57},{2,58},{3,59},{4,60},{5,61},{6,62},{7,63},{8,48},{9,... | collective-permute-start | bytes 110600 | tf_op jit(solution)/shard_map/ppermute | solution.py:560
  53.6 1.3 %unsort.1 = f32[3,4,16,512]{3,2,1,0:T(8,128)} custom-call(f32[192,512]{1,0:T(8,128)S(1)} %get-tuple-element.27.wide_ref), custom_call_target="tpu_custom_call" | custom-call | flops 4000000000 | bytes 1000000 | tf_op jit(solution)/shard_map/unsort/pallas_call | solution.py:502
  54.8 3.1 %collective-permute-done.16 = f32[72,128]{1,0:T(8,128)S(1)} collective-permute-done((f32[72,128]{1,0:T(8,128)S(1)}, f32[72,128]{1,0:T(8,128)S(1)}, u32[]{:S(2)}, u32[]{:S(2)}) %collective-permute-start.16) | collective-permute-done | bytes 36896 | tf_op jit(solution)/shard_map/ppermute | solution.py:560
  58.0 8.9 %basis.1 = f32[1344,128]{1,0:T(8,128)} custom-call(f32[72,128]{1,0:T(8,128)S(1)} %add.43.total_ref, f32[2048,128]{1,0:T(8,128)S(1)} %get-tuple-element.29.snap_ref), custom_call_target="tpu_custom_call" | custom-call | tf_op jit(solution)/shard_map/basis/pallas_call | solution.py:169
  (27 shorter events, 3.5 us)
Async XLA Ops:
  0.6 4.4 %copy-start.1 = (f32[4,16,512]{2,1,0:T(8,128)S(1)}, f32[4,16,512]{2,1,0:T(8,128)}, u32[]{:S(2)}) copy-start(f32[4,16,512]{2,1,0:T(8,128)} %coef_ref.2) | copy-start | bytes 393220
  0.6 4.4 %copy-start = (f32[3,4,16,512]{3,2,1,0:T(8,128)S(1)}, f32[3,4,16,512]{3,2,1,0:T(8,128)}, u32[]{:S(2)}) copy-start(f32[3,4,16,512]{3,2,1,0:T(8,128)} %velocity_ref.2) | copy-start | bytes 1179652
  1.7 8.0 %collective-permute-start.2 = (f32[4,4,4,512]{3,2,1,0:T(4,128)S(1)}, f32[4,4,4,512]{3,2,1,0:T(4,128)S(1)}, u32[]{:S(2)}, u32[]{:S(2)}) collective-permute-start(f32[4,4,4,512]{3,2,1,0:T(4,128)S(1)} %get-tuple-element.22), channel_id=1, source_target_pairs={{0,1},{1,2},{2,3},{3,0},{4,5},{5,6},{6,7},{7,4},{8,9},{9,10},{10,1... | collective-permute-start | bytes 393224 | tf_op jit(solution)/shard_map/ppermute | solution.py:571
  3.3 6.4 %collective-permute-start.3 = (f32[4,4,4,512]{3,2,1,0:T(4,128)S(1)}, f32[4,4,4,512]{3,2,1,0:T(4,128)S(1)}, u32[]{:S(2)}, u32[]{:S(2)}) collective-permute-start(f32[4,4,4,512]{3,2,1,0:T(4,128)S(1)} %get-tuple-element.23), channel_id=1, source_target_pairs={{0,3},{1,0},{2,1},{3,2},{4,7},{5,4},{6,5},{7,6},{8,11},{9,8},{10,9... | collective-permute-start | bytes 393224 | tf_op jit(solution)/shard_map/ppermute | solution.py:571
  5.7 11.6 %collective-permute-start.1 = (f32[15,4,16,128]{3,2,1,0:T(8,128)S(1)}, f32[15,4,16,128]{3,2,1,0:T(8,128)S(1)}, u32[]{:S(2)}, u32[]{:S(2)}) collective-permute-start(f32[15,4,16,128]{3,2,1,0:T(8,128)S(1)} %get-tuple-element.21), channel_id=1, source_target_pairs={{0,0},{4,8},{8,4},{12,16},{16,12},{20,24},{24,20},{28,32},{32,28},... | collective-permute-start | bytes 1474568 | tf_op jit(solution)/shard_map/ppermute | solution.py:578
  7.6 9.6 %collective-permute-start = (f32[4,4,4,16,128]{4,3,2,1,0:T(8,128)S(1)}, f32[4,4,4,16,128]{4,3,2,1,0:T(8,128)S(1)}, u32[]{:S(2)}, u32[]{:S(2)}) collective-permute-start(f32[4,4,4,16,128]{4,3,2,1,0:T(8,128)S(1)} %get-tuple-element.20.block_ref), channel_id=1, source_target_pairs={{0,4},{4,0},{8,12},{12,8},{16,20},{20,16},{24,28},{28,24},{32,36},... | collective-permute-start | bytes 1572872 | tf_op jit(solution)/shard_map/ppermute | solution.py:574
  10.2 2.4 %collective-permute-start.4 = (f32[4,2,4,8,128]{4,3,2,1,0:T(8,128)S(1)}, f32[4,2,4,8,128]{4,3,2,1,0:T(8,128)S(1)}, u32[]{:S(2)}, u32[]{:S(2)}) collective-permute-start(f32[4,2,4,8,128]{4,3,2,1,0:T(8,128)S(1)} %get-tuple-element.25), channel_id=1, source_target_pairs={{0,4},{4,0},{8,12},{12,8},{16,20},{20,16},{24,28},{28,24},{32,36},... | collective-permute-start | bytes 393224 | tf_op jit(solution)/shard_map/ppermute | solution.py:574
  10.3 6.9 %copy-start.2 = (s32[128]{0:T(128)S(1)}, s32[128]{0:T(128)}, u32[]{:S(2)}) copy-start(s32[128]{0:T(128)} %code_ref.1) | copy-start | bytes 1540
  10.3 6.9 %collective-permute-start.5 = (f32[4,2,4,8,128]{4,3,2,1,0:T(8,128)S(1)}, f32[4,2,4,8,128]{4,3,2,1,0:T(8,128)S(1)}, u32[]{:S(2)}, u32[]{:S(2)}) collective-permute-start(f32[4,2,4,8,128]{4,3,2,1,0:T(8,128)S(1)} %get-tuple-element.26), channel_id=1, source_target_pairs={{0,0},{4,8},{8,4},{12,16},{16,12},{20,24},{24,20},{28,32},{32,28},... | collective-permute-start | bytes 393224 | tf_op jit(solution)/shard_map/ppermute | solution.py:578
  22.3 1.3 %collective-permute-start.6 = (f32[72,128]{1,0:T(8,128)S(1)}, f32[72,128]{1,0:T(8,128)S(1)}, u32[]{:S(2)}, u32[]{:S(2)}) collective-permute-start(f32[72,128]{1,0:T(8,128)S(1)} %get-tuple-element.28), channel_id=1, source_target_pairs={{0,4},{1,5},{2,6},{3,7},{4,0},{5,1},{6,2},{7,3},{8,12},{9,13},{10,... | collective-permute-start | bytes 110600 | tf_op jit(solution)/shard_map/ppermute | solution.py:560
  23.6 5.2 %collective-permute-start.9 = (f32[72,128]{1,0:T(8,128)S(1)}, f32[72,128]{1,0:T(8,128)S(1)}, u32[]{:S(2)}, u32[]{:S(2)}) collective-permute-start(f32[72,128]{1,0:T(8,128)S(1)} %add.33), channel_id=1, source_target_pairs={{0,3},{1,2},{2,1},{3,0},{4,7},{5,6},{6,5},{7,4},{8,11},{9,10},{10,... | collective-permute-start | bytes 110600 | tf_op jit(solution)/shard_map/ppermute | solution.py:560
  25.2 5.5 %collective-permute-start.8 = (f32[72,128]{1,0:T(8,128)S(1)}, f32[72,128]{1,0:T(8,128)S(1)}, u32[]{:S(2)}, u32[]{:S(2)}) collective-permute-start(f32[72,128]{1,0:T(8,128)S(1)} %add.33), channel_id=1, source_target_pairs={{0,2},{1,3},{2,0},{3,1},{4,6},{5,7},{6,4},{7,5},{8,10},{9,11},{10,... | collective-permute-start | bytes 110600 | tf_op jit(solution)/shard_map/ppermute | solution.py:560
  26.0 4.7 %collective-permute-start.7 = (f32[72,128]{1,0:T(8,128)S(1)}, f32[72,128]{1,0:T(8,128)S(1)}, u32[]{:S(2)}, u32[]{:S(2)}) collective-permute-start(f32[72,128]{1,0:T(8,128)S(1)} %add.33), channel_id=1, source_target_pairs={{0,1},{1,0},{2,3},{3,2},{4,5},{5,4},{6,7},{7,6},{8,9},{9,8},{10,11... | collective-permute-start | bytes 110600 | tf_op jit(solution)/shard_map/ppermute | solution.py:560
  30.7 5.9 %collective-permute-start.12 = (f32[72,128]{1,0:T(8,128)S(1)}, f32[72,128]{1,0:T(8,128)S(1)}, u32[]{:S(2)}, u32[]{:S(2)}) collective-permute-start(f32[72,128]{1,0:T(8,128)S(1)} %add_add_fusion.2), channel_id=1, source_target_pairs={{0,192},{1,193},{2,194},{3,195},{4,196},{5,197},{6,198},{7,199},{8... | collective-permute-start | bytes 110600 | tf_op jit(solution)/shard_map/ppermute | solution.py:560
  34.6 5.5 %collective-permute-start.11 = (f32[72,128]{1,0:T(8,128)S(1)}, f32[72,128]{1,0:T(8,128)S(1)}, u32[]{:S(2)}, u32[]{:S(2)}) collective-permute-start(f32[72,128]{1,0:T(8,128)S(1)} %add_add_fusion.2), channel_id=1, source_target_pairs={{0,128},{1,129},{2,130},{3,131},{4,132},{5,133},{6,134},{7,135},{8... | collective-permute-start | bytes 110600 | tf_op jit(solution)/shard_map/ppermute | solution.py:560
  35.0 5.1 %collective-permute-start.10 = (f32[72,128]{1,0:T(8,128)S(1)}, f32[72,128]{1,0:T(8,128)S(1)}, u32[]{:S(2)}, u32[]{:S(2)}) collective-permute-start(f32[72,128]{1,0:T(8,128)S(1)} %add_add_fusion.2), channel_id=1, source_target_pairs={{0,64},{1,65},{2,66},{3,67},{4,68},{5,69},{6,70},{7,71},{8,72},{9,... | collective-permute-start | bytes 110600 | tf_op jit(solution)/shard_map/ppermute | solution.py:560
  40.1 6.7 %collective-permute-start.15 = (f32[72,128]{1,0:T(8,128)S(1)}, f32[72,128]{1,0:T(8,128)S(1)}, u32[]{:S(2)}, u32[]{:S(2)}) collective-permute-start(f32[72,128]{1,0:T(8,128)S(1)} %add_add_fusion.1), channel_id=1, source_target_pairs={{0,24},{1,25},{2,26},{3,27},{4,28},{5,29},{6,30},{7,31},{8,16},{9,... | collective-permute-start | bytes 110600 | tf_op jit(solution)/shard_map/ppermute | solution.py:560
  42.0 7.1 %collective-permute-start.14 = (f32[72,128]{1,0:T(8,128)S(1)}, f32[72,128]{1,0:T(8,128)S(1)}, u32[]{:S(2)}, u32[]{:S(2)}) collective-permute-start(f32[72,128]{1,0:T(8,128)S(1)} %add_add_fusion.1), channel_id=1, source_target_pairs={{0,16},{1,17},{2,18},{3,19},{4,20},{5,21},{6,22},{7,23},{8,24},{9,... | collective-permute-start | bytes 110600 | tf_op jit(solution)/shard_map/ppermute | solution.py:560
  46.8 4.0 %collective-permute-start.13 = (f32[72,128]{1,0:T(8,128)S(1)}, f32[72,128]{1,0:T(8,128)S(1)}, u32[]{:S(2)}, u32[]{:S(2)}) collective-permute-start(f32[72,128]{1,0:T(8,128)S(1)} %add_add_fusion.1), channel_id=1, source_target_pairs={{0,8},{1,9},{2,10},{3,11},{4,12},{5,13},{6,14},{7,15},{8,0},{9,1},... | collective-permute-start | bytes 110600 | tf_op jit(solution)/shard_map/ppermute | solution.py:560
  50.7 7.2 %collective-permute-start.16 = (f32[72,128]{1,0:T(8,128)S(1)}, f32[72,128]{1,0:T(8,128)S(1)}, u32[]{:S(2)}, u32[]{:S(2)}) collective-permute-start(f32[72,128]{1,0:T(8,128)S(1)} %add_add_fusion), channel_id=1, source_target_pairs={{0,56},{1,57},{2,58},{3,59},{4,60},{5,61},{6,62},{7,63},{8,48},{9,... | collective-permute-start | bytes 110600 | tf_op jit(solution)/shard_map/ppermute | solution.py:560
